TPU v7x, 32 devices: a whole 2x2x4 slice. The times are simulated.
32 devices in a mesh: user: 8 (over z, y), item: 4 (over x, core).
Axes of the slice: x: 2, y: 2, z: 4, core: 2. Of those that a mesh axis runs over, the one named last changes fastest.
Arguments:
- item_init: float32 [4096, 128], P(('item', 'user')), may hold values from -1.8 to 1.8
- tile_rows: int32 [8, 4, 48], P('user', 'item'), may hold values from 0 to 7, as said below
- tile_cols: int32 [8, 4, 48], P('user', 'item'), may hold values from 0 to 7, as said below
- tile_count: int32 [8, 4], P('user', 'item'), may hold values from 24 to 48, as said below
- conf: int32 [8, 4, 48, 128, 128], P('user', 'item'), may hold values from 0 to 7, as said below
Outputs:
- user_factors: float32 [8192, 128], P(('user', 'item'))
- item_factors: float32 [4096, 128], P(('item', 'user'))
Inputs may be any that keep to these rules, and one draw needn't show every extreme that they name: `tile_rows`: every user block of a group is named by a slot below 24 of some device of that group. `tile_cols`: slot t of device (u, i) names item block (t + s) mod 8, with s fixed for the device; every item block of a group is named by a slot below 24 of some device of that group; device (u, i) owns item block u of its group (item block i * 8 + u in all), and at most 6 slots of one device name blocks of one such device, exactly 6 for some. `tile_count`: some device uses all 48 slots. `conf`: the diagonal entries of every tile are nonzero.
All inputs are finite; a program needn't handle non-finite values.
Results may differ from a plain program's by a relative error of at most 0.0003.
Values sent between devices are 32-bit elements; how exact they have to be, the bound alone decides.
No kernel may reach another device: no remote copies, remote signals or barrier semaphores. Data moves between devices by JAX's collectives and lax.ppermute only.
A program may use at most 64 MiB of HBM per device.

v0:
```python
import jax
import jax.numpy as jnp
from jax import lax
from jax.sharding import PartitionSpec as P

UB = 2
IB = 1
CG_ITERS = 3


highest = lax.Precision.HIGHEST
ridge = 5.0
unobserved = 256.0


def block_sum(slot_terms, block_ids, row_count, block_size):
    block_count = row_count // block_size
    targets = jnp.arange(block_count, dtype=jnp.int32)
    onehot = (block_ids[:, None] == targets[None, :]).astype(jnp.float32)
    summed = jnp.einsum("tr,tik->rik", onehot, slot_terms, precision=highest)
    return summed.reshape(row_count, slot_terms.shape[2])


def group_products(own_blocks, other_blocks, tile_values, own_ids, other_ids):
    own_rows = jnp.take(own_blocks, own_ids, axis=0)
    other_rows = jnp.take(other_blocks, other_ids, axis=0)
    scores = jnp.einsum("tik,tjk->tij", own_rows, other_rows, precision=highest)
    return jnp.einsum("tij,tjk->tik", scores * tile_values, other_rows, precision=highest)


def slot_products(own_blocks, other_blocks, tile_values, own_ids, other_ids):
    return group_products(own_blocks, other_blocks, tile_values, own_ids, other_ids)


def conjugate(right_side, apply_operator):
    solution = jnp.zeros_like(right_side)
    residual = right_side
    direction = right_side
    norm_now = jnp.sum(residual * residual, axis=-1, keepdims=True)
    for iteration in range(CG_ITERS):
        product_vec = apply_operator(direction)
        step_length = norm_now / jnp.sum(direction * product_vec, axis=-1, keepdims=True)
        solution = solution + step_length * direction
        residual = residual - step_length * product_vec
        norm_next = jnp.sum(residual * residual, axis=-1, keepdims=True)
        direction = residual + norm_next / norm_now * direction
        norm_now = norm_next
    return solution


def shards(item_init, tile_rows, tile_cols, tile_count, conf):
    slot_total = tile_rows.shape[-1]
    block_size = conf.shape[-1]
    factor_rank = item_init.shape[1]
    item_devices = lax.axis_size("item")
    user_devices = lax.axis_size("user")
    row_ids = tile_rows.reshape(slot_total)
    col_ids = tile_cols.reshape(slot_total)
    slot_count = tile_count.reshape(())
    counts = conf.reshape(slot_total, block_size, block_size).astype(jnp.float32)
    usable = (jnp.arange(slot_total, dtype=jnp.int32) < slot_count)[:, None, None]
    confidence = jnp.where(usable, counts, 0.0)
    weights = jnp.where(usable & (counts > 0.0), 1.0 + counts, 0.0)
    user_rows = UB * block_size
    item_rows = IB * block_size
    item_shard = lax.all_gather(item_init, "user", axis=0, tiled=True)
    item_blocks = item_shard.reshape(-1, block_size, factor_rank)
    item_gram = lax.psum(jnp.dot(item_init.T, item_init, precision=highest), ("user", "item"))
    user_weight = unobserved / (item_init.shape[0] * user_devices * item_devices)
    user_terms = jnp.einsum(
        "tij,tjk->tik", weights, jnp.take(item_blocks, col_ids, axis=0), precision=highest
    )
    user_side = lax.psum_scatter(
        block_sum(user_terms, row_ids, user_rows * lax.axis_size("item"), block_size),
        "item",
        scatter_dimension=0,
        tiled=True,
    )

    def user_operator(direction):
        shard_direction = lax.all_gather(direction, "item", axis=0, tiled=True)
        slot_terms = slot_products(
            shard_direction.reshape(-1, block_size, factor_rank),
            item_blocks,
            confidence,
            row_ids,
            col_ids,
        )
        summed = lax.psum_scatter(
            block_sum(slot_terms, row_ids, user_rows * lax.axis_size("item"), block_size),
            "item",
            scatter_dimension=0,
            tiled=True,
        )
        return (
            summed
            + user_weight * jnp.dot(direction, item_gram, precision=highest)
            + ridge * direction
        )

    user_factors = conjugate(user_side, user_operator)
    user_shard = lax.all_gather(user_factors, "item", axis=0, tiled=True)
    user_blocks = user_shard.reshape(-1, block_size, factor_rank)
    user_gram = lax.psum(jnp.dot(user_factors.T, user_factors, precision=highest), ("user", "item"))
    item_weight = unobserved / (user_factors.shape[0] * user_devices * item_devices)
    confidence_cols = jnp.swapaxes(confidence, 1, 2)
    slot_users = jnp.take(user_blocks, row_ids, axis=0)
    item_terms = jnp.einsum("tij,tik->tjk", weights, slot_users, precision=highest)
    item_side = lax.psum_scatter(
        block_sum(item_terms, col_ids, item_rows * lax.axis_size("user"), block_size),
        "user",
        scatter_dimension=0,
        tiled=True,
    )

    def item_operator(direction):
        shard_direction = lax.all_gather(direction, "user", axis=0, tiled=True)
        slot_terms = slot_products(
            shard_direction.reshape(-1, block_size, factor_rank),
            user_blocks,
            confidence_cols,
            col_ids,
            row_ids,
        )
        summed = lax.psum_scatter(
            block_sum(slot_terms, col_ids, item_rows * lax.axis_size("user"), block_size),
            "user",
            scatter_dimension=0,
            tiled=True,
        )
        return (
            summed
            + item_weight * jnp.dot(direction, user_gram, precision=highest)
            + ridge * direction
        )

    item_factors = conjugate(item_side, item_operator)
    return (user_factors, item_factors)


def solution(mesh):
    in_specs = (
        P(("item", "user"), None),
        P("user", "item", None),
        P("user", "item", None),
        P("user", "item"),
        P("user", "item", None, None, None),
    )
    out_specs = (P(("user", "item"), None), P(("item", "user"), None))
    return jax.shard_map(shards, mesh=mesh, in_specs=in_specs, out_specs=out_specs, check_vma=False)
```

profile of v0, /device:TPU:0, one launch (start us, length us, event | category | flops | bytes accessed | tf_op | source)
XLA Modules:
  0.0 852.1 jit_solution(14742828375242877306)
XLA Ops:
  10.0 35.4 %all_gather.24 = f32[1024,128]{1,0:T(8,128)} all-gather(f32[128,128]{1,0:T(8,128)} %param.7), channel_id=1, replica_groups=mesh['user'=8,'item'=4] {'user'}, dimensions={0}, use_global_device_ids=true | all-gather | bytes 589824 | tf_op jit(solution)/shard_map/all_gather | solution.py:66
  49.1 6.3 fusion.33
  62.3 21.8 %reduce-scatter.9.cloned.1.call-done = f32[256,128]{0,1:T(8,128)} async-done(((f32[1024,128]{0,1:T(8,128)}), f32[256,128]{0,1:T(8,128)}) %reduce-scatter.9.cloned.1.call-update) | async-done | bytes 131088 | tf_op jit(solution)/shard_map/reduce_scatter | solution.py:73
  84.1 8.2 all_gather.25
  97.8 9.4 %fusion.22 = f32[48,128,128]{2,1,0:T(8,128)S(1)} fusion(f32[48,128,128]{2,1,0:T(8,128)} %gather_fusion.1, f32[48,128,128]{2,1,0:T(8,128)} %gather_fusion, pred[48]{0:T(512)(128)(4,1)S(1)} %compare_and_fusion, pred[48]{0:T(512)(128)(4,1)S(1)} %get-tuple-element.21), kind=kOutput, calls=%fused_computation.36 | convolution fusion | flops 1209532416 | bytes 9437280 | tf_op jit(solution)/shard_map/tik,tjk->tij/dot_general | solution.py:27
  107.3 4.1 fusion.28
  117.3 68.8 %all-reduce.3.cloned.1.call-done = f32[128,128]{1,0:T(8,128)} async-done(((f32[128,128]{1,0:T(8,128)}), f32[128,128]{1,0:T(8,128)}) %all-reduce.3.cloned.1.call-update) | async-done | bytes 65552 | tf_op jit(solution)/shard_map/psum | solution.py:68
  188.0 9.2 %all_gather.26 = f32[1024,128]{0,1:T(8,128)} all-gather(f32[256,128]{0,1:T(8,128)S(1)} %multiply_add_fusion.2), channel_id=1, replica_groups=mesh['user'=8,'item'=4] {'item'}, dimensions={0}, use_global_device_ids=true | all-gather | bytes 655360 | tf_op jit(solution)/shard_map/all_gather | solution.py:81
  202.8 9.4 %fusion.20 = f32[48,128,128]{2,1,0:T(8,128)S(1)} fusion(f32[48,128,128]{2,1,0:T(8,128)} %gather_fusion.2, f32[48,128,128]{2,1,0:T(8,128)} %gather_fusion, pred[48]{0:T(512)(128)(4,1)S(1)} %compare_and_fusion, pred[48]{0:T(512)(128)(4,1)S(1)} %get-tuple-element.21), kind=kOutput, calls=%fused_computation.34 | convolution fusion | flops 1209532416 | bytes 9437280 | tf_op jit(solution)/shard_map/tik,tjk->tij/dot_general | solution.py:27
  212.2 5.4 fusion.26
  217.7 3.6 copy.37
  225.3 20.7 %reduce-scatter.13.cloned.1.call-done = f32[256,128]{0,1:T(8,128)} async-done(((f32[1024,128]{0,1:T(8,128)}), f32[256,128]{0,1:T(8,128)}) %reduce-scatter.13.cloned.1.call-update) | async-done | bytes 131088 | tf_op jit(solution)/shard_map/reduce_scatter | solution.py:89
  249.9 7.4 all_gather.27
  263.0 9.4 %fusion.18 = f32[48,128,128]{2,1,0:T(8,128)S(1)} fusion(f32[48,128,128]{2,1,0:T(8,128)} %gather_fusion.3, f32[48,128,128]{2,1,0:T(8,128)} %gather_fusion, pred[48]{0:T(512)(128)(4,1)S(1)} %compare_and_fusion, pred[48]{0:T(512)(128)(4,1)S(1)} %get-tuple-element.21), kind=kOutput, calls=%fused_computation.32 | convolution fusion | flops 1209532416 | bytes 9437280 | tf_op jit(solution)/shard_map/tik,tjk->tij/dot_general | solution.py:27
  272.5 5.4 fusion.24
  285.4 22.1 %reduce-scatter.15.cloned.1.call-done = f32[256,128]{0,1:T(8,128)} async-done(((f32[1024,128]{0,1:T(8,128)}), f32[256,128]{0,1:T(8,128)}) %reduce-scatter.15.cloned.1.call-update) | async-done | bytes 131088 | tf_op jit(solution)/shard_map/reduce_scatter | solution.py:89
  310.5 7.7 all_gather.28
  323.7 7.8 fusion.31
  338.5 61.9 %reduce-scatter.17.cloned.1.call-done = f32[128,128]{0,1:T(8,128)} async-done(((f32[1024,128]{0,1:T(8,128)}), f32[128,128]{0,1:T(8,128)}) %reduce-scatter.17.cloned.1.call-update) | async-done | bytes 65552 | tf_op jit(solution)/shard_map/reduce_scatter | solution.py:109
  400.4 33.8 %all_gather.29 = f32[1024,128]{0,1:T(8,128)} all-gather(f32[128,128]{0,1:T(8,128)} %reduce-scatter.17.cloned.1.call-done), channel_id=1, replica_groups=mesh['user'=8,'item'=4] {'user'}, dimensions={0}, use_global_device_ids=true | all-gather | bytes 589824 | tf_op jit(solution)/shard_map/all_gather | solution.py:117
  439.9 9.8 %fusion.16 = f32[48,128,128]{1,2,0:T(8,128)S(1)} fusion(f32[48,128,128]{2,1,0:T(8,128)} %gather_fusion.5, f32[48,128,128]{2,1,0:T(8,128)} %gather_fusion.4, pred[48]{0:T(512)(128)(4,1)S(1)} %compare_and_fusion, pred[48]{0:T(512)(128)(4,1)S(1)} %get-tuple-element.21), kind=kOutput, calls=%fused_computation.30 | convolution fusion | flops 1209532416 | bytes 9437280 | tf_op jit(solution)/shard_map/tik,tjk->tij/dot_general | solution.py:27
  449.6 5.8 fusion
  461.3 62.4 %all-reduce.5.cloned.1.call-done = f32[128,128]{1,0:T(8,128)} async-done(((f32[128,128]{1,0:T(8,128)}), f32[128,128]{1,0:T(8,128)}) %all-reduce.5.cloned.1.call-update) | async-done | bytes 65552 | tf_op jit(solution)/shard_map/psum | solution.py:104
  523.7 67.0 %reduce-scatter.19.cloned.1.call-done = f32[128,128]{0,1:T(8,128)} async-done(((f32[1024,128]{0,1:T(8,128)}), f32[128,128]{0,1:T(8,128)}) %reduce-scatter.19.cloned.1.call-update) | async-done | bytes 65552 | tf_op jit(solution)/shard_map/reduce_scatter | solution.py:125
  592.0 33.6 %all_gather.30 = f32[1024,128]{0,1:T(8,128)} all-gather(f32[128,128]{0,1:T(8,128)S(1)} %multiply_add_fusion.5), channel_id=1, replica_groups=mesh['user'=8,'item'=4] {'user'}, dimensions={0}, use_global_device_ids=true | all-gather | bytes 589824 | tf_op jit(solution)/shard_map/all_gather | solution.py:117
  631.2 9.6 %fusion.14 = f32[48,128,128]{1,2,0:T(8,128)S(1)} fusion(f32[48,128,128]{2,1,0:T(8,128)} %gather_fusion.6, f32[48,128,128]{2,1,0:T(8,128)} %gather_fusion.4, pred[48]{0:T(512)(128)(4,1)S(1)} %compare_and_fusion, pred[48]{0:T(512)(128)(4,1)S(1)} %get-tuple-element.21), kind=kOutput, calls=%fused_computation.28 | convolution fusion | flops 1209532416 | bytes 9437280 | tf_op jit(solution)/shard_map/tik,tjk->tij/dot_general | solution.py:27
  640.9 7.2 fusion.1
  655.7 61.4 %reduce-scatter.21.cloned.1.call-done = f32[128,128]{0,1:T(8,128)} async-done(((f32[1024,128]{0,1:T(8,128)}), f32[128,128]{0,1:T(8,128)}) %reduce-scatter.21.cloned.1.call-update) | async-done | bytes 65552 | tf_op jit(solution)/shard_map/reduce_scatter | solution.py:125
  720.3 33.5 %all_gather.31 = f32[1024,128]{0,1:T(8,128)} all-gather(f32[128,128]{0,1:T(8,128)S(1)} %multiply_add_fusion.4), channel_id=1, replica_groups=mesh['user'=8,'item'=4] {'user'}, dimensions={0}, use_global_device_ids=true | all-gather | bytes 589824 | tf_op jit(solution)/shard_map/all_gather | solution.py:117
  759.5 9.6 %fusion.12 = f32[48,128,128]{1,2,0:T(8,128)S(1)} fusion(f32[48,128,128]{2,1,0:T(8,128)} %gather_fusion.7, f32[48,128,128]{2,1,0:T(8,128)} %gather_fusion.4, pred[48]{0:T(512)(128)(4,1)S(1)} %compare_and_fusion, pred[48]{0:T(512)(128)(4,1)S(1)} %get-tuple-element.21), kind=kOutput, calls=%fused_computation.26 | convolution fusion | flops 1209532416 | bytes 9437280 | tf_op jit(solution)/shard_map/tik,tjk->tij/dot_general | solution.py:27
  769.1 7.2 fusion.2
  781.7 60.8 %reduce-scatter.23.cloned.1.call-done = f32[128,128]{0,1:T(8,128)} async-done(((f32[1024,128]{0,1:T(8,128)}), f32[128,128]{0,1:T(8,128)}) %reduce-scatter.23.cloned.1.call-update) | async-done | bytes 65552 | tf_op jit(solution)/shard_map/reduce_scatter | solution.py:125
  (153 shorter events, 109.4 us)
Async XLA Ops:
  8.0 76.1 %reduce-scatter.9.cloned.1.call-start = ((), (), s32[]{:S(2)}) async-start(), calls=%async_computation.8 | async-start | bytes 655360 | tf_op jit(solution)/shard_map/reduce_scatter | solution.py:73
  10.0 39.1 %copy-start.18 = (s32[1024]{0:T(1024)}, s32[1024]{0:T(1024)S(1)}, u32[]{:S(2)}) copy-start(s32[1024]{0:T(1024)S(1)} %pad_clamp_fusion.1) | copy-start | bytes 12292
  49.1 6.3 copy-start.20
  55.4 5.9 copy-start.11
  61.2 124.9 %all-reduce.3.cloned.1.call-start = ((), (), s32[]{:S(2)}) async-start(), calls=%async_computation.10 | async-start | bytes 131072 | tf_op jit(solution)/shard_map/psum | solution.py:68
  62.2 123.9 %reduce-scatter.11.cloned.1.call-start = ((), (), s32[]{:S(2)}) async-start(), calls=%async_computation.9 | async-start | bytes 655360 | tf_op jit(solution)/shard_map/reduce_scatter | solution.py:89
  62.3 137.0 %copy-start.19 = (s32[1024]{0:T(1024)}, s32[1024]{0:T(1024)S(1)}, u32[]{:S(2)}) copy-start(s32[1024]{0:T(1024)S(1)} %pad_clamp_fusion) | copy-start | bytes 12292
  97.8 9.4 %copy-start.1 = (f32[48,128,128]{2,1,0:T(8,128)S(1)}, f32[48,128,128]{2,1,0:T(8,128)}, u32[]{:S(2)}) copy-start(f32[48,128,128]{2,1,0:T(8,128)} %gather_fusion) | copy-start | bytes 9437188
  111.4 74.7 %copy-start.7 = (f32[256,128]{0,1:T(8,128)S(1)}, f32[256,128]{0,1:T(8,128)}, u32[]{:S(2)}) copy-start(f32[256,128]{0,1:T(8,128)} %reduce-scatter.9.cloned.1.call-done) | copy-start | bytes 393220
  117.3 128.7 %reduce-scatter.13.cloned.1.call-start = ((), (), s32[]{:S(2)}) async-start(), calls=%async_computation.11 | async-start | bytes 655360 | tf_op jit(solution)/shard_map/reduce_scatter | solution.py:89
  202.8 9.4 %copy-start.2 = (f32[48,128,128]{2,1,0:T(8,128)S(1)}, f32[48,128,128]{2,1,0:T(8,128)}, u32[]{:S(2)}) copy-start(f32[48,128,128]{2,1,0:T(8,128)} %gather_fusion) | copy-start | bytes 9437188
  217.7 3.6 copy-start.21
  225.2 82.4 %reduce-scatter.15.cloned.1.call-start = ((), (), s32[]{:S(2)}) async-start(), calls=%async_computation.12 | async-start | bytes 655360 | tf_op jit(solution)/shard_map/reduce_scatter | solution.py:89
  263.0 9.4 %copy-start.3 = (f32[48,128,128]{2,1,0:T(8,128)S(1)}, f32[48,128,128]{2,1,0:T(8,128)}, u32[]{:S(2)}) copy-start(f32[48,128,128]{2,1,0:T(8,128)} %gather_fusion) | copy-start | bytes 9437188
  281.4 26.2 %copy-start.9 = (f32[256,128]{0,1:T(8,128)S(1)}, f32[256,128]{0,1:T(8,128)}, u32[]{:S(2)}) copy-start(f32[256,128]{0,1:T(8,128)} %copy-done.8) | copy-start | bytes 393220
  285.4 115.0 %reduce-scatter.17.cloned.1.call-start = ((), (), s32[]{:S(2)}) async-start(), calls=%async_computation.13 | async-start | bytes 589824 | tf_op jit(solution)/shard_map/reduce_scatter | solution.py:109
  323.7 7.9 copy-start.15
  337.5 186.2 %all-reduce.5.cloned.1.call-start = ((), (), s32[]{:S(2)}) async-start(), calls=%async_computation.15 | async-start | bytes 131072 | tf_op jit(solution)/shard_map/psum | solution.py:104
  338.4 252.3 %reduce-scatter.19.cloned.1.call-start = ((), (), s32[]{:S(2)}) async-start(), calls=%async_computation.14 | async-start | bytes 589824 | tf_op jit(solution)/shard_map/reduce_scatter | solution.py:125
  439.9 9.8 %copy-start.4 = (f32[48,128,128]{2,1,0:T(8,128)S(1)}, f32[48,128,128]{2,1,0:T(8,128)}, u32[]{:S(2)}) copy-start(f32[48,128,128]{2,1,0:T(8,128)} %gather_fusion.4) | copy-start | bytes 9437188
  455.4 135.3 %copy-start.10 = (f32[128,128]{0,1:T(8,128)S(1)}, f32[128,128]{0,1:T(8,128)}, u32[]{:S(2)}) copy-start(f32[128,128]{0,1:T(8,128)} %reduce-scatter.17.cloned.1.call-done) | copy-start | bytes 196612
  461.3 255.9 %reduce-scatter.21.cloned.1.call-start = ((), (), s32[]{:S(2)}) async-start(), calls=%async_computation.16 | async-start | bytes 589824 | tf_op jit(solution)/shard_map/reduce_scatter | solution.py:125
  591.9 39.3 %copy-start.24 = (f32[128]{0:T(128)}, f32[128]{0:T(128)S(1)}, u32[]{:S(2)}) copy-start(f32[128]{0:T(128)S(1)} %div.85) | copy-start | bytes 1540
  592.0 39.3 %copy-start.26 = (f32[128]{0:T(128)}, f32[128]{0:T(128)S(1)}, u32[]{:S(2)}) copy-start(f32[128]{0:T(128)S(1)} %get-tuple-element.11) | copy-start | bytes 1540
  631.2 9.6 %copy-start.5 = (f32[48,128,128]{2,1,0:T(8,128)S(1)}, f32[48,128,128]{2,1,0:T(8,128)}, u32[]{:S(2)}) copy-start(f32[48,128,128]{2,1,0:T(8,128)} %gather_fusion.4) | copy-start | bytes 9437188
  651.7 65.4 %copy-start.12 = (f32[128,128]{1,0:T(8,128)S(1)}, f32[128,128]{1,0:T(8,128)}, u32[]{:S(2)}) copy-start(f32[128,128]{1,0:T(8,128)} %all-reduce.5.cloned.1.call-done) | copy-start | bytes 196612
  655.7 186.9 %reduce-scatter.23.cloned.1.call-start = ((), (), s32[]{:S(2)}) async-start(), calls=%async_computation.17 | async-start | bytes 589824 | tf_op jit(solution)/shard_map/reduce_scatter | solution.py:125
  759.5 9.6 %copy-start.6 = (f32[48,128,128]{2,1,0:T(8,128)S(1)}, f32[48,128,128]{2,1,0:T(8,128)}, u32[]{:S(2)}) copy-start(f32[48,128,128]{2,1,0:T(8,128)} %gather_fusion.4) | copy-start | bytes 9437188
  778.9 63.7 %copy-start.13 = (f32[128,128]{1,0:T(8,128)S(1)}, f32[128,128]{1,0:T(8,128)}, u32[]{:S(2)}) copy-start(f32[128,128]{1,0:T(8,128)} %all-reduce.5.cloned.1.call-done) | copy-start | bytes 196612
  778.9 64.8 %copy-start.28 = (f32[128]{0:T(128)S(1)}, f32[128]{0:T(128)}, u32[]{:S(2)}) copy-start(f32[128]{0:T(128)} %copy-done.27) | copy-start | bytes 1540
  778.9 64.8 %copy-start.23 = (f32[128]{0:T(128)S(1)}, f32[128]{0:T(128)}, u32[]{:S(2)}) copy-start(f32[128]{0:T(128)} %copy-done.22) | copy-start | bytes 1540
  778.9 64.8 %copy-start.25 = (f32[128]{0:T(128)S(1)}, f32[128]{0:T(128)}, u32[]{:S(2)}) copy-start(f32[128]{0:T(128)} %copy-done.24) | copy-start | bytes 1540
  (7 other events, 7.9 us)
Sparse Core Ops, SparseCore 0:
  61.4 22.6 reduce-scatter.8
  117.4 22.6 reduce-scatter.10
  225.3 20.5 reduce-scatter.12
  285.5 22.0 reduce-scatter.14
Sparse Core Ops, SparseCore 1:
  67.9 118.2 all-reduce.2
  337.6 62.8 reduce-scatter.16
  407.4 116.2 all-reduce.4
  527.4 63.2 reduce-scatter.18
  655.8 61.3 reduce-scatter.20
  781.1 61.4 reduce-scatter.22
where the time goes:
time: 860 us; the launch traced here: 852 us
  waiting for transfers between devices  447 us (52%)
  blocking collectives  169 us (20%)
  matrix products  137 us (16%)
  local copies, waits for them, and re-layouts  75.5 us (9%)
  between operations  16.8 us (2%)
    reduce_scatter x3, waiting for transfers between devices, item_operator(): lax.psum_scatter(block_sum(slot_terms, col_ids, item_rows * lax.axis_size...  189 us
    all_gather x3, blocking collectives, item_operator(): shard_direction = lax.all_gather(direction, 'user', axis=0, tiled=True)  101 us
    psum x1, waiting for transfers between devices, shards(): lax.psum(jnp.dot(item_init.T, item_init, precision=highest), ('user', 'it...  68.8 us
    psum x1, waiting for transfers between devices, shards(): lax.psum(jnp.dot(user_factors.T, user_factors, precision=highest), ('user...  62.4 us
    reduce_scatter x1, waiting for transfers between devices, shards(): lax.psum_scatter(block_sum(item_terms, col_ids, item_rows * lax.axis_size...  61.9 us
    dot_general x6, matrix products, group_products(): scores = jnp.einsum('tik,tjk->tij', own_rows, other_rows, precision=highest)  57.3 us
    reduce_scatter x3, waiting for transfers between devices, user_operator(): lax.psum_scatter(block_sum(slot_terms, row_ids, user_rows * lax.axis_size...  42.8 us
    all_gather x1, blocking collectives, shards(): item_shard = lax.all_gather(item_init, 'user', axis=0, tiled=True)  35.4 us
  transfers between devices with their start and end apart: 10, of which 9 were waited for; matrix products, arithmetic and copies ran while one was open for 6% of the time, Pallas kernels for 0%

commit v1 on v0

--- a/solution.py
+++ b/solution.py
@@ -1,6 +1,10 @@
+import functools
+
 import jax
 import jax.numpy as jnp
 from jax import lax
+from jax.experimental import pallas as pl
+from jax.experimental.pallas import tpu as pltpu
 from jax.sharding import PartitionSpec as P
 
 UB = 2
@@ -11,6 +15,383 @@
 highest = lax.Precision.HIGHEST
 ridge = 5.0
 unobserved = 256.0
+
+f32 = jnp.float32
+bf16 = jnp.bfloat16
+MIB = 1 << 20
+DENSE_LIMIT = 8 * MIB
+
+
+def pair(value):
+    high = value.astype(bf16)
+    low = (value - high.astype(f32)).astype(bf16)
+    return high, low
+
+
+def row_sum(value):
+    return jnp.sum(value, axis=-1, keepdims=True)
+
+
+def split_rows(value):
+    high, low = pair(value)
+    return jnp.concatenate(
+        [jnp.concatenate([high, low], axis=1), jnp.concatenate([low, high], axis=1)], axis=0
+    )
+
+
+def scores_of(lhs, factors):
+    rows = lhs.shape[0] // 2
+    both = lax.dot_general(lhs, factors, (((1,), (1,)), ((), ())), preferred_element_type=f32)
+    return both[:rows] + both[rows:]
+
+
+def tile_terms(direction, conf_ref, pairs_ref, width):
+    rows, rank = direction.shape
+    lhs = split_rows(direction)
+    total = jnp.zeros((rows, rank), f32)
+    for start in range(0, conf_ref.shape[1], width):
+        factors = pairs_ref[start : start + width, :]
+        weighted = scores_of(lhs, factors) * conf_ref[:, start : start + width]
+        high, low = pair(weighted)
+        out = jnp.dot(jnp.concatenate([high, low], axis=0), factors, preferred_element_type=f32)
+        total = total + (
+            (out[:rows, :rank] + out[:rows, rank:]) + (out[rows:, :rank] + out[rows:, rank:])
+        )
+    return total
+
+
+def tile_squares(direction, conf_ref, pairs_ref, width):
+    rows, rank = direction.shape
+    lhs = split_rows(direction)
+    total = jnp.zeros((rows, rank), f32)
+    for start in range(0, conf_ref.shape[1], width):
+        scores = scores_of(lhs, pairs_ref[start : start + width, :])
+        squares = scores * scores * conf_ref[:, start : start + width]
+        for part in range(0, width, rank):
+            total = total + squares[:, part : part + rank]
+    return total
+
+
+def side_of(weight_ref, pairs_ref):
+    rank = pairs_ref.shape[1] // 2
+    both = jnp.dot(weight_ref[...], pairs_ref[...], preferred_element_type=f32)
+    return both[:, :rank] + both[:, rank:]
+
+
+def advance(solution, residual, direction, product):
+    norm_now = row_sum(residual * residual)
+    step_length = norm_now / row_sum(direction * product)
+    solution = solution + step_length * direction
+    residual = residual - step_length * product
+    direction = residual + row_sum(residual * residual) / norm_now * direction
+    return solution, residual, direction
+
+
+def pack_kernel(slots, ids_ref, conf_ref, send_ref):
+    slot_total, block, _ = conf_ref.shape
+    owners = send_ref.shape[0]
+    shift = ids_ref[slot_total]
+    count = ids_ref[2 * slot_total]
+
+    def one(owner, carry):
+        first = lax.rem(owner - shift + owners, owners)
+        for slot in range(slots):
+            place = first + owners * slot
+            used = place < jnp.minimum(count, slot_total)
+            held = jnp.minimum(place, slot_total - 1)
+            send_ref[owner, slot * block : (slot + 1) * block, :] = jnp.where(used, conf_ref[held], 0)
+            send_ref[owner, slots * block + slot, :] = jnp.full((block,), ids_ref[held], jnp.int32)
+        return carry
+
+    lax.fori_loop(0, owners, one, 0)
+
+
+def user_tiles_kernel(weight_zero, own_ids, other_ids, conf_ref, half_ref, dense_ref, weight_ref):
+    slot_total, block, _ = conf_ref.shape
+    half = block // 2
+    owners = dense_ref.shape[1] // block // 2
+    me = lax.axis_index("user")
+    core = lax.rem(lax.axis_index("item"), 2)
+    dense_ref[...] = jnp.full(dense_ref.shape, weight_zero, f32)
+    weight_ref[...] = jnp.zeros(weight_ref.shape, bf16)
+
+    def place(ids, slot, base, counts):
+        row = pl.multiple_of(ids[slot] * half, half)
+        col = pl.multiple_of((base + jnp.bitwise_xor(ids[slot_total + slot], me)) * block, block)
+        at = (pl.ds(row, half), pl.ds(col, block))
+        value = counts.astype(f32)
+        dense_ref[at] = dense_ref[at] + value
+        weight_ref[at] = weight_ref[at] + jnp.where(value > 0.0, 1.0 + value, 0.0).astype(bf16)
+
+    def own(slot, carry):
+        rows = pl.ds(pl.multiple_of(core * half, half), half)
+        place(own_ids, slot, 0, conf_ref[slot, rows, :])
+        return carry
+
+    def other(slot, carry):
+        place(other_ids, slot, owners, half_ref[slot])
+        return carry
+
+    lax.fori_loop(0, jnp.minimum(own_ids[2 * slot_total], slot_total), own, 0)
+    lax.fori_loop(0, jnp.minimum(other_ids[2 * slot_total], slot_total), other, 0)
+
+
+def user_side_kernel(count, *refs):
+    pieces, (weight_ref, side_ref, pairs_ref) = refs[:count], refs[count:]
+    start = 0
+    for piece in pieces:
+        flat = piece[...].reshape(-1, piece.shape[-1])
+        high, low = pair(flat)
+        pairs_ref[start : start + flat.shape[0], :] = jnp.concatenate([high, low], axis=1)
+        start += flat.shape[0]
+    side_ref[...] = side_of(weight_ref, pairs_ref)
+
+
+def user_first_kernel(width, own_ref, other_ref, conf_ref, pairs_ref, side_ref, out_ref):
+    side = own_ref[...] + other_ref[...]
+    side_ref[...] = side
+    out_ref[...] = tile_terms(side, conf_ref, pairs_ref, width)
+
+
+def user_second_kernel(
+    width, side_ref, own_ref, other_ref, conf_ref, pairs_ref, x_ref, r_ref, d_ref, out_ref
+):
+    side = side_ref[...]
+    product = own_ref[...] + other_ref[...] + ridge * side
+    x, r, d = advance(jnp.zeros_like(side), side, side, product)
+    x_ref[...] = x
+    r_ref[...] = r
+    d_ref[...] = d
+    out_ref[...] = tile_terms(d, conf_ref, pairs_ref, width)
+
+
+def user_third_kernel(
+    width, x_in, r_in, d_in, own_ref, other_ref, conf_ref, pairs_ref, x_ref, r_ref, d_ref, sums_ref
+):
+    direction = d_in[...]
+    product = own_ref[...] + other_ref[...] + ridge * direction
+    x, r, d = advance(x_in[...], r_in[...], direction, product)
+    x_ref[...] = x
+    r_ref[...] = r
+    d_ref[...] = d
+    squares = tile_squares(d, conf_ref, pairs_ref, width)
+    ones = jnp.ones((8, squares.shape[1]), bf16)
+    sums = jnp.zeros(sums_ref.shape, f32)
+    for unused in range(3):
+        part = squares.astype(bf16)
+        squares = squares - part.astype(f32)
+        sums = sums + lax.dot_general(ones, part, (((1,), (1,)), ((), ())), preferred_element_type=f32)
+    sums_ref[...] = sums
+
+
+def user_last_kernel(blocks, x_in, r_in, d_in, own_ref, other_ref, out_ref, keep_ref, give_ref):
+    place = lax.axis_index("item")
+    residual = r_in[...]
+    direction = d_in[...]
+    sums = jnp.transpose(own_ref[...] + other_ref[...])[:, :1]
+    length = row_sum(residual * residual) / (sums + ridge * row_sum(direction * direction))
+    out_ref[...] = x_in[...] + length * direction
+    rows = keep_ref.shape[0]
+    keep_ref[...] = out_ref[pl.ds(pl.multiple_of(place * rows, rows), rows), :]
+    other = jnp.bitwise_xor(place, 1)
+    give_ref[...] = out_ref[pl.ds(pl.multiple_of(other * rows, rows), rows), :]
+
+
+def item_tiles_kernel(weight_zero, slots, row_blocks, ids_ref, tiles_ref, dense_ref, weight_ref):
+    owners = tiles_ref.shape[0]
+    block = tiles_ref.shape[2]
+    me = lax.axis_index("user")
+    dense_ref[...] = jnp.full(dense_ref.shape, weight_zero, f32)
+    weight_ref[...] = jnp.zeros(weight_ref.shape, bf16)
+
+    def one(source, carry):
+        base = jnp.bitwise_xor(source, me) * row_blocks
+        for slot in range(slots):
+            value = jnp.transpose(tiles_ref[source, slot * block : (slot + 1) * block, :].astype(f32))
+            col = pl.multiple_of((base + ids_ref[source * slots + slot]) * block, block)
+            at = (slice(None), pl.ds(col, block))
+            dense_ref[at] = dense_ref[at] + value
+            weight_ref[at] = weight_ref[at] + jnp.where(value > 0.0, 1.0 + value, 0.0).astype(bf16)
+        return carry
+
+    lax.fori_loop(0, owners, one, 0)
+
+
+def item_kernel(width, row_blocks, *refs):
+    pieces, (conf_ref, weight_ref, out_ref, pairs_ref) = refs[:-4], refs[-4:]
+    block = out_ref.shape[0]
+    half = block // 2
+    core = lax.rem(lax.axis_index("item"), 2)
+    group = 0
+    for own_half, piece in pieces_in_order(pieces):
+        offset = pl.multiple_of((core if own_half else 1 - core) * half, half)
+        for row in range(row_blocks):
+            high, low = pair(piece[row * half : (row + 1) * half, :])
+            pairs_ref[pl.ds((group // 2 * row_blocks + row) * block + offset, half), :] = (
+                jnp.concatenate([high, low], axis=1)
+            )
+        group += 1
+    side = side_of(weight_ref, pairs_ref)
+    x, r, d = jnp.zeros_like(side), side, side
+    for unused in range(CG_ITERS - 1):
+        product = tile_terms(d, conf_ref, pairs_ref, width) + ridge * d
+        x, r, d = advance(x, r, d, product)
+    bottom = row_sum(tile_squares(d, conf_ref, pairs_ref, width)) + ridge * row_sum(d * d)
+    out_ref[...] = x + row_sum(r * r) / bottom * d
+
+
+def pieces_in_order(pieces):
+    return [(place % 2 == 0, piece) for place, piece in enumerate(pieces)]
+
+
+VMEM = pltpu.VMEM
+SMEM = pltpu.SMEM
+
+
+def call(kernel, outs, *operands, scalars=0, flops=0, scratch=(), limit=48):
+    size = sum(op.size * op.dtype.itemsize for op in operands)
+    size += sum(out.size * out.dtype.itemsize for out in outs)
+    spaces = [SMEM] * scalars + [VMEM] * (len(operands) - scalars)
+    return pl.pallas_call(
+        kernel,
+        out_shape=tuple(outs),
+        in_specs=[pl.BlockSpec(memory_space=space) for space in spaces],
+        out_specs=tuple(pl.BlockSpec(memory_space=VMEM) for unused in outs),
+        scratch_shapes=scratch,
+        compiler_params=pltpu.CompilerParams(vmem_limit_bytes=limit * MIB),
+        cost_estimate=pl.CostEstimate(flops=flops, bytes_accessed=size, transcendentals=0),
+    )(*operands)
+
+
+def shaped(shape, dtype=f32):
+    return jax.ShapeDtypeStruct(shape, dtype)
+
+
+def dense_shards(item_init, tile_rows, tile_cols, tile_count, conf):
+    slot_total = tile_rows.shape[-1]
+    block, rank = conf.shape[-1], item_init.shape[1]
+    half = block // 2
+    n_item, n_user = lax.axis_size("item"), lax.axis_size("user")
+    row_blocks = UB * n_item
+    rows = row_blocks * half
+    slots = -(-slot_total // n_user)
+    width = 2 * rank
+    me = lax.axis_index("item")
+    core = lax.rem(me, 2)
+
+    def swap(value, axis, mask):
+        size = n_item if axis == "item" else n_user
+        return lax.ppermute(value, axis, [(place, place ^ mask) for place in range(size)])
+
+    def others(value):
+        total = value
+        mask = 2
+        while mask < n_item:
+            moved = swap(total, "item", mask)
+            if mask * 2 >= n_item:
+                return total, moved
+            total = total + moved
+            mask *= 2
+
+    conf = conf.reshape(slot_total, block, block)
+    ids = jnp.concatenate(
+        [tile_rows.reshape(-1), tile_cols.reshape(-1), tile_count.reshape(-1)]
+    ).astype(jnp.int32)
+
+    with jax.named_scope("gather_items"):
+        pieces = {0: item_init, 1: swap(item_init, "user", 1)}
+        for mask in range(2, n_user, 2):
+            pieces[mask] = swap(item_init, "user", mask)
+        for mask in range(2, n_user, 2):
+            pieces[mask + 1] = swap(pieces[mask], "user", 1)
+        own_items = jnp.stack([pieces[mask] for mask in range(n_user)])
+        other_items = swap(own_items, "item", 1)
+
+    with jax.named_scope("user_tiles"):
+        other_ids = swap(ids, "item", 1)
+        given = lax.dynamic_slice(conf, (0, (1 - core) * half, 0), (slot_total, half, block))
+        other_half = swap(given, "item", 1)
+        columns = 2 * n_user * block
+        user_conf, user_weight = call(
+            functools.partial(user_tiles_kernel, unobserved / (item_init.shape[0] * n_user * n_item)),
+            (shaped((rows, columns)), shaped((rows, columns), bf16)),
+            ids, other_ids, conf, other_half, scalars=2, flops=10 ** 9,
+        )
+
+    with jax.named_scope("send_tiles"):
+        tied_ids, tied_conf, own_items = lax.optimization_barrier((ids, conf, own_items))
+        (packed,) = call(
+            functools.partial(pack_kernel, slots),
+            (shaped((n_user, slots * block + 8, block), jnp.int32),),
+            tied_ids, tied_conf, scalars=1, flops=10 ** 9,
+        )
+        item_tiles = lax.all_to_all(packed, "user", 0, 0, tiled=True)
+
+    cost = 2 * rows * columns * rank
+    state = shaped((rows, rank))
+    with jax.named_scope("user_cg"):
+        part, pairs = call(
+            functools.partial(user_side_kernel, 2),
+            (state, shaped((columns, 2 * rank), bf16)),
+            own_items, other_items, user_weight, flops=2 * cost,
+        )
+        side, part = call(
+            functools.partial(user_first_kernel, width), (state, state),
+            *others(part), user_conf, pairs, flops=6 * cost,
+        )
+        x, r, d, part = call(
+            functools.partial(user_second_kernel, width), (state,) * 4,
+            side, *others(part), user_conf, pairs, flops=6 * cost,
+        )
+        x, r, d, sums = call(
+            functools.partial(user_third_kernel, width), (state,) * 3 + (shaped((8, rows)),),
+            x, r, d, *others(part), user_conf, pairs, flops=3 * cost,
+        )
+        shard = shaped((UB * half, rank))
+        users, keep, give = call(
+            functools.partial(user_last_kernel, row_blocks), (state, shard, shard),
+            x, r, d, *others(sums), flops=10 ** 6,
+        )
+        taken = swap(give, "item", 1)
+        keep, taken = keep.reshape(UB, half, rank), taken.reshape(UB, half, rank)
+        user_factors = jnp.stack(
+            [jnp.where(core == 0, keep, taken), jnp.where(core == 0, taken, keep)], axis=1
+        ).reshape(UB * block, rank)
+
+    with jax.named_scope("gather_users"):
+        pieces = {0: users, 1: swap(users, "user", 1)}
+        for mask in range(2, n_user, 2):
+            pieces[mask] = swap(users, "user", mask)
+        for mask in range(2, n_user, 2):
+            pieces[mask + 1] = swap(pieces[mask], "user", 1)
+        ordered = []
+        for mask in range(n_user):
+            ordered += [pieces[mask], swap(pieces[mask], "item", 1)]
+
+    with jax.named_scope("item_half"):
+        row_ids = item_tiles[:, slots * block : slots * block + slots, 0].reshape(-1)
+        columns = n_user * row_blocks * block
+        item_conf, item_weight = call(
+            functools.partial(
+                item_tiles_kernel, unobserved / (user_factors.shape[0] * n_user * n_item), slots, row_blocks
+            ),
+            (shaped((block, columns)), shaped((block, columns), bf16)),
+            row_ids, item_tiles, scalars=1, flops=10 ** 9,
+        )
+        (item_factors,) = call(
+            functools.partial(item_kernel, width, row_blocks),
+            (shaped((block, rank)),),
+            *ordered, item_conf, item_weight, flops=20 * 2 * block * columns * rank,
+            scratch=(pltpu.VMEM((columns, 2 * rank), bf16),),
+        )
+    return (user_factors, item_factors)
+
+
+def fits_dense(mesh):
+    n_user, n_item = mesh.shape["user"], mesh.shape["item"]
+    block = 128
+    user_bytes = UB * n_item * block * n_user * block * 4
+    return user_bytes <= DENSE_LIMIT and n_item % 2 == 0 and n_user % 2 == 0
 
 
 def block_sum(slot_terms, block_ids, row_count, block_size):
@@ -147,4 +528,5 @@
         P("user", "item", None, None, None),
     )
     out_specs = (P(("user", "item"), None), P(("item", "user"), None))
-    return jax.shard_map(shards, mesh=mesh, in_specs=in_specs, out_specs=out_specs, check_vma=False)
+    program = dense_shards if fits_dense(mesh) else shards
+    return jax.shard_map(program, mesh=mesh, in_specs=in_specs, out_specs=out_specs, check_vma=False)

time: 860 us -> 150 us (0.17)
  waiting for transfers between devices: 447 us -> 68.6 us
  blocking collectives: 169 us -> 0 us
  matrix products: 137 us -> 0 us
  local copies, waits for them, and re-layouts: 75.5 us -> 7.62 us
  Pallas kernels: 0 us -> 43.3 us
  starting transfers between devices: 0.43 us -> 27.4 us
  between operations: 16.8 us -> 1.48 us
    reduce_scatter x8 -> x0, waiting for transfers between devices: 316 us -> none  [the longest x3 189 us: item_operator(): lax.psum_scatter(block_sum(slot_terms, col_ids, item_rows * lax.axis_size...]
    all_gather x8 -> x0, blocking collectives: 169 us -> none  [the longest x3 101 us: item_operator(): shard_direction = lax.all_gather(direction, 'user', axis=0, tiled=True)]
    dot_general x30 -> x0, matrix products: 137 us -> none  [the longest x6 57.3 us: group_products(): scores = jnp.einsum('tik,tjk->tij', own_rows, other_rows, precision=highest)]
    psum x2 -> x0, waiting for transfers between devices: 131 us -> none  [the longest x1 68.8 us: shards(): lax.psum(jnp.dot(item_init.T, item_init, precision=highest), ('user', 'it...]
    ppermute x0 -> x30, waiting for transfers between devices: none -> 68.6 us  [swap(): lax.ppermute(value, axis, [(place, place ^ mask) for place in range(size)])]
    pallas_call x0 -> x9, Pallas kernels: none -> 43.3 us  [call(): pl.pallas_call(kernel, out_shape=tuple(outs), in_specs=[pl.BlockSpec(memo...]
    gather x8 -> x0, local copies, waits for them, and re-layouts: 28.6 us -> none  [the longest x6 21.4 us: group_products(): own_rows = jnp.take(own_blocks, own_ids, axis=0)]
    ppermute x0 -> x30, starting transfers between devices: none -> 22.7 us  [swap(): lax.ppermute(value, axis, [(place, place ^ mask) for place in range(size)])]
  transfers between devices with their start and end apart: 10 -> 31, of which waited for: 9 -> 14; matrix products, arithmetic and copies ran while one was open for 6% -> 2% of each run, Pallas kernels for 0% -> 18%
where the time goes in v1:
time: 150 us; the launch traced here: 149 us
  waiting for transfers between devices  68.6 us (46%)
  Pallas kernels  43.3 us (29%)
  starting transfers between devices  27.4 us (18%)
  local copies, waits for them, and re-layouts  7.62 us (5%)
    ppermute x30, waiting for transfers between devices, swap(): lax.ppermute(value, axis, [(place, place ^ mask) for place in range(size)])  68.6 us
    pallas_call x9, Pallas kernels, call(): pl.pallas_call(kernel, out_shape=tuple(outs), in_specs=[pl.BlockSpec(memo...  43.3 us
    ppermute x30, starting transfers between devices, swap(): lax.ppermute(value, axis, [(place, place ^ mask) for place in range(size)])  22.7 us
    unnamed x17, local copies, waits for them, and re-layouts  5.8 us
    all_to_all x1, starting transfers between devices, dense_shards(): item_tiles = lax.all_to_all(packed, 'user', 0, 0, tiled=True)  4.74 us
  transfers between devices with their start and end apart: 31, of which 14 were waited for; matrix products, arithmetic and copies ran while one was open for 2% of the time, Pallas kernels for 18%

profile of v1, /device:TPU:0, one launch (start us, length us, event | category | flops | bytes accessed | tf_op | source)
XLA Modules:
  0.0 149.1 jit_solution(2039120547860945717)
XLA Ops:
  0.6 3.0 %collective-permute-start = (f32[128,128]{1,0:T(8,128)}, f32[128,128]{1,0:T(8,128)S(1)}, u32[]{:S(2)}, u32[]{:S(2)}) collective-permute-start(f32[128,128]{1,0:T(8,128)} %param.5), channel_id=1, source_target_pairs={{0,4},{4,0},{8,12},{12,8},{16,20},{20,16},{24,28},{28,24},{1,5},{5... | collective-permute-start | bytes 196616 | tf_op jit(solution)/shard_map/gather_items/ppermute | solution.py:284
  3.7 1.6 %collective-permute-start.1 = (f32[128,128]{1,0:T(8,128)}, f32[128,128]{1,0:T(8,128)S(1)}, u32[]{:S(2)}, u32[]{:S(2)}) collective-permute-start(f32[128,128]{1,0:T(8,128)} %param.5), channel_id=1, source_target_pairs={{0,8},{4,12},{8,0},{12,4},{16,24},{20,28},{24,16},{28,20},{1,9},{5... | collective-permute-start | bytes 196616 | tf_op jit(solution)/shard_map/gather_items/ppermute | solution.py:284
  5.2 2.6 %collective-permute-start.3 = (f32[128,128]{1,0:T(8,128)}, f32[128,128]{1,0:T(8,128)S(1)}, u32[]{:S(2)}, u32[]{:S(2)}) collective-permute-start(f32[128,128]{1,0:T(8,128)} %param.5), channel_id=1, source_target_pairs={{0,16},{4,20},{8,24},{12,28},{16,0},{20,4},{24,8},{28,12},{1,17},{... | collective-permute-start | bytes 196616 | tf_op jit(solution)/shard_map/gather_items/ppermute | solution.py:284
  10.7 1.8 %collective-permute-done.3 = f32[128,128]{1,0:T(8,128)S(1)} collective-permute-done((f32[128,128]{1,0:T(8,128)}, f32[128,128]{1,0:T(8,128)S(1)}, u32[]{:S(2)}, u32[]{:S(2)}) %collective-permute-start.3) | collective-permute-done | bytes 65568 | tf_op jit(solution)/shard_map/gather_items/ppermute | solution.py:284
  13.0 1.1 collective-permute-done.5
  14.6 2.1 %collective-permute-done.4 = f32[128,128]{1,0:T(8,128)S(1)} collective-permute-done((f32[128,128]{1,0:T(8,128)S(1)}, f32[128,128]{1,0:T(8,128)S(1)}, u32[]{:S(2)}, u32[]{:S(2)}) %collective-permute-start.4) | collective-permute-done | bytes 65568 | tf_op jit(solution)/shard_map/gather_items/ppermute | solution.py:284
  16.7 1.6 %collective-permute-done.6 = f32[128,128]{1,0:T(8,128)S(1)} collective-permute-done((f32[128,128]{1,0:T(8,128)S(1)}, f32[128,128]{1,0:T(8,128)S(1)}, u32[]{:S(2)}, u32[]{:S(2)}) %collective-permute-start.6) | collective-permute-done | bytes 65568 | tf_op jit(solution)/shard_map/gather_items/ppermute | solution.py:284
  19.2 1.9 %copy-done = s32[1,1,48,128,128]{4,3,2,1,0:T(8,128)S(1)} copy-done((s32[1,1,48,128,128]{4,3,2,1,0:T(8,128)S(1)}, s32[1,1,48,128,128]{4,3,2,1,0:T(8,128)}, u32[]{:S(2)}) %copy-start) | copy-done | bytes 3145752
  21.0 2.8 %send_tiles.1 = s32[8,776,128]{2,1,0:T(8,128)} custom-call(s32[97]{0:T(128)S(1)} %pad_add_fusion.own_ids.ids_ref, s32[48,128,128]{2,1,0:T(8,128)S(1)} %bitcast.27), custom_call_target="tpu_custom_call" | custom-call | flops 1000000000 | bytes 6324612 | tf_op jit(solution)/shard_map/send_tiles/pallas_call | solution.py:255
  23.8 4.7 %all-to-all-start = ((s32[8,776,128]{2,1,0:T(8,128)}), s32[8,776,128]{2,1,0:T(8,128)}, u32[]{:S(2)}, u32[]{:S(2)}) async-start(s32[8,776,128]{2,1,0:T(8,128)} %send_tiles.1), calls=%async_computation | async-start | bytes 6356992 | tf_op jit(solution)/shard_map/send_tiles/all_to_all | solution.py:328
  30.1 2.8 %collective-permute-done.8.other_ids = s32[97]{0:T(128)S(1)} collective-permute-done((s32[97]{0:T(128)S(1)}, s32[97]{0:T(128)S(1)}, u32[]{:S(2)}, u32[]{:S(2)}) %collective-permute-start.8) | collective-permute-done | bytes 420 | tf_op jit(solution)/shard_map/user_tiles/ppermute | solution.py:284
  32.9 5.9 %user_tiles.1 = (f32[512,2048]{1,0:T(8,128)}, bf16[512,2048]{1,0:T(8,128)(2,1)S(1)}) custom-call(s32[97]{0:T(128)S(1)} %pad_add_fusion.own_ids.ids_ref, s32[97]{0:T(128)S(1)} %collective-permute-done.8.other_ids, s32[48,128,128]{2,1,0:T(8,128)} %bitcast.26, s32[48,64,128]{2,1,0:T(8,128)S(1)} %collective-permute-done.9.half_ref), custom_call_target="tpu_custom_call" | custom-call | flops 1000000000 | bytes 11010824 | tf_op jit(solution)/shard_map/user_tiles/pallas_call | solution.py:255
  39.6 1.1 collective-permute-start.10
  40.7 7.3 %collective-permute-done.10.other_ref = f32[512,128]{1,0:T(8,128)S(1)} collective-permute-done((f32[512,128]{1,0:T(8,128)S(1)}, f32[512,128]{1,0:T(8,128)S(1)}, u32[]{:S(2)}, u32[]{:S(2)}) %collective-permute-start.10) | collective-permute-done | bytes 262176 | tf_op jit(solution)/shard_map/user_cg/ppermute | solution.py:284
  48.0 5.1 %user_cg.6 = (f32[512,128]{1,0:T(8,128)S(1)}, f32[512,128]{1,0:T(8,128)S(1)}) custom-call(f32[512,128]{1,0:T(8,128)S(1)} %get-tuple-element.26.own_ref, f32[512,128]{1,0:T(8,128)S(1)} %collective-permute-done.10.other_ref, f32[512,2048]{1,0:T(8,128)} %get-tuple-element.27.conf_ref, bf16[2048,256]{1,0:T(8,128)(2,1)S(1)} %get-tuple-element.28.pairs_ref), custom_call_target="tpu_custom_call" | custom-call | flops 1610612736 | bytes 6291456 | tf_op jit(solution)/shard_map/user_cg/pallas_call | solution.py:255
  54.2 6.6 %collective-permute-done.11.other_ref = f32[512,128]{1,0:T(8,128)S(1)} collective-permute-done((f32[512,128]{1,0:T(8,128)S(1)}, f32[512,128]{1,0:T(8,128)S(1)}, u32[]{:S(2)}, u32[]{:S(2)}) %collective-permute-start.11) | collective-permute-done | bytes 262176 | tf_op jit(solution)/shard_map/user_cg/ppermute | solution.py:284
  60.8 5.2 %user_cg.7 = (f32[512,128]{1,0:T(8,128)S(1)}, f32[512,128]{1,0:T(8,128)S(1)}, f32[512,128]{1,0:T(8,128)S(1)}, f32[512,128]{1,0:T(8,128)S(1)}) custom-call(f32[512,128]{1,0:T(8,128)S(1)} %get-tuple-element.29.side_ref, f32[512,128]{1,0:T(8,128)S(1)} %get-tuple-element.30.own_ref, f32[512,128]{1,0:T(8,128)S(1)} %collective-permute-done.11.other_ref, ...), custom_call_target="tpu_custom_call" | custom-call | flops 1610612736 | bytes 7077888 | tf_op jit(solution)/shard_map/user_cg/pallas_call | solution.py:255
  67.1 5.8 %collective-permute-done.12.other_ref = f32[512,128]{1,0:T(8,128)S(1)} collective-permute-done((f32[512,128]{1,0:T(8,128)S(1)}, f32[512,128]{1,0:T(8,128)S(1)}, u32[]{:S(2)}, u32[]{:S(2)}) %collective-permute-start.12) | collective-permute-done | bytes 262176 | tf_op jit(solution)/shard_map/user_cg/ppermute | solution.py:284
  72.9 3.8 %user_cg.8 = (f32[512,128]{1,0:T(8,128)S(1)}, f32[512,128]{1,0:T(8,128)S(1)}, f32[512,128]{1,0:T(8,128)S(1)}, f32[8,512]{1,0:T(8,128)S(1)}) custom-call(f32[512,128]{1,0:T(8,128)S(1)} %get-tuple-element.31.x_in, f32[512,128]{1,0:T(8,128)S(1)} %get-tuple-element.32.r_in, f32[512,128]{1,0:T(8,128)S(1)} %get-tuple-element.33.d_in, ...), custom_call_target="tpu_custom_call" | custom-call | flops 805306368 | bytes 7356416 | tf_op jit(solution)/shard_map/user_cg/pallas_call | solution.py:255
  77.8 2.7 %collective-permute-done.13.other_ref = f32[8,512]{1,0:T(8,128)S(1)} collective-permute-done((f32[8,512]{1,0:T(8,128)S(1)}, f32[8,512]{1,0:T(8,128)S(1)}, u32[]{:S(2)}, u32[]{:S(2)}) %collective-permute-start.13) | collective-permute-done | bytes 16416 | tf_op jit(solution)/shard_map/user_cg/ppermute | solution.py:284
  81.0 1.7 %collective-permute-start.16 = (f32[512,128]{1,0:T(8,128)S(1)}, f32[512,128]{1,0:T(8,128)S(1)}, u32[]{:S(2)}, u32[]{:S(2)}) collective-permute-start(f32[512,128]{1,0:T(8,128)S(1)} %get-tuple-element.41.refs_0_), channel_id=1, source_target_pairs={{0,4},{4,0},{8,12},{12,8},{16,20},{20,16},{24,28},{28,24},{1,5},{5... | collective-permute-start | bytes 786440 | tf_op jit(solution)/shard_map/gather_users/ppermute | solution.py:284
  82.7 1.5 collective-permute-start.18
  84.1 2.4 %collective-permute-start.22 = (f32[512,128]{1,0:T(8,128)S(1)}, f32[512,128]{1,0:T(8,128)S(1)}, u32[]{:S(2)}, u32[]{:S(2)}) collective-permute-start(f32[512,128]{1,0:T(8,128)S(1)} %get-tuple-element.41.refs_0_), channel_id=1, source_target_pairs={{0,16},{4,20},{8,24},{12,28},{16,0},{20,4},{24,8},{28,12},{1,17},{... | collective-permute-start | bytes 786440 | tf_op jit(solution)/shard_map/gather_users/ppermute | solution.py:284
  87.1 6.4 %collective-permute-done.16.refs_2_ = f32[512,128]{1,0:T(8,128)S(1)} collective-permute-done((f32[512,128]{1,0:T(8,128)S(1)}, f32[512,128]{1,0:T(8,128)S(1)}, u32[]{:S(2)}, u32[]{:S(2)}) %collective-permute-start.16) | collective-permute-done | bytes 262176 | tf_op jit(solution)/shard_map/gather_users/ppermute | solution.py:284
  93.5 5.9 %collective-permute-done.18.refs_4_ = f32[512,128]{1,0:T(8,128)S(1)} collective-permute-done((f32[512,128]{1,0:T(8,128)S(1)}, f32[512,128]{1,0:T(8,128)S(1)}, u32[]{:S(2)}, u32[]{:S(2)}) %collective-permute-start.18) | collective-permute-done | bytes 262176 | tf_op jit(solution)/shard_map/gather_users/ppermute | solution.py:284
  99.5 17.7 %collective-permute-done.22.refs_8_ = f32[512,128]{1,0:T(8,128)S(1)} collective-permute-done((f32[512,128]{1,0:T(8,128)S(1)}, f32[512,128]{1,0:T(8,128)S(1)}, u32[]{:S(2)}, u32[]{:S(2)}) %collective-permute-start.22) | collective-permute-done | bytes 262176 | tf_op jit(solution)/shard_map/gather_users/ppermute | solution.py:284
  117.2 2.0 %collective-permute-start.28 = (f32[512,128]{1,0:T(8,128)S(1)}, f32[512,128]{1,0:T(8,128)S(1)}, u32[]{:S(2)}, u32[]{:S(2)}) collective-permute-start(f32[512,128]{1,0:T(8,128)S(1)} %collective-permute-done.26.refs_12_), channel_id=1, source_target_pairs={{0,4},{4,0},{8,12},{12,8},{16,20},{20,16},{24,28},{28,24},{1,5},{5... | collective-permute-start | bytes 786440 | tf_op jit(solution)/shard_map/gather_users/ppermute | solution.py:284
  119.9 3.9 %collective-permute-done.24.refs_10_ = f32[512,128]{1,0:T(8,128)S(1)} collective-permute-done((f32[512,128]{1,0:T(8,128)S(1)}, f32[512,128]{1,0:T(8,128)S(1)}, u32[]{:S(2)}, u32[]{:S(2)}) %collective-permute-start.24) | collective-permute-done | bytes 262176 | tf_op jit(solution)/shard_map/gather_users/ppermute | solution.py:284
  123.9 2.8 %collective-permute-done.28.refs_14_ = f32[512,128]{1,0:T(8,128)S(1)} collective-permute-done((f32[512,128]{1,0:T(8,128)S(1)}, f32[512,128]{1,0:T(8,128)S(1)}, u32[]{:S(2)}, u32[]{:S(2)}) %collective-permute-start.28) | collective-permute-done | bytes 262176 | tf_op jit(solution)/shard_map/gather_users/ppermute | solution.py:284
  128.4 6.3 %item_half.2 = (f32[128,8192]{1,0:T(8,128)}, bf16[128,8192]{1,0:T(8,128)(2,1)S(1)}) custom-call(s32[48]{0:T(128)S(1)} %squeeze.3.ids_ref, s32[8,776,128]{2,1,0:T(8,128)} %all-to-all-done.tiles_ref), custom_call_target="tpu_custom_call" | custom-call | flops 1000000000 | bytes 9470144 | tf_op jit(solution)/shard_map/item_half/pallas_call | solution.py:255
  134.7 1.4 copy-done.4
  136.1 13.0 %item_half.3 = f32[128,128]{1,0:T(8,128)} custom-call(f32[512,128]{1,0:T(8,128)S(1)} %get-tuple-element.41.refs_0_, f32[512,128]{1,0:T(8,128)S(1)} %collective-permute-done.15.refs_1_, f32[512,128]{1,0:T(8,128)S(1)} %collective-permute-done.16.refs_2_, f32[512,128]{1,0:T(8,128)S(1)} %collective-permute-done.17.refs_3_, ...), custom_call_target="tpu_custom_call" | custom-call | flops 5368709120 | bytes 10551296 | tf_op jit(solution)/shard_map/item_half/pallas_call | solution.py:255
  (64 shorter events, 13.1 us)
Async XLA Ops:
  0.6 10.0 %collective-permute-start = (f32[128,128]{1,0:T(8,128)}, f32[128,128]{1,0:T(8,128)S(1)}, u32[]{:S(2)}, u32[]{:S(2)}) collective-permute-start(f32[128,128]{1,0:T(8,128)} %param.5), channel_id=1, source_target_pairs={{0,4},{4,0},{8,12},{12,8},{16,20},{20,16},{24,28},{28,24},{1,5},{5... | collective-permute-start | bytes 196616 | tf_op jit(solution)/shard_map/gather_items/ppermute | solution.py:284
  3.7 6.7 %collective-permute-start.1 = (f32[128,128]{1,0:T(8,128)}, f32[128,128]{1,0:T(8,128)S(1)}, u32[]{:S(2)}, u32[]{:S(2)}) collective-permute-start(f32[128,128]{1,0:T(8,128)} %param.5), channel_id=1, source_target_pairs={{0,8},{4,12},{8,0},{12,4},{16,24},{20,28},{24,16},{28,20},{1,9},{5... | collective-permute-start | bytes 196616 | tf_op jit(solution)/shard_map/gather_items/ppermute | solution.py:284
  5.2 7.2 %collective-permute-start.3 = (f32[128,128]{1,0:T(8,128)}, f32[128,128]{1,0:T(8,128)S(1)}, u32[]{:S(2)}, u32[]{:S(2)}) collective-permute-start(f32[128,128]{1,0:T(8,128)} %param.5), channel_id=1, source_target_pairs={{0,16},{4,20},{8,24},{12,28},{16,0},{20,4},{24,8},{28,12},{1,17},{... | collective-permute-start | bytes 196616 | tf_op jit(solution)/shard_map/gather_items/ppermute | solution.py:284
  7.8 6.3 %collective-permute-start.5 = (f32[128,128]{1,0:T(8,128)}, f32[128,128]{1,0:T(8,128)S(1)}, u32[]{:S(2)}, u32[]{:S(2)}) collective-permute-start(f32[128,128]{1,0:T(8,128)} %param.5), channel_id=1, source_target_pairs={{0,24},{4,28},{8,16},{12,20},{16,8},{20,12},{24,0},{28,4},{1,25},{... | collective-permute-start | bytes 196616 | tf_op jit(solution)/shard_map/gather_items/ppermute | solution.py:284
  10.3 4.3 %collective-permute-start.2 = (f32[128,128]{1,0:T(8,128)S(1)}, f32[128,128]{1,0:T(8,128)S(1)}, u32[]{:S(2)}, u32[]{:S(2)}) collective-permute-start(f32[128,128]{1,0:T(8,128)S(1)} %collective-permute-done.1), channel_id=1, source_target_pairs={{0,4},{4,0},{8,12},{12,8},{16,20},{20,16},{24,28},{28,24},{1,5},{5... | collective-permute-start | bytes 196616 | tf_op jit(solution)/shard_map/gather_items/ppermute | solution.py:284
  12.4 4.3 %collective-permute-start.4 = (f32[128,128]{1,0:T(8,128)S(1)}, f32[128,128]{1,0:T(8,128)S(1)}, u32[]{:S(2)}, u32[]{:S(2)}) collective-permute-start(f32[128,128]{1,0:T(8,128)S(1)} %collective-permute-done.3), channel_id=1, source_target_pairs={{0,4},{4,0},{8,12},{12,8},{16,20},{20,16},{24,28},{28,24},{1,5},{5... | collective-permute-start | bytes 196616 | tf_op jit(solution)/shard_map/gather_items/ppermute | solution.py:284
  14.1 4.3 %collective-permute-start.6 = (f32[128,128]{1,0:T(8,128)S(1)}, f32[128,128]{1,0:T(8,128)S(1)}, u32[]{:S(2)}, u32[]{:S(2)}) collective-permute-start(f32[128,128]{1,0:T(8,128)S(1)} %collective-permute-done.5), channel_id=1, source_target_pairs={{0,4},{4,0},{8,12},{12,8},{16,20},{20,16},{24,28},{28,24},{1,5},{5... | collective-permute-start | bytes 196616 | tf_op jit(solution)/shard_map/gather_items/ppermute | solution.py:284
  23.8 4.8 %copy-start.1 = (s32[1,1,48,128,128]{4,3,2,1,0:T(8,128)S(1)}, s32[1,1,48,128,128]{4,3,2,1,0:T(8,128)}, u32[]{:S(2)}) copy-start(s32[1,1,48,128,128]{4,3,2,1,0:T(8,128)} %param.9) | copy-start | bytes 9437188
  23.8 103.5 %all-to-all-start = ((s32[8,776,128]{2,1,0:T(8,128)}), s32[8,776,128]{2,1,0:T(8,128)}, u32[]{:S(2)}, u32[]{:S(2)}) async-start(s32[8,776,128]{2,1,0:T(8,128)} %send_tiles.1), calls=%async_computation | async-start | bytes 6356992 | tf_op jit(solution)/shard_map/send_tiles/all_to_all | solution.py:328
  28.7 4.2 %collective-permute-start.9 = (s32[48,64,128]{2,1,0:T(8,128)S(1)}, s32[48,64,128]{2,1,0:T(8,128)S(1)}, u32[]{:S(2)}, u32[]{:S(2)}) collective-permute-start(s32[48,64,128]{2,1,0:T(8,128)S(1)} %dynamic-slice_bitcast_fusion), channel_id=1, source_target_pairs={{0,1},{1,0},{2,3},{3,2},{4,5},{5,4},{6,7},{7,6},{8,9},{9,8},{10,11... | collective-permute-start | bytes 4718600 | tf_op jit(solution)/shard_map/user_tiles/ppermute | solution.py:284
  29.6 9.2 %collective-permute-start.7 = (f32[8,128,128]{2,1,0:T(8,128)S(1)}, f32[8,128,128]{2,1,0:T(8,128)S(1)}, u32[]{:S(2)}, u32[]{:S(2)}) collective-permute-start(f32[8,128,128]{2,1,0:T(8,128)S(1)} %copy-done.3), channel_id=1, source_target_pairs={{0,1},{1,0},{2,3},{3,2},{4,5},{5,4},{6,7},{7,6},{8,9},{9,8},{10,11... | collective-permute-start | bytes 1572872 | tf_op jit(solution)/shard_map/gather_items/ppermute | solution.py:284
  29.6 3.3 %collective-permute-start.8 = (s32[97]{0:T(128)S(1)}, s32[97]{0:T(128)S(1)}, u32[]{:S(2)}, u32[]{:S(2)}) collective-permute-start(s32[97]{0:T(128)S(1)} %pad_add_fusion.own_ids.ids_ref), channel_id=1, source_target_pairs={{0,1},{1,0},{2,3},{3,2},{4,5},{5,4},{6,7},{7,6},{8,9},{9,8},{10,11... | collective-permute-start | bytes 1172 | tf_op jit(solution)/shard_map/user_tiles/ppermute | solution.py:284
  39.6 8.4 %collective-permute-start.10 = (f32[512,128]{1,0:T(8,128)S(1)}, f32[512,128]{1,0:T(8,128)S(1)}, u32[]{:S(2)}, u32[]{:S(2)}) collective-permute-start(f32[512,128]{1,0:T(8,128)S(1)} %get-tuple-element.26.own_ref), channel_id=1, source_target_pairs={{0,2},{1,3},{2,0},{3,1},{4,6},{5,7},{6,4},{7,5},{8,10},{9,11},{10,... | collective-permute-start | bytes 786440 | tf_op jit(solution)/shard_map/user_cg/ppermute | solution.py:284
  53.1 7.7 %collective-permute-start.11 = (f32[512,128]{1,0:T(8,128)S(1)}, f32[512,128]{1,0:T(8,128)S(1)}, u32[]{:S(2)}, u32[]{:S(2)}) collective-permute-start(f32[512,128]{1,0:T(8,128)S(1)} %get-tuple-element.30.own_ref), channel_id=1, source_target_pairs={{0,2},{1,3},{2,0},{3,1},{4,6},{5,7},{6,4},{7,5},{8,10},{9,11},{10,... | collective-permute-start | bytes 786440 | tf_op jit(solution)/shard_map/user_cg/ppermute | solution.py:284
  66.0 6.9 %collective-permute-start.12 = (f32[512,128]{1,0:T(8,128)S(1)}, f32[512,128]{1,0:T(8,128)S(1)}, u32[]{:S(2)}, u32[]{:S(2)}) collective-permute-start(f32[512,128]{1,0:T(8,128)S(1)} %get-tuple-element.34.own_ref), channel_id=1, source_target_pairs={{0,2},{1,3},{2,0},{3,1},{4,6},{5,7},{6,4},{7,5},{8,10},{9,11},{10,... | collective-permute-start | bytes 786440 | tf_op jit(solution)/shard_map/user_cg/ppermute | solution.py:284
  76.7 3.8 %collective-permute-start.13 = (f32[8,512]{1,0:T(8,128)S(1)}, f32[8,512]{1,0:T(8,128)S(1)}, u32[]{:S(2)}, u32[]{:S(2)}) collective-permute-start(f32[8,512]{1,0:T(8,128)S(1)} %get-tuple-element.38.own_ref), channel_id=1, source_target_pairs={{0,2},{1,3},{2,0},{3,1},{4,6},{5,7},{6,4},{7,5},{8,10},{9,11},{10,... | collective-permute-start | bytes 49160 | tf_op jit(solution)/shard_map/user_cg/ppermute | solution.py:284
  80.9 5.7 %collective-permute-start.14 = (f32[128,128]{1,0:T(8,128)S(1)}, f32[128,128]{1,0:T(8,128)S(1)}, u32[]{:S(2)}, u32[]{:S(2)}) collective-permute-start(f32[128,128]{1,0:T(8,128)S(1)} %get-tuple-element.40), channel_id=1, source_target_pairs={{0,1},{1,0},{2,3},{3,2},{4,5},{5,4},{6,7},{7,6},{8,9},{9,8},{10,11... | collective-permute-start | bytes 196616 | tf_op jit(solution)/shard_map/user_cg/ppermute | solution.py:284
  81.0 12.5 %collective-permute-start.16 = (f32[512,128]{1,0:T(8,128)S(1)}, f32[512,128]{1,0:T(8,128)S(1)}, u32[]{:S(2)}, u32[]{:S(2)}) collective-permute-start(f32[512,128]{1,0:T(8,128)S(1)} %get-tuple-element.41.refs_0_), channel_id=1, source_target_pairs={{0,4},{4,0},{8,12},{12,8},{16,20},{20,16},{24,28},{28,24},{1,5},{5... | collective-permute-start | bytes 786440 | tf_op jit(solution)/shard_map/gather_users/ppermute | solution.py:284
  82.7 16.8 %collective-permute-start.18 = (f32[512,128]{1,0:T(8,128)S(1)}, f32[512,128]{1,0:T(8,128)S(1)}, u32[]{:S(2)}, u32[]{:S(2)}) collective-permute-start(f32[512,128]{1,0:T(8,128)S(1)} %get-tuple-element.41.refs_0_), channel_id=1, source_target_pairs={{0,8},{4,12},{8,0},{12,4},{16,24},{20,28},{24,16},{28,20},{1,9},{5... | collective-permute-start | bytes 786440 | tf_op jit(solution)/shard_map/gather_users/ppermute | solution.py:284
  84.1 15.3 %collective-permute-start.15 = (f32[512,128]{1,0:T(8,128)S(1)}, f32[512,128]{1,0:T(8,128)S(1)}, u32[]{:S(2)}, u32[]{:S(2)}) collective-permute-start(f32[512,128]{1,0:T(8,128)S(1)} %get-tuple-element.41.refs_0_), channel_id=1, source_target_pairs={{0,1},{1,0},{2,3},{3,2},{4,5},{5,4},{6,7},{7,6},{8,9},{9,8},{10,11... | collective-permute-start | bytes 786440 | tf_op jit(solution)/shard_map/gather_users/ppermute | solution.py:284
  84.1 33.1 %collective-permute-start.22 = (f32[512,128]{1,0:T(8,128)S(1)}, f32[512,128]{1,0:T(8,128)S(1)}, u32[]{:S(2)}, u32[]{:S(2)}) collective-permute-start(f32[512,128]{1,0:T(8,128)S(1)} %get-tuple-element.41.refs_0_), channel_id=1, source_target_pairs={{0,16},{4,20},{8,24},{12,28},{16,0},{20,4},{24,8},{28,12},{1,17},{... | collective-permute-start | bytes 786440 | tf_op jit(solution)/shard_map/gather_users/ppermute | solution.py:284
  86.6 30.6 %collective-permute-start.26 = (f32[512,128]{1,0:T(8,128)S(1)}, f32[512,128]{1,0:T(8,128)S(1)}, u32[]{:S(2)}, u32[]{:S(2)}) collective-permute-start(f32[512,128]{1,0:T(8,128)S(1)} %get-tuple-element.41.refs_0_), channel_id=1, source_target_pairs={{0,24},{4,28},{8,16},{12,20},{16,8},{20,12},{24,0},{28,4},{1,25},{... | collective-permute-start | bytes 786440 | tf_op jit(solution)/shard_map/gather_users/ppermute | solution.py:284
  93.5 25.8 %collective-permute-start.17 = (f32[512,128]{1,0:T(8,128)S(1)}, f32[512,128]{1,0:T(8,128)S(1)}, u32[]{:S(2)}, u32[]{:S(2)}) collective-permute-start(f32[512,128]{1,0:T(8,128)S(1)} %collective-permute-done.16.refs_2_), channel_id=1, source_target_pairs={{0,1},{1,0},{2,3},{3,2},{4,5},{5,4},{6,7},{7,6},{8,9},{9,8},{10,11... | collective-permute-start | bytes 786440 | tf_op jit(solution)/shard_map/gather_users/ppermute | solution.py:284
  99.4 19.9 %collective-permute-start.19 = (f32[512,128]{1,0:T(8,128)S(1)}, f32[512,128]{1,0:T(8,128)S(1)}, u32[]{:S(2)}, u32[]{:S(2)}) collective-permute-start(f32[512,128]{1,0:T(8,128)S(1)} %collective-permute-done.18.refs_4_), channel_id=1, source_target_pairs={{0,1},{1,0},{2,3},{3,2},{4,5},{5,4},{6,7},{7,6},{8,9},{9,8},{10,11... | collective-permute-start | bytes 786440 | tf_op jit(solution)/shard_map/gather_users/ppermute | solution.py:284
  99.5 20.4 %collective-permute-start.20 = (f32[512,128]{1,0:T(8,128)S(1)}, f32[512,128]{1,0:T(8,128)S(1)}, u32[]{:S(2)}, u32[]{:S(2)}) collective-permute-start(f32[512,128]{1,0:T(8,128)S(1)} %collective-permute-done.18.refs_4_), channel_id=1, source_target_pairs={{0,4},{4,0},{8,12},{12,8},{16,20},{20,16},{24,28},{28,24},{1,5},{5... | collective-permute-start | bytes 786440 | tf_op jit(solution)/shard_map/gather_users/ppermute | solution.py:284
  117.2 6.6 %collective-permute-start.24 = (f32[512,128]{1,0:T(8,128)S(1)}, f32[512,128]{1,0:T(8,128)S(1)}, u32[]{:S(2)}, u32[]{:S(2)}) collective-permute-start(f32[512,128]{1,0:T(8,128)S(1)} %collective-permute-done.22.refs_8_), channel_id=1, source_target_pairs={{0,4},{4,0},{8,12},{12,8},{16,20},{20,16},{24,28},{28,24},{1,5},{5... | collective-permute-start | bytes 786440 | tf_op jit(solution)/shard_map/gather_users/ppermute | solution.py:284
  117.2 9.4 %collective-permute-start.28 = (f32[512,128]{1,0:T(8,128)S(1)}, f32[512,128]{1,0:T(8,128)S(1)}, u32[]{:S(2)}, u32[]{:S(2)}) collective-permute-start(f32[512,128]{1,0:T(8,128)S(1)} %collective-permute-done.26.refs_12_), channel_id=1, source_target_pairs={{0,4},{4,0},{8,12},{12,8},{16,20},{20,16},{24,28},{28,24},{1,5},{5... | collective-permute-start | bytes 786440 | tf_op jit(solution)/shard_map/gather_users/ppermute | solution.py:284
  119.3 16.8 %collective-permute-start.23 = (f32[512,128]{1,0:T(8,128)S(1)}, f32[512,128]{1,0:T(8,128)S(1)}, u32[]{:S(2)}, u32[]{:S(2)}) collective-permute-start(f32[512,128]{1,0:T(8,128)S(1)} %collective-permute-done.22.refs_8_), channel_id=1, source_target_pairs={{0,1},{1,0},{2,3},{3,2},{4,5},{5,4},{6,7},{7,6},{8,9},{9,8},{10,11... | collective-permute-start | bytes 786440 | tf_op jit(solution)/shard_map/gather_users/ppermute | solution.py:284
  119.4 16.7 %collective-permute-start.27 = (f32[512,128]{1,0:T(8,128)S(1)}, f32[512,128]{1,0:T(8,128)S(1)}, u32[]{:S(2)}, u32[]{:S(2)}) collective-permute-start(f32[512,128]{1,0:T(8,128)S(1)} %collective-permute-done.26.refs_12_), channel_id=1, source_target_pairs={{0,1},{1,0},{2,3},{3,2},{4,5},{5,4},{6,7},{7,6},{8,9},{9,8},{10,11... | collective-permute-start | bytes 786440 | tf_op jit(solution)/shard_map/gather_users/ppermute | solution.py:284
  119.9 16.2 %collective-permute-start.21 = (f32[512,128]{1,0:T(8,128)S(1)}, f32[512,128]{1,0:T(8,128)}, u32[]{:S(2)}, u32[]{:S(2)}) collective-permute-start(f32[512,128]{1,0:T(8,128)S(1)} %collective-permute-done.20.refs_6_), channel_id=1, source_target_pairs={{0,1},{1,0},{2,3},{3,2},{4,5},{5,4},{6,7},{7,6},{8,9},{9,8},{10,11... | collective-permute-start | bytes 786440 | tf_op jit(solution)/shard_map/gather_users/ppermute | solution.py:284
  123.9 12.2 %collective-permute-start.25 = (f32[512,128]{1,0:T(8,128)S(1)}, f32[512,128]{1,0:T(8,128)}, u32[]{:S(2)}, u32[]{:S(2)}) collective-permute-start(f32[512,128]{1,0:T(8,128)S(1)} %collective-permute-done.24.refs_10_), channel_id=1, source_target_pairs={{0,1},{1,0},{2,3},{3,2},{4,5},{5,4},{6,7},{7,6},{8,9},{9,8},{10,11... | collective-permute-start | bytes 786440 | tf_op jit(solution)/shard_map/gather_users/ppermute | solution.py:284
  126.7 9.4 %collective-permute-start.29 = (f32[512,128]{1,0:T(8,128)S(1)}, f32[512,128]{1,0:T(8,128)}, u32[]{:S(2)}, u32[]{:S(2)}) collective-permute-start(f32[512,128]{1,0:T(8,128)S(1)} %collective-permute-done.28.refs_14_), channel_id=1, source_target_pairs={{0,1},{1,0},{2,3},{3,2},{4,5},{5,4},{6,7},{7,6},{8,9},{9,8},{10,11... | collective-permute-start | bytes 786440 | tf_op jit(solution)/shard_map/gather_users/ppermute | solution.py:284
  (4 other events, 5.1 us)

commit v2 on v1

--- a/solution.py
+++ b/solution.py
@@ -1,4 +1,5 @@
 import functools
+import math
 
 import jax
 import jax.numpy as jnp
@@ -10,6 +11,7 @@
 UB = 2
 IB = 1
 CG_ITERS = 3
+CHUNKS = 2
 
 
 highest = lax.Precision.HIGHEST
@@ -45,13 +47,13 @@
     return both[:rows] + both[rows:]
 
 
-def tile_terms(direction, conf_ref, pairs_ref, width):
+def tile_terms(direction, conf_ref, pairs_ref, width, begin):
     rows, rank = direction.shape
     lhs = split_rows(direction)
     total = jnp.zeros((rows, rank), f32)
     for start in range(0, conf_ref.shape[1], width):
         factors = pairs_ref[start : start + width, :]
-        weighted = scores_of(lhs, factors) * conf_ref[:, start : start + width]
+        weighted = scores_of(lhs, factors) * conf_ref[begin : begin + rows, start : start + width]
         high, low = pair(weighted)
         out = jnp.dot(jnp.concatenate([high, low], axis=0), factors, preferred_element_type=f32)
         total = total + (
@@ -60,22 +62,26 @@
     return total
 
 
-def tile_squares(direction, conf_ref, pairs_ref, width):
+def tile_squares(direction, conf_ref, pairs_ref, width, begin):
     rows, rank = direction.shape
     lhs = split_rows(direction)
     total = jnp.zeros((rows, rank), f32)
     for start in range(0, conf_ref.shape[1], width):
         scores = scores_of(lhs, pairs_ref[start : start + width, :])
-        squares = scores * scores * conf_ref[:, start : start + width]
+        squares = scores * scores * conf_ref[begin : begin + rows, start : start + width]
         for part in range(0, width, rank):
             total = total + squares[:, part : part + rank]
     return total
 
 
-def side_of(weight_ref, pairs_ref):
+def write_sides(weight_ref, pairs_ref, side_refs):
     rank = pairs_ref.shape[1] // 2
     both = jnp.dot(weight_ref[...], pairs_ref[...], preferred_element_type=f32)
-    return both[:, :rank] + both[:, rank:]
+    start = 0
+    for side_ref in side_refs:
+        rows = slice(start, start + side_ref.shape[0])
+        side_ref[...] = both[rows, :rank] + both[rows, rank:]
+        start += side_ref.shape[0]
 
 
 def advance(solution, residual, direction, product):
@@ -87,23 +93,21 @@
     return solution, residual, direction
 
 
-def pack_kernel(slots, ids_ref, conf_ref, send_ref):
+def pack_kernel(slots, ids_ref, conf_ref, given_ref, send_ref):
     slot_total, block, _ = conf_ref.shape
-    owners = send_ref.shape[0]
+    half = block // 2
+    owners = slot_total // slots
+    near = owners // 2
+    core = lax.rem(lax.axis_index("item"), 2)
     shift = ids_ref[slot_total]
     count = ids_ref[2 * slot_total]
-
-    def one(owner, carry):
+    given_ref[...] = conf_ref[:, pl.ds(pl.multiple_of((1 - core) * half, half), half), :]
+    for owner in range(owners):
         first = lax.rem(owner - shift + owners, owners)
         for slot in range(slots):
             place = first + owners * slot
             used = place < jnp.minimum(count, slot_total)
-            held = jnp.minimum(place, slot_total - 1)
-            send_ref[owner, slot * block : (slot + 1) * block, :] = jnp.where(used, conf_ref[held], 0)
-            send_ref[owner, slots * block + slot, :] = jnp.full((block,), ids_ref[held], jnp.int32)
-        return carry
-
-    lax.fori_loop(0, owners, one, 0)
+            send_ref[owner % near, owner // near * slots + slot] = jnp.where(used, conf_ref[place], 0)
 
 
 def user_tiles_kernel(weight_zero, own_ids, other_ids, conf_ref, half_ref, dense_ref, weight_ref):
@@ -137,24 +141,22 @@
 
 
 def user_side_kernel(count, *refs):
-    pieces, (weight_ref, side_ref, pairs_ref) = refs[:count], refs[count:]
-    start = 0
-    for piece in pieces:
-        flat = piece[...].reshape(-1, piece.shape[-1])
-        high, low = pair(flat)
-        pairs_ref[start : start + flat.shape[0], :] = jnp.concatenate([high, low], axis=1)
-        start += flat.shape[0]
-    side_ref[...] = side_of(weight_ref, pairs_ref)
-
-
-def user_first_kernel(width, own_ref, other_ref, conf_ref, pairs_ref, side_ref, out_ref):
+    pieces, (weight_ref, *side_refs, pairs_ref) = refs[:count], refs[count:]
+    block = pairs_ref.shape[0] // count
+    for place, piece in enumerate(pieces):
+        high, low = pair(piece[:block, :])
+        pairs_ref[place * block : (place + 1) * block, :] = jnp.concatenate([high, low], axis=1)
+    write_sides(weight_ref, pairs_ref, side_refs)
+
+
+def first_kernel(width, begin, own_ref, other_ref, conf_ref, pairs_ref, side_ref, out_ref):
     side = own_ref[...] + other_ref[...]
     side_ref[...] = side
-    out_ref[...] = tile_terms(side, conf_ref, pairs_ref, width)
-
-
-def user_second_kernel(
-    width, side_ref, own_ref, other_ref, conf_ref, pairs_ref, x_ref, r_ref, d_ref, out_ref
+    out_ref[...] = tile_terms(side, conf_ref, pairs_ref, width, begin)
+
+
+def second_kernel(
+    width, begin, side_ref, own_ref, other_ref, conf_ref, pairs_ref, x_ref, r_ref, d_ref, out_ref
 ):
     side = side_ref[...]
     product = own_ref[...] + other_ref[...] + ridge * side
@@ -162,11 +164,11 @@
     x_ref[...] = x
     r_ref[...] = r
     d_ref[...] = d
-    out_ref[...] = tile_terms(d, conf_ref, pairs_ref, width)
-
-
-def user_third_kernel(
-    width, x_in, r_in, d_in, own_ref, other_ref, conf_ref, pairs_ref, x_ref, r_ref, d_ref, sums_ref
+    out_ref[...] = tile_terms(d, conf_ref, pairs_ref, width, begin)
+
+
+def third_kernel(
+    width, begin, x_in, r_in, d_in, own_ref, other_ref, conf_ref, pairs_ref, x_ref, r_ref, d_ref, sums_ref
 ):
     direction = d_in[...]
     product = own_ref[...] + other_ref[...] + ridge * direction
@@ -174,7 +176,7 @@
     x_ref[...] = x
     r_ref[...] = r
     d_ref[...] = d
-    squares = tile_squares(d, conf_ref, pairs_ref, width)
+    squares = tile_squares(d, conf_ref, pairs_ref, width, begin)
     ones = jnp.ones((8, squares.shape[1]), bf16)
     sums = jnp.zeros(sums_ref.shape, f32)
     for unused in range(3):
@@ -184,73 +186,84 @@
     sums_ref[...] = sums
 
 
-def user_last_kernel(blocks, x_in, r_in, d_in, own_ref, other_ref, out_ref, keep_ref, give_ref):
+def solve(refs, out_ref):
+    start = 0
+    for place in range(0, len(refs), 5):
+        x_in, r_in, d_in, own_ref, other_ref = refs[place : place + 5]
+        residual, direction = r_in[...], d_in[...]
+        sums = jnp.transpose(own_ref[...] + other_ref[...])[:, :1]
+        length = row_sum(residual * residual) / (sums + ridge * row_sum(direction * direction))
+        out_ref[start : start + residual.shape[0], :] = x_in[...] + length * direction
+        start += residual.shape[0]
+
+
+def user_last_kernel(*refs):
+    out_ref, keep_ref, give_ref = refs[-3:]
+    solve(refs[:-3], out_ref)
     place = lax.axis_index("item")
-    residual = r_in[...]
-    direction = d_in[...]
-    sums = jnp.transpose(own_ref[...] + other_ref[...])[:, :1]
-    length = row_sum(residual * residual) / (sums + ridge * row_sum(direction * direction))
-    out_ref[...] = x_in[...] + length * direction
     rows = keep_ref.shape[0]
     keep_ref[...] = out_ref[pl.ds(pl.multiple_of(place * rows, rows), rows), :]
     other = jnp.bitwise_xor(place, 1)
     give_ref[...] = out_ref[pl.ds(pl.multiple_of(other * rows, rows), rows), :]
 
 
-def item_tiles_kernel(weight_zero, slots, row_blocks, ids_ref, tiles_ref, dense_ref, weight_ref):
-    owners = tiles_ref.shape[0]
-    block = tiles_ref.shape[2]
-    me = lax.axis_index("user")
+def item_tiles_kernel(weight_zero, row_blocks, lists_ref, tiles_ref, dense_ref, weight_ref, token_ref):
+    near, count, block, _ = tiles_ref.shape
+    slots = count // 2
+    me = lax.rem(lax.axis_index("user"), near)
+    token_ref[...] = jnp.zeros(token_ref.shape, f32)
     dense_ref[...] = jnp.full(dense_ref.shape, weight_zero, f32)
     weight_ref[...] = jnp.zeros(weight_ref.shape, bf16)
-
-    def one(source, carry):
-        base = jnp.bitwise_xor(source, me) * row_blocks
-        for slot in range(slots):
-            value = jnp.transpose(tiles_ref[source, slot * block : (slot + 1) * block, :].astype(f32))
-            col = pl.multiple_of((base + ids_ref[source * slots + slot]) * block, block)
-            at = (slice(None), pl.ds(col, block))
-            dense_ref[at] = dense_ref[at] + value
-            weight_ref[at] = weight_ref[at] + jnp.where(value > 0.0, 1.0 + value, 0.0).astype(bf16)
-        return carry
-
-    lax.fori_loop(0, owners, one, 0)
-
-
-def item_kernel(width, row_blocks, *refs):
-    pieces, (conf_ref, weight_ref, out_ref, pairs_ref) = refs[:-4], refs[-4:]
-    block = out_ref.shape[0]
+    for source in range(near):
+        mask = jnp.bitwise_xor(source, me)
+        for upper in range(2):
+            first = lax.rem(me + upper * near - lists_ref[mask, 1, 0] + 2 * near, 2 * near)
+            for slot in range(slots):
+                value = jnp.transpose(tiles_ref[source, upper * slots + slot].astype(f32))
+                row = lists_ref[mask, 0, first + 2 * near * slot]
+                col = pl.multiple_of((mask * row_blocks + row) * block, block)
+                at = (slice(upper * block, (upper + 1) * block), pl.ds(col, block))
+                dense_ref[at] = dense_ref[at] + value
+                weight_ref[at] = weight_ref[at] + jnp.where(value > 0.0, 1.0 + value, 0.0).astype(bf16)
+
+
+def join_kernel(block, own_ref, other_ref, out_ref):
     half = block // 2
     core = lax.rem(lax.axis_index("item"), 2)
-    group = 0
-    for own_half, piece in pieces_in_order(pieces):
+    for start in range(0, out_ref.shape[0], block):
+        for offset, part_ref in ((core, own_ref), (1 - core, other_ref)):
+            rows = pl.ds(pl.multiple_of(start + offset * half, half), half)
+            out_ref[rows, :] = part_ref[start // 2 : start // 2 + half, :]
+
+
+def item_side_kernel(row_blocks, block, marks, *refs):
+    pieces, (weight_ref, *side_refs, pairs_ref) = refs[: len(marks)], refs[len(marks) :]
+    half = block // 2
+    core = lax.rem(lax.axis_index("item"), 2)
+    for (mask, own_half), piece in zip(marks, pieces):
         offset = pl.multiple_of((core if own_half else 1 - core) * half, half)
         for row in range(row_blocks):
             high, low = pair(piece[row * half : (row + 1) * half, :])
-            pairs_ref[pl.ds((group // 2 * row_blocks + row) * block + offset, half), :] = (
-                jnp.concatenate([high, low], axis=1)
-            )
-        group += 1
-    side = side_of(weight_ref, pairs_ref)
-    x, r, d = jnp.zeros_like(side), side, side
-    for unused in range(CG_ITERS - 1):
-        product = tile_terms(d, conf_ref, pairs_ref, width) + ridge * d
-        x, r, d = advance(x, r, d, product)
-    bottom = row_sum(tile_squares(d, conf_ref, pairs_ref, width)) + ridge * row_sum(d * d)
-    out_ref[...] = x + row_sum(r * r) / bottom * d
-
-
-def pieces_in_order(pieces):
-    return [(place % 2 == 0, piece) for place, piece in enumerate(pieces)]
+            start = (mask * row_blocks + row) * block
+            pairs_ref[pl.ds(start + offset, half), :] = jnp.concatenate([high, low], axis=1)
+    write_sides(weight_ref, pairs_ref, side_refs)
+
+
+def item_last_kernel(*refs):
+    out_ref, all_ref = refs[-2:]
+    solve(refs[:-2], all_ref)
+    rows = out_ref.shape[0]
+    upper = lax.axis_index("user") // (lax.axis_size("user") // 2)
+    out_ref[...] = all_ref[pl.ds(pl.multiple_of(upper * rows, rows), rows), :]
 
 
 VMEM = pltpu.VMEM
 SMEM = pltpu.SMEM
 
 
-def call(kernel, outs, *operands, scalars=0, flops=0, scratch=(), limit=48):
+def call(kernel, outs, *operands, scalars=0, flops=0, scratch=(), limit=16):
     size = sum(op.size * op.dtype.itemsize for op in operands)
-    size += sum(out.size * out.dtype.itemsize for out in outs)
+    size += sum(4 * math.prod(out.shape) for out in outs)
     spaces = [SMEM] * scalars + [VMEM] * (len(operands) - scalars)
     return pl.pallas_call(
         kernel,
@@ -276,9 +289,6 @@
     rows = row_blocks * half
     slots = -(-slot_total // n_user)
     width = 2 * rank
-    me = lax.axis_index("item")
-    core = lax.rem(me, 2)
-
     def swap(value, axis, mask):
         size = n_item if axis == "item" else n_user
         return lax.ppermute(value, axis, [(place, place ^ mask) for place in range(size)])
@@ -298,19 +308,47 @@
         [tile_rows.reshape(-1), tile_cols.reshape(-1), tile_count.reshape(-1)]
     ).astype(jnp.int32)
 
+    def after(value, *tokens):
+        return lax.optimization_barrier((value, *tokens))[0]
+
+    named = jnp.concatenate([tile_rows.reshape(1, -1), tile_cols.reshape(1, -1)])
+    named = jnp.pad(named.astype(f32), ((0, 6), (0, rank - slot_total)))
+    sent = jnp.concatenate([item_init, named], axis=0)
+    near = n_user // 2
+    token = shaped((8, rank))
     with jax.named_scope("gather_items"):
-        pieces = {0: item_init, 1: swap(item_init, "user", 1)}
-        for mask in range(2, n_user, 2):
-            pieces[mask] = swap(item_init, "user", mask)
-        for mask in range(2, n_user, 2):
+        pieces = {0: sent}
+        for mask in (6, 4, 2, 1):
+            pieces[mask] = swap(sent, "user", mask)
+
+    with jax.named_scope("pack_tiles"):
+        given, packed = call(
+            functools.partial(pack_kernel, slots),
+            (
+                shaped((slot_total, half, block), jnp.int32),
+                pltpu.HBM((near, 2 * slots, block, block), jnp.int32),
+            ),
+            after(ids, *pieces.values()), conf, scalars=1, flops=10 ** 9,
+        )
+        other_ids = swap(ids, "item", 1)
+        other_half = swap(given, "item", 1)
+
+    with jax.named_scope("gather_items"):
+        for mask in (2, 6, 4):
             pieces[mask + 1] = swap(pieces[mask], "user", 1)
-        own_items = jnp.stack([pieces[mask] for mask in range(n_user)])
-        other_items = swap(own_items, "item", 1)
+        own_items = [pieces[mask] for mask in range(n_user)]
+        ids, *own_items, other_half = lax.optimization_barrier((ids, *own_items, other_half))
+
+    with jax.named_scope("send_tiles"):
+        halves = [list(range(start, start + near)) for start in (0, near)]
+        tiles = lax.all_to_all(
+            after(packed, own_items[-1]), "user", 0, 0, tiled=True, axis_index_groups=halves
+        )
+
+    with jax.named_scope("gather_items"):
+        other_items = [swap(piece, "item", 1) for piece in own_items]
 
     with jax.named_scope("user_tiles"):
-        other_ids = swap(ids, "item", 1)
-        given = lax.dynamic_slice(conf, (0, (1 - core) * half, 0), (slot_total, half, block))
-        other_half = swap(given, "item", 1)
         columns = 2 * n_user * block
         user_conf, user_weight = call(
             functools.partial(user_tiles_kernel, unobserved / (item_init.shape[0] * n_user * n_item)),
@@ -318,71 +356,79 @@
             ids, other_ids, conf, other_half, scalars=2, flops=10 ** 9,
         )
 
-    with jax.named_scope("send_tiles"):
-        tied_ids, tied_conf, own_items = lax.optimization_barrier((ids, conf, own_items))
-        (packed,) = call(
-            functools.partial(pack_kernel, slots),
-            (shaped((n_user, slots * block + 8, block), jnp.int32),),
-            tied_ids, tied_conf, scalars=1, flops=10 ** 9,
-        )
-        item_tiles = lax.all_to_all(packed, "user", 0, 0, tiled=True)
-
-    cost = 2 * rows * columns * rank
+    def iterate(sides, confidence, pairs, both):
+        work = 2 * sides[0].shape[0] * pairs.shape[0] * rank
+        states = []
+        for place, part in enumerate(sides):
+            size = part.shape[0]
+            state, begin = shaped(part.shape), place * size
+            side, part = call(
+                functools.partial(first_kernel, width, begin), (state, state),
+                *both(part), confidence, pairs, flops=6 * work,
+            )
+            states.append((begin, state, (side,), part))
+        for kernel in (second_kernel, third_kernel):
+            for place, (begin, state, carried, part) in enumerate(states):
+                last = shaped((8, state.shape[0])) if kernel is third_kernel else state
+                *carried, part = call(
+                    functools.partial(kernel, width, begin), (state, state, state, last),
+                    *carried, *both(part), confidence, pairs, flops=6 * work,
+                )
+                states[place] = (begin, state, carried, part)
+        return [value for _, _, carried, sums in states for value in (*carried, *both(sums))]
+
     state = shaped((rows, rank))
     with jax.named_scope("user_cg"):
-        part, pairs = call(
-            functools.partial(user_side_kernel, 2),
-            (state, shaped((columns, 2 * rank), bf16)),
-            own_items, other_items, user_weight, flops=2 * cost,
-        )
-        side, part = call(
-            functools.partial(user_first_kernel, width), (state, state),
-            *others(part), user_conf, pairs, flops=6 * cost,
-        )
-        x, r, d, part = call(
-            functools.partial(user_second_kernel, width), (state,) * 4,
-            side, *others(part), user_conf, pairs, flops=6 * cost,
-        )
-        x, r, d, sums = call(
-            functools.partial(user_third_kernel, width), (state,) * 3 + (shaped((8, rows)),),
-            x, r, d, *others(part), user_conf, pairs, flops=3 * cost,
+        *sides, pairs = call(
+            functools.partial(user_side_kernel, 2 * n_user),
+            (shaped((rows // CHUNKS, rank)),) * CHUNKS + (shaped((columns, 2 * rank), bf16),),
+            *own_items, *other_items, user_weight, flops=4 * rows * columns * rank,
         )
         shard = shaped((UB * half, rank))
         users, keep, give = call(
-            functools.partial(user_last_kernel, row_blocks), (state, shard, shard),
-            x, r, d, *others(sums), flops=10 ** 6,
+            user_last_kernel, (state, shard, shard),
+            *iterate(sides, user_conf, pairs, others), flops=10 ** 6,
         )
         taken = swap(give, "item", 1)
-        keep, taken = keep.reshape(UB, half, rank), taken.reshape(UB, half, rank)
-        user_factors = jnp.stack(
-            [jnp.where(core == 0, keep, taken), jnp.where(core == 0, taken, keep)], axis=1
-        ).reshape(UB * block, rank)
+        (user_factors,) = call(
+            functools.partial(join_kernel, block), (shaped((UB * block, rank)),), keep, taken
+        )
 
     with jax.named_scope("gather_users"):
-        pieces = {0: users, 1: swap(users, "user", 1)}
-        for mask in range(2, n_user, 2):
-            pieces[mask] = swap(users, "user", mask)
-        for mask in range(2, n_user, 2):
-            pieces[mask + 1] = swap(pieces[mask], "user", 1)
-        ordered = []
-        for mask in range(n_user):
-            ordered += [pieces[mask], swap(pieces[mask], "item", 1)]
-
-    with jax.named_scope("item_half"):
-        row_ids = item_tiles[:, slots * block : slots * block + slots, 0].reshape(-1)
-        columns = n_user * row_blocks * block
-        item_conf, item_weight = call(
+        users, tiles = lax.optimization_barrier((users, tiles))
+        found = [users, swap(users, "user", 1), swap(users, "user", 2)]
+
+    with jax.named_scope("item_tiles"):
+        lists = jnp.stack([pieces[mask][block : block + 2] for mask in range(near)]).astype(jnp.int32)
+        columns = near * row_blocks * block
+        item_conf, item_weight, laid = call(
             functools.partial(
-                item_tiles_kernel, unobserved / (user_factors.shape[0] * n_user * n_item), slots, row_blocks
+                item_tiles_kernel, unobserved / (user_factors.shape[0] * n_user * n_item), row_blocks
             ),
-            (shaped((block, columns)), shaped((block, columns), bf16)),
-            row_ids, item_tiles, scalars=1, flops=10 ** 9,
-        )
-        (item_factors,) = call(
-            functools.partial(item_kernel, width, row_blocks),
-            (shaped((block, rank)),),
-            *ordered, item_conf, item_weight, flops=20 * 2 * block * columns * rank,
-            scratch=(pltpu.VMEM((columns, 2 * rank), bf16),),
+            (shaped((2 * block, columns)), shaped((2 * block, columns), bf16), token),
+            lists, tiles, scalars=1, flops=10 ** 9,
+        )
+
+    with jax.named_scope("gather_users"):
+        found.append(swap(after(found[2], laid), "user", 1))
+        marks, ordered = [], []
+        for mask, piece in enumerate(found):
+            marks += [(mask, True), (mask, False)]
+            ordered += [piece, swap(piece, "item", 1)]
+
+    def both(value):
+        return value, swap(value, "user", near)
+
+    rows = 2 * block
+    with jax.named_scope("item_cg"):
+        *sides, pairs = call(
+            functools.partial(item_side_kernel, row_blocks, block, marks),
+            (shaped((rows // CHUNKS, rank)),) * CHUNKS + (shaped((columns, 2 * rank), bf16),),
+            *ordered, item_weight, flops=4 * rows * columns * rank,
+        )
+        item_factors, unused = call(
+            item_last_kernel, (shaped((block, rank)), shaped((rows, rank))),
+            *iterate(sides, item_conf, pairs, both), flops=10 ** 6,
         )
     return (user_factors, item_factors)
 
@@ -391,7 +437,7 @@
     n_user, n_item = mesh.shape["user"], mesh.shape["item"]
     block = 128
     user_bytes = UB * n_item * block * n_user * block * 4
-    return user_bytes <= DENSE_LIMIT and n_item % 2 == 0 and n_user % 2 == 0
+    return user_bytes <= DENSE_LIMIT and n_item % 2 == 0 and n_user == 8
 
 
 def block_sum(slot_terms, block_ids, row_count, block_size):

time: 150 us -> 123 us (0.82)
  waiting for transfers between devices: 68.6 us -> 38.6 us
  starting transfers between devices: 27.4 us -> 44.7 us
  Pallas kernels: 43.3 us -> 30.2 us
  local copies, waits for them, and re-layouts: 7.62 us -> 5.22 us
  other arithmetic: 0.77 us -> 2.29 us
    ppermute x30 -> x41, waiting for transfers between devices: 68.6 us -> 38.6 us  [swap(): lax.ppermute(value, axis, [(place, place ^ mask) for place in range(size)])]
    ppermute x30 -> x41, starting transfers between devices: 22.7 us -> 39.8 us  [swap(): lax.ppermute(value, axis, [(place, place ^ mask) for place in range(size)])]
    pallas_call x9 -> x20, Pallas kernels: 43.3 us -> 30.2 us  [call(): pl.pallas_call(kernel, out_shape=tuple(outs), in_specs=[pl.BlockSpec(memo...]
    unnamed x17 -> x20, local copies, waits for them, and re-layouts: 5.8 us -> 5.2 us
  transfers between devices with their start and end apart: 31 -> 42, of which waited for: 14 -> 17; matrix products, arithmetic and copies ran while one was open for 2% -> 1% of each run, Pallas kernels for 18% -> 21%
where the time goes in v2:
time: 123 us
  starting transfers between devices  44.7 us (36%)
  waiting for transfers between devices  38.6 us (31%)
  Pallas kernels  30.2 us (25%)
  local copies, waits for them, and re-layouts  5.22 us (4%)
  other arithmetic  2.29 us (2%)
  between operations  1.55 us (1%)
    ppermute x41, starting transfers between devices, swap(): lax.ppermute(value, axis, [(place, place ^ mask) for place in range(size)])  39.8 us
    ppermute x41, waiting for transfers between devices, swap(): lax.ppermute(value, axis, [(place, place ^ mask) for place in range(size)])  38.6 us
    pallas_call x20, Pallas kernels, call(): pl.pallas_call(kernel, out_shape=tuple(outs), in_specs=[pl.BlockSpec(memo...  30.2 us
    unnamed x20, local copies, waits for them, and re-layouts  5.2 us
    all_to_all x1, starting transfers between devices, dense_shards(): lax.all_to_all(after(packed, own_items[-1]), 'user', 0, 0, tiled=True, ax...  4.92 us
  transfers between devices with their start and end apart: 42, of which 17 were waited for; matrix products, arithmetic and copies ran while one was open for 1% of the time, Pallas kernels for 21%

profile of v2, /device:TPU:0, one launch (start us, length us, event | category | flops | bytes accessed | tf_op | source)
XLA Modules:
  0.0 122.5 jit_solution(4898684737462550566)
XLA Ops:
  2.2 3.0 %collective-permute-start.1 = (f32[136,128]{1,0:T(8,128)S(1)}, f32[136,128]{1,0:T(8,128)S(1)}, u32[]{:S(2)}, u32[]{:S(2)}) collective-permute-start(f32[136,128]{1,0:T(8,128)S(1)} %pad_maximum_fusion.refs_0_), channel_id=1, source_target_pairs={{0,8},{4,12},{8,0},{12,4},{16,24},{20,28},{24,16},{28,20},{1,9},{5... | collective-permute-start | bytes 208904 | tf_op jit(solution)/shard_map/gather_items/ppermute | solution.py:294
  6.7 2.6 %collective-permute-start.3 = (f32[136,128]{1,0:T(8,128)S(1)}, f32[136,128]{1,0:T(8,128)S(1)}, u32[]{:S(2)}, u32[]{:S(2)}) collective-permute-start(f32[136,128]{1,0:T(8,128)S(1)} %pad_maximum_fusion.refs_0_), channel_id=1, source_target_pairs={{0,16},{4,20},{8,24},{12,28},{16,0},{20,4},{24,8},{28,12},{1,17},{... | collective-permute-start | bytes 208904 | tf_op jit(solution)/shard_map/gather_items/ppermute | solution.py:294
  10.9 3.0 %collective-permute-done.3.refs_4_ = f32[136,128]{1,0:T(8,128)S(1)} collective-permute-done((f32[136,128]{1,0:T(8,128)S(1)}, f32[136,128]{1,0:T(8,128)S(1)}, u32[]{:S(2)}, u32[]{:S(2)}) %collective-permute-start.3) | collective-permute-done | bytes 69664 | tf_op jit(solution)/shard_map/gather_items/ppermute | solution.py:294
  15.4 1.9 %copy-done = s32[1,1,48,128,128]{4,3,2,1,0:T(8,128)S(1)} copy-done((s32[1,1,48,128,128]{4,3,2,1,0:T(8,128)S(1)}, s32[1,1,48,128,128]{4,3,2,1,0:T(8,128)}, u32[]{:S(2)}) %copy-start) | copy-done | bytes 3145752
  17.3 2.5 %pack_tiles.1 = (s32[48,64,128]{2,1,0:T(8,128)S(1)}, s32[4,12,128,128]{3,2,1,0:T(8,128)}) custom-call(s32[97]{0:T(128)S(1)} %pad_add_fusion.ids_ref.own_ids, s32[48,128,128]{2,1,0:T(8,128)S(1)} %bitcast.15), custom_call_target="tpu_custom_call" | custom-call | flops 1000000000 | bytes 7864708 | tf_op jit(solution)/shard_map/pack_tiles/pallas_call | solution.py:268
  22.4 2.4 %collective-permute-done.2.refs_3_ = f32[136,128]{1,0:T(8,128)S(1)} collective-permute-done((f32[136,128]{1,0:T(8,128)S(1)}, f32[136,128]{1,0:T(8,128)S(1)}, u32[]{:S(2)}, u32[]{:S(2)}) %collective-permute-start.2) | collective-permute-done | bytes 69664 | tf_op jit(solution)/shard_map/gather_items/ppermute | solution.py:294
  29.3 4.9 %all-to-all-start = ((s32[4,12,128,128]{3,2,1,0:T(8,128)}), s32[4,12,128,128]{3,2,1,0:T(8,128)}, u32[]{:S(2)}, u32[]{:S(2)}) async-start(s32[4,12,128,128]{3,2,1,0:T(8,128)} %get-tuple-element.113), calls=%async_computation | async-start | bytes 6291456 | tf_op jit(solution)/shard_map/send_tiles/all_to_all | solution.py:344
  38.5 2.3 %user_tiles.1 = (f32[512,2048]{1,0:T(8,128)S(1)}, bf16[512,2048]{1,0:T(8,128)(2,1)S(1)}) custom-call(s32[97]{0:T(128)S(1)} %pad_add_fusion.ids_ref.own_ids, s32[97]{0:T(128)S(1)} %collective-permute-done.16.other_ids, s32[48,128,128]{2,1,0:T(8,128)S(1)} %bitcast.16, s32[48,64,128]{2,1,0:T(8,128)S(1)} %copy-done.3), custom_call_target="tpu_custom_call" | custom-call | flops 1000000000 | bytes 13107976 | tf_op jit(solution)/shard_map/user_tiles/pallas_call | solution.py:268
  41.7 1.8 %collective-permute-start.21 = (f32[256,128]{1,0:T(8,128)S(1)}, f32[256,128]{1,0:T(8,128)S(1)}, u32[]{:S(2)}, u32[]{:S(2)}) collective-permute-start(f32[256,128]{1,0:T(8,128)S(1)} %get-tuple-element.98.own_ref), channel_id=1, source_target_pairs={{0,2},{1,3},{2,0},{3,1},{4,6},{5,7},{6,4},{7,5},{8,10},{9,11},{10,... | collective-permute-start | bytes 393224 | tf_op jit(solution)/shard_map/user_cg/ppermute | solution.py:294
  43.8 4.3 %collective-permute-done.21.other_ref = f32[256,128]{1,0:T(8,128)S(1)} collective-permute-done((f32[256,128]{1,0:T(8,128)S(1)}, f32[256,128]{1,0:T(8,128)S(1)}, u32[]{:S(2)}, u32[]{:S(2)}) %collective-permute-start.21) | collective-permute-done | bytes 131104 | tf_op jit(solution)/shard_map/user_cg/ppermute | solution.py:294
  48.1 1.6 %user_cg.13 = (f32[256,128]{1,0:T(8,128)S(1)}, f32[256,128]{1,0:T(8,128)S(1)}) custom-call(f32[256,128]{1,0:T(8,128)S(1)} %get-tuple-element.98.own_ref, f32[256,128]{1,0:T(8,128)S(1)} %collective-permute-done.21.other_ref, f32[512,2048]{1,0:T(8,128)S(1)} %get-tuple-element.86.conf_ref, bf16[2048,256]{1,0:T(8,128)(2,1)S(1)} %get-tuple-element.87.pairs_ref), custom_call_target="tpu_custom_call" | custom-call | flops 805306368 | bytes 5767168 | tf_op jit(solution)/shard_map/user_cg/pallas_call | solution.py:268
  49.7 1.8 %collective-permute-start.22 = (f32[256,128]{1,0:T(8,128)S(1)}, f32[256,128]{1,0:T(8,128)S(1)}, u32[]{:S(2)}, u32[]{:S(2)}) collective-permute-start(f32[256,128]{1,0:T(8,128)S(1)} %get-tuple-element.100.own_ref), channel_id=1, source_target_pairs={{0,2},{1,3},{2,0},{3,1},{4,6},{5,7},{6,4},{7,5},{8,10},{9,11},{10,... | collective-permute-start | bytes 393224 | tf_op jit(solution)/shard_map/user_cg/ppermute | solution.py:294
  51.5 1.6 %user_cg.10 = (f32[256,128]{1,0:T(8,128)S(1)}, f32[256,128]{1,0:T(8,128)S(1)}) custom-call(f32[256,128]{1,0:T(8,128)S(1)} %get-tuple-element.85.own_ref, f32[256,128]{1,0:T(8,128)S(1)} %collective-permute-done.17.other_ref, f32[512,2048]{1,0:T(8,128)S(1)} %get-tuple-element.86.conf_ref, bf16[2048,256]{1,0:T(8,128)(2,1)S(1)} %get-tuple-element.87.pairs_ref), custom_call_target="tpu_custom_call" | custom-call | flops 805306368 | bytes 5767168 | tf_op jit(solution)/shard_map/user_cg/pallas_call | solution.py:268
  55.0 1.8 %user_cg.14 = (f32[256,128]{1,0:T(8,128)S(1)}, f32[256,128]{1,0:T(8,128)S(1)}, f32[256,128]{1,0:T(8,128)S(1)}, f32[256,128]{1,0:T(8,128)S(1)}) custom-call(f32[256,128]{1,0:T(8,128)S(1)} %get-tuple-element.99.side_ref, f32[256,128]{1,0:T(8,128)S(1)} %get-tuple-element.100.own_ref, f32[256,128]{1,0:T(8,128)S(1)} %collective-permute-done.22.other_ref, ...), custom_call_target="tpu_custom_call" | custom-call | flops 805306368 | bytes 6160384 | tf_op jit(solution)/shard_map/user_cg/pallas_call | solution.py:268
  56.8 2.2 %collective-permute-start.23 = (f32[256,128]{1,0:T(8,128)S(1)}, f32[256,128]{1,0:T(8,128)S(1)}, u32[]{:S(2)}, u32[]{:S(2)}) collective-permute-start(f32[256,128]{1,0:T(8,128)S(1)} %get-tuple-element.104.own_ref), channel_id=1, source_target_pairs={{0,2},{1,3},{2,0},{3,1},{4,6},{5,7},{6,4},{7,5},{8,10},{9,11},{10,... | collective-permute-start | bytes 393224 | tf_op jit(solution)/shard_map/user_cg/ppermute | solution.py:294
  59.0 1.8 %user_cg.11 = (f32[256,128]{1,0:T(8,128)S(1)}, f32[256,128]{1,0:T(8,128)S(1)}, f32[256,128]{1,0:T(8,128)S(1)}, f32[256,128]{1,0:T(8,128)S(1)}) custom-call(f32[256,128]{1,0:T(8,128)S(1)} %get-tuple-element.88.side_ref, f32[256,128]{1,0:T(8,128)S(1)} %get-tuple-element.89.own_ref, f32[256,128]{1,0:T(8,128)S(1)} %collective-permute-done.18.other_ref, ...), custom_call_target="tpu_custom_call" | custom-call | flops 805306368 | bytes 6160384 | tf_op jit(solution)/shard_map/user_cg/pallas_call | solution.py:268
  63.5 2.4 %collective-permute-start.24 = (f32[8,256]{1,0:T(8,128)S(1)}, f32[8,256]{1,0:T(8,128)S(1)}, u32[]{:S(2)}, u32[]{:S(2)}) collective-permute-start(f32[8,256]{1,0:T(8,128)S(1)} %get-tuple-element.108.refs_8_), channel_id=1, source_target_pairs={{0,2},{1,3},{2,0},{3,1},{4,6},{5,7},{6,4},{7,5},{8,10},{9,11},{10,... | collective-permute-start | bytes 24584 | tf_op jit(solution)/shard_map/user_cg/ppermute | solution.py:294
  67.9 2.7 %collective-permute-done.20.refs_4_ = f32[8,256]{1,0:T(8,128)S(1)} collective-permute-done((f32[8,256]{1,0:T(8,128)S(1)}, f32[8,256]{1,0:T(8,128)S(1)}, u32[]{:S(2)}, u32[]{:S(2)}) %collective-permute-start.20) | collective-permute-done | bytes 8224 | tf_op jit(solution)/shard_map/user_cg/ppermute | solution.py:294
  71.1 2.0 %collective-permute-start.29 = (f32[512,128]{1,0:T(8,128)S(1)}, f32[512,128]{1,0:T(8,128)S(1)}, u32[]{:S(2)}, u32[]{:S(2)}) collective-permute-start(f32[512,128]{1,0:T(8,128)S(1)} %get-tuple-element.114.refs_0_), channel_id=1, source_target_pairs={{0,8},{4,12},{8,0},{12,4},{16,24},{20,28},{24,16},{28,20},{1,9},{5... | collective-permute-start | bytes 786440 | tf_op jit(solution)/shard_map/gather_users/ppermute | solution.py:294
  74.6 3.8 %collective-permute-done.29.refs_4_ = f32[512,128]{1,0:T(8,128)S(1)} collective-permute-done((f32[512,128]{1,0:T(8,128)S(1)}, f32[512,128]{1,0:T(8,128)S(1)}, u32[]{:S(2)}, u32[]{:S(2)}) %collective-permute-start.29) | collective-permute-done | bytes 262176 | tf_op jit(solution)/shard_map/gather_users/ppermute | solution.py:294
  80.6 4.9 %collective-permute-done.31.refs_6_ = f32[512,128]{1,0:T(8,128)S(1)} collective-permute-done((f32[512,128]{1,0:T(8,128)S(1)}, f32[512,128]{1,0:T(8,128)S(1)}, u32[]{:S(2)}, u32[]{:S(2)}) %collective-permute-start.31) | collective-permute-done | bytes 262176 | tf_op jit(solution)/shard_map/gather_users/ppermute | solution.py:294
  85.5 4.1 %item_tiles.1 = (f32[256,4096]{1,0:T(8,128)S(1)}, bf16[256,4096]{1,0:T(8,128)(2,1)S(1)}, f32[8,128]{1,0:T(8,128)}) custom-call(s32[4,2,128]{2,1,0:T(2,128)S(1)} %maximum_convert_fusion.lists_ref, s32[4,12,128,128]{3,2,1,0:T(8,128)} %all-to-all-done.tiles_ref), custom_call_target="tpu_custom_call" | custom-call | flops 1000000000 | bytes 11542528 | tf_op jit(solution)/shard_map/item_tiles/pallas_call | solution.py:268
  90.6 1.7 %collective-permute-start.37 = (f32[128,128]{1,0:T(8,128)S(1)}, f32[128,128]{1,0:T(8,128)S(1)}, u32[]{:S(2)}, u32[]{:S(2)}) collective-permute-start(f32[128,128]{1,0:T(8,128)S(1)} %get-tuple-element.130.own_ref), channel_id=1, source_target_pairs={{0,16},{4,20},{8,24},{12,28},{16,0},{20,4},{24,8},{28,12},{1,17},{... | collective-permute-start | bytes 196616 | tf_op jit(solution)/shard_map/item_cg/ppermute | solution.py:294
  93.8 5.5 %collective-permute-done.37.other_ref = f32[128,128]{1,0:T(8,128)S(1)} collective-permute-done((f32[128,128]{1,0:T(8,128)S(1)}, f32[128,128]{1,0:T(8,128)S(1)}, u32[]{:S(2)}, u32[]{:S(2)}) %collective-permute-start.37) | collective-permute-done | bytes 65568 | tf_op jit(solution)/shard_map/item_cg/ppermute | solution.py:294
  99.3 1.8 %item_cg.12 = (f32[128,128]{1,0:T(8,128)S(1)}, f32[128,128]{1,0:T(8,128)S(1)}) custom-call(f32[128,128]{1,0:T(8,128)S(1)} %get-tuple-element.130.own_ref, f32[128,128]{1,0:T(8,128)S(1)} %collective-permute-done.37.other_ref, f32[256,4096]{1,0:T(8,128)S(1)} %get-tuple-element.118.conf_ref, bf16[4096,256]{1,0:T(8,128)(2,1)S(1)} %get-tuple-element.119.pairs_ref), custom_call_target="tpu_custom_call" | custom-call | flops 805306368 | bytes 6553600 | tf_op jit(solution)/shard_map/item_cg/pallas_call | solution.py:268
  101.1 1.6 %item_cg.9 = (f32[128,128]{1,0:T(8,128)S(1)}, f32[128,128]{1,0:T(8,128)S(1)}) custom-call(f32[128,128]{1,0:T(8,128)S(1)} %get-tuple-element.117.own_ref, f32[128,128]{1,0:T(8,128)S(1)} %collective-permute-done.33.other_ref, f32[256,4096]{1,0:T(8,128)S(1)} %get-tuple-element.118.conf_ref, bf16[4096,256]{1,0:T(8,128)(2,1)S(1)} %get-tuple-element.119.pairs_ref), custom_call_target="tpu_custom_call" | custom-call | flops 805306368 | bytes 6553600 | tf_op jit(solution)/shard_map/item_cg/pallas_call | solution.py:268
  102.7 3.0 %collective-permute-start.34 = (f32[128,128]{1,0:T(8,128)S(1)}, f32[128,128]{1,0:T(8,128)S(1)}, u32[]{:S(2)}, u32[]{:S(2)}) collective-permute-start(f32[128,128]{1,0:T(8,128)S(1)} %get-tuple-element.121.own_ref), channel_id=1, source_target_pairs={{0,16},{4,20},{8,24},{12,28},{16,0},{20,4},{24,8},{28,12},{1,17},{... | collective-permute-start | bytes 196616 | tf_op jit(solution)/shard_map/item_cg/ppermute | solution.py:294
  106.9 1.7 %item_cg.13 = (f32[128,128]{1,0:T(8,128)S(1)}, f32[128,128]{1,0:T(8,128)S(1)}, f32[128,128]{1,0:T(8,128)S(1)}, f32[128,128]{1,0:T(8,128)S(1)}) custom-call(f32[128,128]{1,0:T(8,128)S(1)} %get-tuple-element.131.side_ref, f32[128,128]{1,0:T(8,128)S(1)} %get-tuple-element.132.own_ref, f32[128,128]{1,0:T(8,128)S(1)} %collective-permute-done.38.other_ref, ...), custom_call_target="tpu_custom_call" | custom-call | flops 805306368 | bytes 6750208 | tf_op jit(solution)/shard_map/item_cg/pallas_call | solution.py:268
  108.7 1.7 %item_cg.10 = (f32[128,128]{1,0:T(8,128)S(1)}, f32[128,128]{1,0:T(8,128)S(1)}, f32[128,128]{1,0:T(8,128)S(1)}, f32[128,128]{1,0:T(8,128)S(1)}) custom-call(f32[128,128]{1,0:T(8,128)S(1)} %get-tuple-element.120.side_ref, f32[128,128]{1,0:T(8,128)S(1)} %get-tuple-element.121.own_ref, f32[128,128]{1,0:T(8,128)S(1)} %collective-permute-done.34.other_ref, ...), custom_call_target="tpu_custom_call" | custom-call | flops 805306368 | bytes 6750208 | tf_op jit(solution)/shard_map/item_cg/pallas_call | solution.py:268
  110.4 3.0 %collective-permute-start.35 = (f32[128,128]{1,0:T(8,128)S(1)}, f32[128,128]{1,0:T(8,128)S(1)}, u32[]{:S(2)}, u32[]{:S(2)}) collective-permute-start(f32[128,128]{1,0:T(8,128)S(1)} %get-tuple-element.125.own_ref), channel_id=1, source_target_pairs={{0,16},{4,20},{8,24},{12,28},{16,0},{20,4},{24,8},{28,12},{1,17},{... | collective-permute-start | bytes 196616 | tf_op jit(solution)/shard_map/item_cg/ppermute | solution.py:294
  113.3 1.7 %collective-permute-done.39.other_ref = f32[128,128]{1,0:T(8,128)S(1)} collective-permute-done((f32[128,128]{1,0:T(8,128)S(1)}, f32[128,128]{1,0:T(8,128)S(1)}, u32[]{:S(2)}, u32[]{:S(2)}) %collective-permute-start.39) | collective-permute-done | bytes 65568 | tf_op jit(solution)/shard_map/item_cg/ppermute | solution.py:294
  117.0 3.0 %collective-permute-start.36 = (f32[8,128]{1,0:T(8,128)S(1)}, f32[8,128]{1,0:T(8,128)S(1)}, u32[]{:S(2)}, u32[]{:S(2)}) collective-permute-start(f32[8,128]{1,0:T(8,128)S(1)} %get-tuple-element.129.refs_3_), channel_id=1, source_target_pairs={{0,16},{4,20},{8,24},{12,28},{16,0},{20,4},{24,8},{28,12},{1,17},{... | collective-permute-start | bytes 12296 | tf_op jit(solution)/shard_map/item_cg/ppermute | solution.py:294
  (101 shorter events, 37.0 us)
Async XLA Ops:
  2.2 8.8 %collective-permute-start.1 = (f32[136,128]{1,0:T(8,128)S(1)}, f32[136,128]{1,0:T(8,128)S(1)}, u32[]{:S(2)}, u32[]{:S(2)}) collective-permute-start(f32[136,128]{1,0:T(8,128)S(1)} %pad_maximum_fusion.refs_0_), channel_id=1, source_target_pairs={{0,8},{4,12},{8,0},{12,4},{16,24},{20,28},{24,16},{28,20},{1,9},{5... | collective-permute-start | bytes 208904 | tf_op jit(solution)/shard_map/gather_items/ppermute | solution.py:294
  5.2 5.7 %collective-permute-start = (f32[136,128]{1,0:T(8,128)S(1)}, f32[136,128]{1,0:T(8,128)S(1)}, u32[]{:S(2)}, u32[]{:S(2)}) collective-permute-start(f32[136,128]{1,0:T(8,128)S(1)} %pad_maximum_fusion.refs_0_), channel_id=1, source_target_pairs={{0,4},{4,0},{8,12},{12,8},{16,20},{20,16},{24,28},{28,24},{1,5},{5... | collective-permute-start | bytes 208904 | tf_op jit(solution)/shard_map/gather_items/ppermute | solution.py:294
  6.7 7.2 %collective-permute-start.3 = (f32[136,128]{1,0:T(8,128)S(1)}, f32[136,128]{1,0:T(8,128)S(1)}, u32[]{:S(2)}, u32[]{:S(2)}) collective-permute-start(f32[136,128]{1,0:T(8,128)S(1)} %pad_maximum_fusion.refs_0_), channel_id=1, source_target_pairs={{0,16},{4,20},{8,24},{12,28},{16,0},{20,4},{24,8},{28,12},{1,17},{... | collective-permute-start | bytes 208904 | tf_op jit(solution)/shard_map/gather_items/ppermute | solution.py:294
  9.3 6.1 %collective-permute-start.5 = (f32[136,128]{1,0:T(8,128)S(1)}, f32[136,128]{1,0:T(8,128)S(1)}, u32[]{:S(2)}, u32[]{:S(2)}) collective-permute-start(f32[136,128]{1,0:T(8,128)S(1)} %pad_maximum_fusion.refs_0_), channel_id=1, source_target_pairs={{0,24},{4,28},{8,16},{12,20},{16,8},{20,12},{24,0},{28,4},{1,25},{... | collective-permute-start | bytes 208904 | tf_op jit(solution)/shard_map/gather_items/ppermute | solution.py:294
  19.8 7.6 %collective-permute-start.7 = (s32[48,64,128]{2,1,0:T(8,128)S(1)}, s32[48,64,128]{2,1,0:T(8,128)S(1)}, u32[]{:S(2)}, u32[]{:S(2)}) collective-permute-start(s32[48,64,128]{2,1,0:T(8,128)S(1)} %get-tuple-element.73), channel_id=1, source_target_pairs={{0,1},{1,0},{2,3},{3,2},{4,5},{5,4},{6,7},{7,6},{8,9},{9,8},{10,11... | collective-permute-start | bytes 4718600 | tf_op jit(solution)/shard_map/pack_tiles/ppermute | solution.py:294
  19.8 5.0 %collective-permute-start.2 = (f32[136,128]{1,0:T(8,128)S(1)}, f32[136,128]{1,0:T(8,128)S(1)}, u32[]{:S(2)}, u32[]{:S(2)}) collective-permute-start(f32[136,128]{1,0:T(8,128)S(1)} %collective-permute-done.1.refs_2_), channel_id=1, source_target_pairs={{0,4},{4,0},{8,12},{12,8},{16,20},{20,16},{24,28},{28,24},{1,5},{5... | collective-permute-start | bytes 208904 | tf_op jit(solution)/shard_map/gather_items/ppermute | solution.py:294
  20.4 5.9 %collective-permute-start.4 = (f32[136,128]{1,0:T(8,128)S(1)}, f32[136,128]{1,0:T(8,128)S(1)}, u32[]{:S(2)}, u32[]{:S(2)}) collective-permute-start(f32[136,128]{1,0:T(8,128)S(1)} %collective-permute-done.3.refs_4_), channel_id=1, source_target_pairs={{0,4},{4,0},{8,12},{12,8},{16,20},{20,16},{24,28},{28,24},{1,5},{5... | collective-permute-start | bytes 208904 | tf_op jit(solution)/shard_map/gather_items/ppermute | solution.py:294
  21.8 5.6 %collective-permute-start.6 = (f32[136,128]{1,0:T(8,128)S(1)}, f32[136,128]{1,0:T(8,128)S(1)}, u32[]{:S(2)}, u32[]{:S(2)}) collective-permute-start(f32[136,128]{1,0:T(8,128)S(1)} %collective-permute-done.5.refs_6_), channel_id=1, source_target_pairs={{0,4},{4,0},{8,12},{12,8},{16,20},{20,16},{24,28},{28,24},{1,5},{5... | collective-permute-start | bytes 208904 | tf_op jit(solution)/shard_map/gather_items/ppermute | solution.py:294
  29.3 41.8 %all-to-all-start = ((s32[4,12,128,128]{3,2,1,0:T(8,128)}), s32[4,12,128,128]{3,2,1,0:T(8,128)}, u32[]{:S(2)}, u32[]{:S(2)}) async-start(s32[4,12,128,128]{3,2,1,0:T(8,128)} %get-tuple-element.113), calls=%async_computation | async-start | bytes 6291456 | tf_op jit(solution)/shard_map/send_tiles/all_to_all | solution.py:344
  35.3 5.6 %collective-permute-start.12 = (f32[136,128]{1,0:T(8,128)S(1)}, f32[136,128]{1,0:T(8,128)S(1)}, u32[]{:S(2)}, u32[]{:S(2)}) collective-permute-start(f32[136,128]{1,0:T(8,128)S(1)} %collective-permute-done.3.refs_4_), channel_id=1, source_target_pairs={{0,1},{1,0},{2,3},{3,2},{4,5},{5,4},{6,7},{7,6},{8,9},{9,8},{10,11... | collective-permute-start | bytes 208904 | tf_op jit(solution)/shard_map/gather_items/ppermute | solution.py:294
  36.1 4.8 %collective-permute-start.13 = (f32[136,128]{1,0:T(8,128)}, f32[136,128]{1,0:T(8,128)S(1)}, u32[]{:S(2)}, u32[]{:S(2)}) collective-permute-start(f32[136,128]{1,0:T(8,128)} %copy-done.6), channel_id=1, source_target_pairs={{0,1},{1,0},{2,3},{3,2},{4,5},{5,4},{6,7},{7,6},{8,9},{9,8},{10,11... | collective-permute-start | bytes 208904 | tf_op jit(solution)/shard_map/gather_items/ppermute | solution.py:294
  41.7 6.4 %collective-permute-start.21 = (f32[256,128]{1,0:T(8,128)S(1)}, f32[256,128]{1,0:T(8,128)S(1)}, u32[]{:S(2)}, u32[]{:S(2)}) collective-permute-start(f32[256,128]{1,0:T(8,128)S(1)} %get-tuple-element.98.own_ref), channel_id=1, source_target_pairs={{0,2},{1,3},{2,0},{3,1},{4,6},{5,7},{6,4},{7,5},{8,10},{9,11},{10,... | collective-permute-start | bytes 393224 | tf_op jit(solution)/shard_map/user_cg/ppermute | solution.py:294
  43.5 8.0 %collective-permute-start.17 = (f32[256,128]{1,0:T(8,128)S(1)}, f32[256,128]{1,0:T(8,128)S(1)}, u32[]{:S(2)}, u32[]{:S(2)}) collective-permute-start(f32[256,128]{1,0:T(8,128)S(1)} %get-tuple-element.85.own_ref), channel_id=1, source_target_pairs={{0,2},{1,3},{2,0},{3,1},{4,6},{5,7},{6,4},{7,5},{8,10},{9,11},{10,... | collective-permute-start | bytes 393224 | tf_op jit(solution)/shard_map/user_cg/ppermute | solution.py:294
  49.7 5.3 %collective-permute-start.22 = (f32[256,128]{1,0:T(8,128)S(1)}, f32[256,128]{1,0:T(8,128)S(1)}, u32[]{:S(2)}, u32[]{:S(2)}) collective-permute-start(f32[256,128]{1,0:T(8,128)S(1)} %get-tuple-element.100.own_ref), channel_id=1, source_target_pairs={{0,2},{1,3},{2,0},{3,1},{4,6},{5,7},{6,4},{7,5},{8,10},{9,11},{10,... | collective-permute-start | bytes 393224 | tf_op jit(solution)/shard_map/user_cg/ppermute | solution.py:294
  53.2 5.9 %collective-permute-start.18 = (f32[256,128]{1,0:T(8,128)S(1)}, f32[256,128]{1,0:T(8,128)S(1)}, u32[]{:S(2)}, u32[]{:S(2)}) collective-permute-start(f32[256,128]{1,0:T(8,128)S(1)} %get-tuple-element.89.own_ref), channel_id=1, source_target_pairs={{0,2},{1,3},{2,0},{3,1},{4,6},{5,7},{6,4},{7,5},{8,10},{9,11},{10,... | collective-permute-start | bytes 393224 | tf_op jit(solution)/shard_map/user_cg/ppermute | solution.py:294
  56.8 5.7 %collective-permute-start.23 = (f32[256,128]{1,0:T(8,128)S(1)}, f32[256,128]{1,0:T(8,128)S(1)}, u32[]{:S(2)}, u32[]{:S(2)}) collective-permute-start(f32[256,128]{1,0:T(8,128)S(1)} %get-tuple-element.104.own_ref), channel_id=1, source_target_pairs={{0,2},{1,3},{2,0},{3,1},{4,6},{5,7},{6,4},{7,5},{8,10},{9,11},{10,... | collective-permute-start | bytes 393224 | tf_op jit(solution)/shard_map/user_cg/ppermute | solution.py:294
  60.8 5.1 %collective-permute-start.19 = (f32[256,128]{1,0:T(8,128)S(1)}, f32[256,128]{1,0:T(8,128)S(1)}, u32[]{:S(2)}, u32[]{:S(2)}) collective-permute-start(f32[256,128]{1,0:T(8,128)S(1)} %get-tuple-element.93.own_ref), channel_id=1, source_target_pairs={{0,2},{1,3},{2,0},{3,1},{4,6},{5,7},{6,4},{7,5},{8,10},{9,11},{10,... | collective-permute-start | bytes 393224 | tf_op jit(solution)/shard_map/user_cg/ppermute | solution.py:294
  71.1 7.3 %collective-permute-start.29 = (f32[512,128]{1,0:T(8,128)S(1)}, f32[512,128]{1,0:T(8,128)S(1)}, u32[]{:S(2)}, u32[]{:S(2)}) collective-permute-start(f32[512,128]{1,0:T(8,128)S(1)} %get-tuple-element.114.refs_0_), channel_id=1, source_target_pairs={{0,8},{4,12},{8,0},{12,4},{16,24},{20,28},{24,16},{28,20},{1,9},{5... | collective-permute-start | bytes 786440 | tf_op jit(solution)/shard_map/gather_users/ppermute | solution.py:294
  73.1 7.5 %collective-permute-start.27 = (f32[512,128]{1,0:T(8,128)S(1)}, f32[512,128]{1,0:T(8,128)S(1)}, u32[]{:S(2)}, u32[]{:S(2)}) collective-permute-start(f32[512,128]{1,0:T(8,128)S(1)} %get-tuple-element.114.refs_0_), channel_id=1, source_target_pairs={{0,4},{4,0},{8,12},{12,8},{16,20},{20,16},{24,28},{28,24},{1,5},{5... | collective-permute-start | bytes 786440 | tf_op jit(solution)/shard_map/gather_users/ppermute | solution.py:294
  78.4 7.1 %collective-permute-start.31 = (f32[512,128]{1,0:T(8,128)S(1)}, f32[512,128]{1,0:T(8,128)S(1)}, u32[]{:S(2)}, u32[]{:S(2)}) collective-permute-start(f32[512,128]{1,0:T(8,128)S(1)} %collective-permute-done.29.refs_4_), channel_id=1, source_target_pairs={{0,4},{4,0},{8,12},{12,8},{16,20},{20,16},{24,28},{28,24},{1,5},{5... | collective-permute-start | bytes 786440 | tf_op jit(solution)/shard_map/gather_users/ppermute | solution.py:294
  79.4 10.2 %collective-permute-start.26 = (f32[512,128]{1,0:T(8,128)S(1)}, f32[512,128]{1,0:T(8,128)S(1)}, u32[]{:S(2)}, u32[]{:S(2)}) collective-permute-start(f32[512,128]{1,0:T(8,128)S(1)} %get-tuple-element.114.refs_0_), channel_id=1, source_target_pairs={{0,1},{1,0},{2,3},{3,2},{4,5},{5,4},{6,7},{7,6},{8,9},{9,8},{10,11... | collective-permute-start | bytes 786440 | tf_op jit(solution)/shard_map/gather_users/ppermute | solution.py:294
  79.4 10.2 %collective-permute-start.30 = (f32[512,128]{1,0:T(8,128)S(1)}, f32[512,128]{1,0:T(8,128)S(1)}, u32[]{:S(2)}, u32[]{:S(2)}) collective-permute-start(f32[512,128]{1,0:T(8,128)S(1)} %collective-permute-done.29.refs_4_), channel_id=1, source_target_pairs={{0,1},{1,0},{2,3},{3,2},{4,5},{5,4},{6,7},{7,6},{8,9},{9,8},{10,11... | collective-permute-start | bytes 786440 | tf_op jit(solution)/shard_map/gather_users/ppermute | solution.py:294
  80.6 9.1 %collective-permute-start.28 = (f32[512,128]{1,0:T(8,128)S(1)}, f32[512,128]{1,0:T(8,128)S(1)}, u32[]{:S(2)}, u32[]{:S(2)}) collective-permute-start(f32[512,128]{1,0:T(8,128)S(1)} %collective-permute-done.27.refs_2_), channel_id=1, source_target_pairs={{0,1},{1,0},{2,3},{3,2},{4,5},{5,4},{6,7},{7,6},{8,9},{9,8},{10,11... | collective-permute-start | bytes 786440 | tf_op jit(solution)/shard_map/gather_users/ppermute | solution.py:294
  90.6 8.7 %collective-permute-start.37 = (f32[128,128]{1,0:T(8,128)S(1)}, f32[128,128]{1,0:T(8,128)S(1)}, u32[]{:S(2)}, u32[]{:S(2)}) collective-permute-start(f32[128,128]{1,0:T(8,128)S(1)} %get-tuple-element.130.own_ref), channel_id=1, source_target_pairs={{0,16},{4,20},{8,24},{12,28},{16,0},{20,4},{24,8},{28,12},{1,17},{... | collective-permute-start | bytes 196616 | tf_op jit(solution)/shard_map/item_cg/ppermute | solution.py:294
  92.3 27.7 %collective-permute-start.25 = (f32[128,128]{1,0:T(8,128)S(1)}, f32[128,128]{1,0:T(8,128)S(1)}, u32[]{:S(2)}, u32[]{:S(2)}) collective-permute-start(f32[128,128]{1,0:T(8,128)S(1)} %get-tuple-element.110), channel_id=1, source_target_pairs={{0,1},{1,0},{2,3},{3,2},{4,5},{5,4},{6,7},{7,6},{8,9},{9,8},{10,11... | collective-permute-start | bytes 196616 | tf_op jit(solution)/shard_map/user_cg/ppermute | solution.py:294
  92.5 8.7 %collective-permute-start.33 = (f32[128,128]{1,0:T(8,128)S(1)}, f32[128,128]{1,0:T(8,128)S(1)}, u32[]{:S(2)}, u32[]{:S(2)}) collective-permute-start(f32[128,128]{1,0:T(8,128)S(1)} %get-tuple-element.117.own_ref), channel_id=1, source_target_pairs={{0,16},{4,20},{8,24},{12,28},{16,0},{20,4},{24,8},{28,12},{1,17},{... | collective-permute-start | bytes 196616 | tf_op jit(solution)/shard_map/item_cg/ppermute | solution.py:294
  101.0 5.9 %collective-permute-start.38 = (f32[128,128]{1,0:T(8,128)S(1)}, f32[128,128]{1,0:T(8,128)S(1)}, u32[]{:S(2)}, u32[]{:S(2)}) collective-permute-start(f32[128,128]{1,0:T(8,128)S(1)} %get-tuple-element.132.own_ref), channel_id=1, source_target_pairs={{0,16},{4,20},{8,24},{12,28},{16,0},{20,4},{24,8},{28,12},{1,17},{... | collective-permute-start | bytes 196616 | tf_op jit(solution)/shard_map/item_cg/ppermute | solution.py:294
  102.7 6.0 %collective-permute-start.34 = (f32[128,128]{1,0:T(8,128)S(1)}, f32[128,128]{1,0:T(8,128)S(1)}, u32[]{:S(2)}, u32[]{:S(2)}) collective-permute-start(f32[128,128]{1,0:T(8,128)S(1)} %get-tuple-element.121.own_ref), channel_id=1, source_target_pairs={{0,16},{4,20},{8,24},{12,28},{16,0},{20,4},{24,8},{28,12},{1,17},{... | collective-permute-start | bytes 196616 | tf_op jit(solution)/shard_map/item_cg/ppermute | solution.py:294
  108.6 6.4 %collective-permute-start.39 = (f32[128,128]{1,0:T(8,128)S(1)}, f32[128,128]{1,0:T(8,128)S(1)}, u32[]{:S(2)}, u32[]{:S(2)}) collective-permute-start(f32[128,128]{1,0:T(8,128)S(1)} %get-tuple-element.136.own_ref), channel_id=1, source_target_pairs={{0,16},{4,20},{8,24},{12,28},{16,0},{20,4},{24,8},{28,12},{1,17},{... | collective-permute-start | bytes 196616 | tf_op jit(solution)/shard_map/item_cg/ppermute | solution.py:294
  110.4 5.6 %collective-permute-start.35 = (f32[128,128]{1,0:T(8,128)S(1)}, f32[128,128]{1,0:T(8,128)S(1)}, u32[]{:S(2)}, u32[]{:S(2)}) collective-permute-start(f32[128,128]{1,0:T(8,128)S(1)} %get-tuple-element.125.own_ref), channel_id=1, source_target_pairs={{0,16},{4,20},{8,24},{12,28},{16,0},{20,4},{24,8},{28,12},{1,17},{... | collective-permute-start | bytes 196616 | tf_op jit(solution)/shard_map/item_cg/ppermute | solution.py:294
  116.0 4.7 %collective-permute-start.40 = (f32[8,128]{1,0:T(8,128)S(1)}, f32[8,128]{1,0:T(8,128)S(1)}, u32[]{:S(2)}, u32[]{:S(2)}) collective-permute-start(f32[8,128]{1,0:T(8,128)S(1)} %get-tuple-element.140.refs_8_), channel_id=1, source_target_pairs={{0,16},{4,20},{8,24},{12,28},{16,0},{20,4},{24,8},{28,12},{1,17},{... | collective-permute-start | bytes 12296 | tf_op jit(solution)/shard_map/item_cg/ppermute | solution.py:294
  117.0 4.6 %collective-permute-start.36 = (f32[8,128]{1,0:T(8,128)S(1)}, f32[8,128]{1,0:T(8,128)S(1)}, u32[]{:S(2)}, u32[]{:S(2)}) collective-permute-start(f32[8,128]{1,0:T(8,128)S(1)} %get-tuple-element.129.refs_3_), channel_id=1, source_target_pairs={{0,16},{4,20},{8,24},{12,28},{16,0},{20,4},{24,8},{28,12},{1,17},{... | collective-permute-start | bytes 12296 | tf_op jit(solution)/shard_map/item_cg/ppermute | solution.py:294
  (20 other events, 66.5 us)

commit v3 on v2

--- a/solution.py
+++ b/solution.py
@@ -207,11 +207,10 @@
     give_ref[...] = out_ref[pl.ds(pl.multiple_of(other * rows, rows), rows), :]
 
 
-def item_tiles_kernel(weight_zero, row_blocks, lists_ref, tiles_ref, dense_ref, weight_ref, token_ref):
+def item_tiles_kernel(weight_zero, row_blocks, lists_ref, tiles_ref, dense_ref, weight_ref):
     near, count, block, _ = tiles_ref.shape
     slots = count // 2
     me = lax.rem(lax.axis_index("user"), near)
-    token_ref[...] = jnp.zeros(token_ref.shape, f32)
     dense_ref[...] = jnp.full(dense_ref.shape, weight_zero, f32)
     weight_ref[...] = jnp.zeros(weight_ref.shape, bf16)
     for source in range(near):
@@ -315,38 +314,35 @@
     named = jnp.pad(named.astype(f32), ((0, 6), (0, rank - slot_total)))
     sent = jnp.concatenate([item_init, named], axis=0)
     near = n_user // 2
-    token = shaped((8, rank))
     with jax.named_scope("gather_items"):
         pieces = {0: sent}
         for mask in (6, 4, 2, 1):
             pieces[mask] = swap(sent, "user", mask)
 
+    with jax.named_scope("gather_items"):
+        for mask in (2, 6, 4):
+            pieces[mask + 1] = swap(pieces[mask], "user", 1)
+        own_items = [pieces[mask] for mask in range(n_user)]
+        other_items = [swap(piece, "item", 1) for piece in own_items]
+
     with jax.named_scope("pack_tiles"):
         given, packed = call(
             functools.partial(pack_kernel, slots),
             (
-                shaped((slot_total, half, block), jnp.int32),
+                pltpu.HBM((slot_total, half, block), jnp.int32),
                 pltpu.HBM((near, 2 * slots, block, block), jnp.int32),
             ),
-            after(ids, *pieces.values()), conf, scalars=1, flops=10 ** 9,
+            after(ids, pieces[3]), conf, scalars=1, flops=10 ** 9,
         )
         other_ids = swap(ids, "item", 1)
         other_half = swap(given, "item", 1)
-
-    with jax.named_scope("gather_items"):
-        for mask in (2, 6, 4):
-            pieces[mask + 1] = swap(pieces[mask], "user", 1)
-        own_items = [pieces[mask] for mask in range(n_user)]
-        ids, *own_items, other_half = lax.optimization_barrier((ids, *own_items, other_half))
 
     with jax.named_scope("send_tiles"):
         halves = [list(range(start, start + near)) for start in (0, near)]
         tiles = lax.all_to_all(
-            after(packed, own_items[-1]), "user", 0, 0, tiled=True, axis_index_groups=halves
-        )
-
-    with jax.named_scope("gather_items"):
-        other_items = [swap(piece, "item", 1) for piece in own_items]
+            after(packed, *own_items), "user", 0, 0, tiled=True, axis_index_groups=halves
+        )
+        ids = after(ids, *own_items)
 
     with jax.named_scope("user_tiles"):
         columns = 2 * n_user * block
@@ -401,16 +397,17 @@
     with jax.named_scope("item_tiles"):
         lists = jnp.stack([pieces[mask][block : block + 2] for mask in range(near)]).astype(jnp.int32)
         columns = near * row_blocks * block
-        item_conf, item_weight, laid = call(
+        item_conf, item_weight = call(
             functools.partial(
                 item_tiles_kernel, unobserved / (user_factors.shape[0] * n_user * n_item), row_blocks
             ),
-            (shaped((2 * block, columns)), shaped((2 * block, columns), bf16), token),
+            (shaped((2 * block, columns)), shaped((2 * block, columns), bf16)),
             lists, tiles, scalars=1, flops=10 ** 9,
         )
 
     with jax.named_scope("gather_users"):
-        found.append(swap(after(found[2], laid), "user", 1))
+        neighbour, item_conf = lax.optimization_barrier((found[2], item_conf))
+        found.append(swap(neighbour, "user", 1))
         marks, ordered = [], []
         for mask, piece in enumerate(found):
             marks += [(mask, True), (mask, False)]

time: 123 us -> 114 us (0.927)
  waiting for transfers between devices: 38.6 us -> 32.9 us
  local copies, waits for them, and re-layouts: 5.22 us -> 3.16 us
  starting transfers between devices: 44.7 us -> 42.8 us
    ppermute x41, waiting for transfers between devices: 38.6 us -> 32.9 us  [swap(): lax.ppermute(value, axis, [(place, place ^ mask) for place in range(size)])]
    unnamed x20 -> x16, local copies, waits for them, and re-layouts: 5.2 us -> 3.15 us
    ppermute x41, starting transfers between devices: 39.8 us -> 37.9 us  [swap(): lax.ppermute(value, axis, [(place, place ^ mask) for place in range(size)])]
  transfers between devices with their start and end apart: 42 -> 42, of which waited for: 17 -> 16; matrix products, arithmetic and copies ran while one was open for 1% -> 1% of each run, Pallas kernels for 21% -> 25%
where the time goes in v3:
time: 114 us; the launch traced here: 113 us
  starting transfers between devices  42.8 us (38%)
  waiting for transfers between devices  32.9 us (29%)
  Pallas kernels  30.6 us (27%)
  local copies, waits for them, and re-layouts  3.16 us (3%)
  other arithmetic  2.29 us (2%)
  between operations  1.59 us (1%)
    ppermute x41, starting transfers between devices, swap(): lax.ppermute(value, axis, [(place, place ^ mask) for place in range(size)])  37.9 us
    ppermute x41, waiting for transfers between devices, swap(): lax.ppermute(value, axis, [(place, place ^ mask) for place in range(size)])  32.9 us
    pallas_call x20, Pallas kernels, call(): pl.pallas_call(kernel, out_shape=tuple(outs), in_specs=[pl.BlockSpec(memo...  30.6 us
    all_to_all x1, starting transfers between devices, dense_shards(): lax.all_to_all(after(packed, *own_items), 'user', 0, 0, tiled=True, axis_...  4.91 us
    unnamed x16, local copies, waits for them, and re-layouts  3.15 us
  transfers between devices with their start and end apart: 42, of which 16 were waited for; matrix products, arithmetic and copies ran while one was open for 1% of the time, Pallas kernels for 25%

profile of v3, /device:TPU:0, one launch (start us, length us, event | category | flops | bytes accessed | tf_op | source)
XLA Modules:
  0.0 113.3 jit_solution(9798169221463452287)
XLA Ops:
  2.2 3.0 %collective-permute-start.1 = (f32[136,128]{1,0:T(8,128)S(1)}, f32[136,128]{1,0:T(8,128)S(1)}, u32[]{:S(2)}, u32[]{:S(2)}) collective-permute-start(f32[136,128]{1,0:T(8,128)S(1)} %pad_maximum_fusion.refs_0_), channel_id=1, source_target_pairs={{0,8},{4,12},{8,0},{12,4},{16,24},{20,28},{24,16},{28,20},{1,9},{5... | collective-permute-start | bytes 208904 | tf_op jit(solution)/shard_map/gather_items/ppermute | solution.py:293
  5.2 2.6 %collective-permute-start.3 = (f32[136,128]{1,0:T(8,128)S(1)}, f32[136,128]{1,0:T(8,128)S(1)}, u32[]{:S(2)}, u32[]{:S(2)}) collective-permute-start(f32[136,128]{1,0:T(8,128)S(1)} %pad_maximum_fusion.refs_0_), channel_id=1, source_target_pairs={{0,16},{4,20},{8,24},{12,28},{16,0},{20,4},{24,8},{28,12},{1,17},{... | collective-permute-start | bytes 208904 | tf_op jit(solution)/shard_map/gather_items/ppermute | solution.py:293
  7.8 1.7 %collective-permute-start = (f32[136,128]{1,0:T(8,128)S(1)}, f32[136,128]{1,0:T(8,128)S(1)}, u32[]{:S(2)}, u32[]{:S(2)}) collective-permute-start(f32[136,128]{1,0:T(8,128)S(1)} %pad_maximum_fusion.refs_0_), channel_id=1, source_target_pairs={{0,4},{4,0},{8,12},{12,8},{16,20},{20,16},{24,28},{28,24},{1,5},{5... | collective-permute-start | bytes 208904 | tf_op jit(solution)/shard_map/gather_items/ppermute | solution.py:293
  15.5 1.9 %copy-done = s32[1,1,48,128,128]{4,3,2,1,0:T(8,128)S(1)} copy-done((s32[1,1,48,128,128]{4,3,2,1,0:T(8,128)S(1)}, s32[1,1,48,128,128]{4,3,2,1,0:T(8,128)}, u32[]{:S(2)}) %copy-start) | copy-done | bytes 3145752
  17.4 3.0 %pack_tiles.1 = (s32[48,64,128]{2,1,0:T(8,128)}, s32[4,12,128,128]{3,2,1,0:T(8,128)}) custom-call(s32[97]{0:T(128)S(1)} %pad_add_fusion.ids_ref.own_ids, s32[48,128,128]{2,1,0:T(8,128)S(1)} %bitcast.15), custom_call_target="tpu_custom_call" | custom-call | flops 1000000000 | bytes 7864708 | tf_op jit(solution)/shard_map/pack_tiles/pallas_call | solution.py:267
  21.7 4.9 %all-to-all-start = ((s32[4,12,128,128]{3,2,1,0:T(8,128)}), s32[4,12,128,128]{3,2,1,0:T(8,128)}, u32[]{:S(2)}, u32[]{:S(2)}) async-start(s32[4,12,128,128]{3,2,1,0:T(8,128)} %get-tuple-element.97), calls=%async_computation | async-start | bytes 6291456 | tf_op jit(solution)/shard_map/send_tiles/all_to_all | solution.py:342
  27.8 2.2 %collective-permute-done.15.other_ids = s32[97]{0:T(128)S(1)} collective-permute-done((s32[97]{0:T(128)S(1)}, s32[97]{0:T(128)S(1)}, u32[]{:S(2)}, u32[]{:S(2)}) %collective-permute-start.15) | collective-permute-done | bytes 420 | tf_op jit(solution)/shard_map/pack_tiles/ppermute | solution.py:293
  31.5 2.7 %user_tiles.1 = (f32[512,2048]{1,0:T(8,128)S(1)}, bf16[512,2048]{1,0:T(8,128)(2,1)S(1)}) custom-call(s32[97]{0:T(128)S(1)} %pad_add_fusion.ids_ref.own_ids, s32[97]{0:T(128)S(1)} %collective-permute-done.15.other_ids, s32[48,128,128]{2,1,0:T(8,128)S(1)} %bitcast.16, s32[48,64,128]{2,1,0:T(8,128)S(1)} %collective-permute-done.16.half_ref), custom_call_target="tpu_custom_call" | custom-call | flops 1000000000 | bytes 13107976 | tf_op jit(solution)/shard_map/user_tiles/pallas_call | solution.py:267
  35.0 1.6 %collective-permute-start.21 = (f32[256,128]{1,0:T(8,128)S(1)}, f32[256,128]{1,0:T(8,128)S(1)}, u32[]{:S(2)}, u32[]{:S(2)}) collective-permute-start(f32[256,128]{1,0:T(8,128)S(1)} %get-tuple-element.82.own_ref), channel_id=1, source_target_pairs={{0,2},{1,3},{2,0},{3,1},{4,6},{5,7},{6,4},{7,5},{8,10},{9,11},{10,... | collective-permute-start | bytes 393224 | tf_op jit(solution)/shard_map/user_cg/ppermute | solution.py:293
  37.1 4.3 %collective-permute-done.21.other_ref = f32[256,128]{1,0:T(8,128)S(1)} collective-permute-done((f32[256,128]{1,0:T(8,128)S(1)}, f32[256,128]{1,0:T(8,128)S(1)}, u32[]{:S(2)}, u32[]{:S(2)}) %collective-permute-start.21) | collective-permute-done | bytes 131104 | tf_op jit(solution)/shard_map/user_cg/ppermute | solution.py:293
  41.4 1.7 %user_cg.13 = (f32[256,128]{1,0:T(8,128)S(1)}, f32[256,128]{1,0:T(8,128)S(1)}) custom-call(f32[256,128]{1,0:T(8,128)S(1)} %get-tuple-element.82.own_ref, f32[256,128]{1,0:T(8,128)S(1)} %collective-permute-done.21.other_ref, f32[512,2048]{1,0:T(8,128)S(1)} %get-tuple-element.70.conf_ref, bf16[2048,256]{1,0:T(8,128)(2,1)S(1)} %get-tuple-element.71.pairs_ref), custom_call_target="tpu_custom_call" | custom-call | flops 805306368 | bytes 5767168 | tf_op jit(solution)/shard_map/user_cg/pallas_call | solution.py:267
  43.1 1.6 %collective-permute-start.22 = (f32[256,128]{1,0:T(8,128)S(1)}, f32[256,128]{1,0:T(8,128)S(1)}, u32[]{:S(2)}, u32[]{:S(2)}) collective-permute-start(f32[256,128]{1,0:T(8,128)S(1)} %get-tuple-element.84.own_ref), channel_id=1, source_target_pairs={{0,2},{1,3},{2,0},{3,1},{4,6},{5,7},{6,4},{7,5},{8,10},{9,11},{10,... | collective-permute-start | bytes 393224 | tf_op jit(solution)/shard_map/user_cg/ppermute | solution.py:293
  44.7 1.7 %user_cg.10 = (f32[256,128]{1,0:T(8,128)S(1)}, f32[256,128]{1,0:T(8,128)S(1)}) custom-call(f32[256,128]{1,0:T(8,128)S(1)} %get-tuple-element.69.own_ref, f32[256,128]{1,0:T(8,128)S(1)} %collective-permute-done.17.other_ref, f32[512,2048]{1,0:T(8,128)S(1)} %get-tuple-element.70.conf_ref, bf16[2048,256]{1,0:T(8,128)(2,1)S(1)} %get-tuple-element.71.pairs_ref), custom_call_target="tpu_custom_call" | custom-call | flops 805306368 | bytes 5767168 | tf_op jit(solution)/shard_map/user_cg/pallas_call | solution.py:267
  46.9 2.1 %collective-permute-done.22.other_ref = f32[256,128]{1,0:T(8,128)S(1)} collective-permute-done((f32[256,128]{1,0:T(8,128)S(1)}, f32[256,128]{1,0:T(8,128)S(1)}, u32[]{:S(2)}, u32[]{:S(2)}) %collective-permute-start.22) | collective-permute-done | bytes 131104 | tf_op jit(solution)/shard_map/user_cg/ppermute | solution.py:293
  49.0 1.8 %user_cg.14 = (f32[256,128]{1,0:T(8,128)S(1)}, f32[256,128]{1,0:T(8,128)S(1)}, f32[256,128]{1,0:T(8,128)S(1)}, f32[256,128]{1,0:T(8,128)S(1)}) custom-call(f32[256,128]{1,0:T(8,128)S(1)} %get-tuple-element.83.side_ref, f32[256,128]{1,0:T(8,128)S(1)} %get-tuple-element.84.own_ref, f32[256,128]{1,0:T(8,128)S(1)} %collective-permute-done.22.other_ref, ...), custom_call_target="tpu_custom_call" | custom-call | flops 805306368 | bytes 6160384 | tf_op jit(solution)/shard_map/user_cg/pallas_call | solution.py:267
  50.8 1.8 %collective-permute-start.23 = (f32[256,128]{1,0:T(8,128)S(1)}, f32[256,128]{1,0:T(8,128)S(1)}, u32[]{:S(2)}, u32[]{:S(2)}) collective-permute-start(f32[256,128]{1,0:T(8,128)S(1)} %get-tuple-element.88.own_ref), channel_id=1, source_target_pairs={{0,2},{1,3},{2,0},{3,1},{4,6},{5,7},{6,4},{7,5},{8,10},{9,11},{10,... | collective-permute-start | bytes 393224 | tf_op jit(solution)/shard_map/user_cg/ppermute | solution.py:293
  52.6 1.8 %user_cg.11 = (f32[256,128]{1,0:T(8,128)S(1)}, f32[256,128]{1,0:T(8,128)S(1)}, f32[256,128]{1,0:T(8,128)S(1)}, f32[256,128]{1,0:T(8,128)S(1)}) custom-call(f32[256,128]{1,0:T(8,128)S(1)} %get-tuple-element.72.side_ref, f32[256,128]{1,0:T(8,128)S(1)} %get-tuple-element.73.own_ref, f32[256,128]{1,0:T(8,128)S(1)} %collective-permute-done.18.other_ref, ...), custom_call_target="tpu_custom_call" | custom-call | flops 805306368 | bytes 6160384 | tf_op jit(solution)/shard_map/user_cg/pallas_call | solution.py:267
  54.8 2.4 %collective-permute-done.23.other_ref = f32[256,128]{1,0:T(8,128)S(1)} collective-permute-done((f32[256,128]{1,0:T(8,128)S(1)}, f32[256,128]{1,0:T(8,128)S(1)}, u32[]{:S(2)}, u32[]{:S(2)}) %collective-permute-start.23) | collective-permute-done | bytes 131104 | tf_op jit(solution)/shard_map/user_cg/ppermute | solution.py:293
  58.2 1.8 %collective-permute-start.24 = (f32[8,256]{1,0:T(8,128)S(1)}, f32[8,256]{1,0:T(8,128)S(1)}, u32[]{:S(2)}, u32[]{:S(2)}) collective-permute-start(f32[8,256]{1,0:T(8,128)S(1)} %get-tuple-element.92.refs_8_), channel_id=1, source_target_pairs={{0,2},{1,3},{2,0},{3,1},{4,6},{5,7},{6,4},{7,5},{8,10},{9,11},{10,... | collective-permute-start | bytes 24584 | tf_op jit(solution)/shard_map/user_cg/ppermute | solution.py:293
  61.9 2.8 %collective-permute-done.20.refs_4_ = f32[8,256]{1,0:T(8,128)S(1)} collective-permute-done((f32[8,256]{1,0:T(8,128)S(1)}, f32[8,256]{1,0:T(8,128)S(1)}, u32[]{:S(2)}, u32[]{:S(2)}) %collective-permute-start.20) | collective-permute-done | bytes 8224 | tf_op jit(solution)/shard_map/user_cg/ppermute | solution.py:293
  65.2 1.6 %collective-permute-start.29 = (f32[512,128]{1,0:T(8,128)S(1)}, f32[512,128]{1,0:T(8,128)S(1)}, u32[]{:S(2)}, u32[]{:S(2)}) collective-permute-start(f32[512,128]{1,0:T(8,128)S(1)} %get-tuple-element.98.refs_0_), channel_id=1, source_target_pairs={{0,8},{4,12},{8,0},{12,4},{16,24},{20,28},{24,16},{28,20},{1,9},{5... | collective-permute-start | bytes 786440 | tf_op jit(solution)/shard_map/gather_users/ppermute | solution.py:293
  67.9 3.5 %item_tiles.1 = (f32[256,4096]{1,0:T(8,128)S(1)}, bf16[256,4096]{1,0:T(8,128)(2,1)S(1)}) custom-call(s32[4,2,128]{2,1,0:T(2,128)S(1)} %maximum_convert_fusion.lists_ref, s32[4,12,128,128]{3,2,1,0:T(8,128)} %all-to-all-done.tiles_ref), custom_call_target="tpu_custom_call" | custom-call | flops 1000000000 | bytes 11538432 | tf_op jit(solution)/shard_map/item_tiles/pallas_call | solution.py:267
  73.7 2.2 %collective-permute-done.27.refs_2_ = f32[512,128]{1,0:T(8,128)S(1)} collective-permute-done((f32[512,128]{1,0:T(8,128)S(1)}, f32[512,128]{1,0:T(8,128)S(1)}, u32[]{:S(2)}, u32[]{:S(2)}) %collective-permute-start.27) | collective-permute-done | bytes 262176 | tf_op jit(solution)/shard_map/gather_users/ppermute | solution.py:293
  75.9 2.8 %collective-permute-done.31.refs_6_ = f32[512,128]{1,0:T(8,128)S(1)} collective-permute-done((f32[512,128]{1,0:T(8,128)S(1)}, f32[512,128]{1,0:T(8,128)S(1)}, u32[]{:S(2)}, u32[]{:S(2)}) %collective-permute-start.31) | collective-permute-done | bytes 262176 | tf_op jit(solution)/shard_map/gather_users/ppermute | solution.py:293
  81.2 1.9 %collective-permute-start.37 = (f32[128,128]{1,0:T(8,128)S(1)}, f32[128,128]{1,0:T(8,128)S(1)}, u32[]{:S(2)}, u32[]{:S(2)}) collective-permute-start(f32[128,128]{1,0:T(8,128)S(1)} %get-tuple-element.116.own_ref), channel_id=1, source_target_pairs={{0,16},{4,20},{8,24},{12,28},{16,0},{20,4},{24,8},{28,12},{1,17},{... | collective-permute-start | bytes 196616 | tf_op jit(solution)/shard_map/item_cg/ppermute | solution.py:293
  84.1 5.3 %collective-permute-done.37.other_ref = f32[128,128]{1,0:T(8,128)S(1)} collective-permute-done((f32[128,128]{1,0:T(8,128)S(1)}, f32[128,128]{1,0:T(8,128)S(1)}, u32[]{:S(2)}, u32[]{:S(2)}) %collective-permute-start.37) | collective-permute-done | bytes 65568 | tf_op jit(solution)/shard_map/item_cg/ppermute | solution.py:293
  89.5 1.8 %item_cg.12 = (f32[128,128]{1,0:T(8,128)S(1)}, f32[128,128]{1,0:T(8,128)S(1)}) custom-call(f32[128,128]{1,0:T(8,128)S(1)} %get-tuple-element.116.own_ref, f32[128,128]{1,0:T(8,128)S(1)} %collective-permute-done.37.other_ref, f32[256,4096]{1,0:T(8,128)S(1)} %get-tuple-element.104.conf_ref, bf16[4096,256]{1,0:T(8,128)(2,1)S(1)} %get-tuple-element.105.pairs_ref), custom_call_target="tpu_custom_call" | custom-call | flops 805306368 | bytes 6553600 | tf_op jit(solution)/shard_map/item_cg/pallas_call | solution.py:267
  92.9 3.0 %collective-permute-start.34 = (f32[128,128]{1,0:T(8,128)S(1)}, f32[128,128]{1,0:T(8,128)S(1)}, u32[]{:S(2)}, u32[]{:S(2)}) collective-permute-start(f32[128,128]{1,0:T(8,128)S(1)} %get-tuple-element.107.own_ref), channel_id=1, source_target_pairs={{0,16},{4,20},{8,24},{12,28},{16,0},{20,4},{24,8},{28,12},{1,17},{... | collective-permute-start | bytes 196616 | tf_op jit(solution)/shard_map/item_cg/ppermute | solution.py:293
  97.4 1.7 %item_cg.13 = (f32[128,128]{1,0:T(8,128)S(1)}, f32[128,128]{1,0:T(8,128)S(1)}, f32[128,128]{1,0:T(8,128)S(1)}, f32[128,128]{1,0:T(8,128)S(1)}) custom-call(f32[128,128]{1,0:T(8,128)S(1)} %get-tuple-element.117.side_ref, f32[128,128]{1,0:T(8,128)S(1)} %get-tuple-element.118.own_ref, f32[128,128]{1,0:T(8,128)S(1)} %collective-permute-done.38.other_ref, ...), custom_call_target="tpu_custom_call" | custom-call | flops 805306368 | bytes 6750208 | tf_op jit(solution)/shard_map/item_cg/pallas_call | solution.py:267
  99.2 1.7 %item_cg.10 = (f32[128,128]{1,0:T(8,128)S(1)}, f32[128,128]{1,0:T(8,128)S(1)}, f32[128,128]{1,0:T(8,128)S(1)}, f32[128,128]{1,0:T(8,128)S(1)}) custom-call(f32[128,128]{1,0:T(8,128)S(1)} %get-tuple-element.106.side_ref, f32[128,128]{1,0:T(8,128)S(1)} %get-tuple-element.107.own_ref, f32[128,128]{1,0:T(8,128)S(1)} %collective-permute-done.34.other_ref, ...), custom_call_target="tpu_custom_call" | custom-call | flops 805306368 | bytes 6750208 | tf_op jit(solution)/shard_map/item_cg/pallas_call | solution.py:267
  100.9 3.0 %collective-permute-start.35 = (f32[128,128]{1,0:T(8,128)S(1)}, f32[128,128]{1,0:T(8,128)S(1)}, u32[]{:S(2)}, u32[]{:S(2)}) collective-permute-start(f32[128,128]{1,0:T(8,128)S(1)} %get-tuple-element.111.own_ref), channel_id=1, source_target_pairs={{0,16},{4,20},{8,24},{12,28},{16,0},{20,4},{24,8},{28,12},{1,17},{... | collective-permute-start | bytes 196616 | tf_op jit(solution)/shard_map/item_cg/ppermute | solution.py:293
  107.8 2.3 %collective-permute-start.36 = (f32[8,128]{1,0:T(8,128)S(1)}, f32[8,128]{1,0:T(8,128)S(1)}, u32[]{:S(2)}, u32[]{:S(2)}) collective-permute-start(f32[8,128]{1,0:T(8,128)S(1)} %get-tuple-element.115.refs_3_), channel_id=1, source_target_pairs={{0,16},{4,20},{8,24},{12,28},{16,0},{20,4},{24,8},{28,12},{1,17},{... | collective-permute-start | bytes 12296 | tf_op jit(solution)/shard_map/item_cg/ppermute | solution.py:293
  (97 shorter events, 33.4 us)
Async XLA Ops:
  2.2 8.0 %collective-permute-start.1 = (f32[136,128]{1,0:T(8,128)S(1)}, f32[136,128]{1,0:T(8,128)S(1)}, u32[]{:S(2)}, u32[]{:S(2)}) collective-permute-start(f32[136,128]{1,0:T(8,128)S(1)} %pad_maximum_fusion.refs_0_), channel_id=1, source_target_pairs={{0,8},{4,12},{8,0},{12,4},{16,24},{20,28},{24,16},{28,20},{1,9},{5... | collective-permute-start | bytes 208904 | tf_op jit(solution)/shard_map/gather_items/ppermute | solution.py:293
  5.2 7.5 %collective-permute-start.3 = (f32[136,128]{1,0:T(8,128)S(1)}, f32[136,128]{1,0:T(8,128)S(1)}, u32[]{:S(2)}, u32[]{:S(2)}) collective-permute-start(f32[136,128]{1,0:T(8,128)S(1)} %pad_maximum_fusion.refs_0_), channel_id=1, source_target_pairs={{0,16},{4,20},{8,24},{12,28},{16,0},{20,4},{24,8},{28,12},{1,17},{... | collective-permute-start | bytes 208904 | tf_op jit(solution)/shard_map/gather_items/ppermute | solution.py:293
  7.8 6.5 %collective-permute-start.5 = (f32[136,128]{1,0:T(8,128)S(1)}, f32[136,128]{1,0:T(8,128)S(1)}, u32[]{:S(2)}, u32[]{:S(2)}) collective-permute-start(f32[136,128]{1,0:T(8,128)S(1)} %pad_maximum_fusion.refs_0_), channel_id=1, source_target_pairs={{0,24},{4,28},{8,16},{12,20},{16,8},{20,12},{24,0},{28,4},{1,25},{... | collective-permute-start | bytes 208904 | tf_op jit(solution)/shard_map/gather_items/ppermute | solution.py:293
  7.8 12.7 %collective-permute-start = (f32[136,128]{1,0:T(8,128)S(1)}, f32[136,128]{1,0:T(8,128)S(1)}, u32[]{:S(2)}, u32[]{:S(2)}) collective-permute-start(f32[136,128]{1,0:T(8,128)S(1)} %pad_maximum_fusion.refs_0_), channel_id=1, source_target_pairs={{0,4},{4,0},{8,12},{12,8},{16,20},{20,16},{24,28},{28,24},{1,5},{5... | collective-permute-start | bytes 208904 | tf_op jit(solution)/shard_map/gather_items/ppermute | solution.py:293
  10.2 5.3 %collective-permute-start.2 = (f32[136,128]{1,0:T(8,128)S(1)}, f32[136,128]{1,0:T(8,128)S(1)}, u32[]{:S(2)}, u32[]{:S(2)}) collective-permute-start(f32[136,128]{1,0:T(8,128)S(1)} %collective-permute-done.1.refs_2_), channel_id=1, source_target_pairs={{0,4},{4,0},{8,12},{12,8},{16,20},{20,16},{24,28},{28,24},{1,5},{5... | collective-permute-start | bytes 208904 | tf_op jit(solution)/shard_map/gather_items/ppermute | solution.py:293
  12.7 7.7 %collective-permute-start.4 = (f32[136,128]{1,0:T(8,128)S(1)}, f32[136,128]{1,0:T(8,128)S(1)}, u32[]{:S(2)}, u32[]{:S(2)}) collective-permute-start(f32[136,128]{1,0:T(8,128)S(1)} %collective-permute-done.3.refs_4_), channel_id=1, source_target_pairs={{0,4},{4,0},{8,12},{12,8},{16,20},{20,16},{24,28},{28,24},{1,5},{5... | collective-permute-start | bytes 208904 | tf_op jit(solution)/shard_map/gather_items/ppermute | solution.py:293
  14.2 6.2 %collective-permute-start.6 = (f32[136,128]{1,0:T(8,128)S(1)}, f32[136,128]{1,0:T(8,128)S(1)}, u32[]{:S(2)}, u32[]{:S(2)}) collective-permute-start(f32[136,128]{1,0:T(8,128)S(1)} %collective-permute-done.5.refs_6_), channel_id=1, source_target_pairs={{0,4},{4,0},{8,12},{12,8},{16,20},{20,16},{24,28},{28,24},{1,5},{5... | collective-permute-start | bytes 208904 | tf_op jit(solution)/shard_map/gather_items/ppermute | solution.py:293
  21.7 43.5 %all-to-all-start = ((s32[4,12,128,128]{3,2,1,0:T(8,128)}), s32[4,12,128,128]{3,2,1,0:T(8,128)}, u32[]{:S(2)}, u32[]{:S(2)}) async-start(s32[4,12,128,128]{3,2,1,0:T(8,128)} %get-tuple-element.97), calls=%async_computation | async-start | bytes 6291456 | tf_op jit(solution)/shard_map/send_tiles/all_to_all | solution.py:342
  26.7 4.4 %collective-permute-start.16 = (s32[48,64,128]{2,1,0:T(8,128)}, s32[48,64,128]{2,1,0:T(8,128)S(1)}, u32[]{:S(2)}, u32[]{:S(2)}) collective-permute-start(s32[48,64,128]{2,1,0:T(8,128)} %get-tuple-element.67), channel_id=1, source_target_pairs={{0,1},{1,0},{2,3},{3,2},{4,5},{5,4},{6,7},{7,6},{8,9},{9,8},{10,11... | collective-permute-start | bytes 4718600 | tf_op jit(solution)/shard_map/pack_tiles/ppermute | solution.py:293
  30.1 4.1 %collective-permute-start.13 = (f32[136,128]{1,0:T(8,128)}, f32[136,128]{1,0:T(8,128)S(1)}, u32[]{:S(2)}, u32[]{:S(2)}) collective-permute-start(f32[136,128]{1,0:T(8,128)} %copy-done.2), channel_id=1, source_target_pairs={{0,1},{1,0},{2,3},{3,2},{4,5},{5,4},{6,7},{7,6},{8,9},{9,8},{10,11... | collective-permute-start | bytes 208904 | tf_op jit(solution)/shard_map/gather_items/ppermute | solution.py:293
  30.5 3.7 %collective-permute-start.8 = (f32[136,128]{1,0:T(8,128)S(1)}, f32[136,128]{1,0:T(8,128)S(1)}, u32[]{:S(2)}, u32[]{:S(2)}) collective-permute-start(f32[136,128]{1,0:T(8,128)S(1)} %collective-permute-done.refs_1_), channel_id=1, source_target_pairs={{0,1},{1,0},{2,3},{3,2},{4,5},{5,4},{6,7},{7,6},{8,9},{9,8},{10,11... | collective-permute-start | bytes 208904 | tf_op jit(solution)/shard_map/gather_items/ppermute | solution.py:293
  35.0 6.4 %collective-permute-start.21 = (f32[256,128]{1,0:T(8,128)S(1)}, f32[256,128]{1,0:T(8,128)S(1)}, u32[]{:S(2)}, u32[]{:S(2)}) collective-permute-start(f32[256,128]{1,0:T(8,128)S(1)} %get-tuple-element.82.own_ref), channel_id=1, source_target_pairs={{0,2},{1,3},{2,0},{3,1},{4,6},{5,7},{6,4},{7,5},{8,10},{9,11},{10,... | collective-permute-start | bytes 393224 | tf_op jit(solution)/shard_map/user_cg/ppermute | solution.py:293
  36.6 8.1 %collective-permute-start.17 = (f32[256,128]{1,0:T(8,128)S(1)}, f32[256,128]{1,0:T(8,128)S(1)}, u32[]{:S(2)}, u32[]{:S(2)}) collective-permute-start(f32[256,128]{1,0:T(8,128)S(1)} %get-tuple-element.69.own_ref), channel_id=1, source_target_pairs={{0,2},{1,3},{2,0},{3,1},{4,6},{5,7},{6,4},{7,5},{8,10},{9,11},{10,... | collective-permute-start | bytes 393224 | tf_op jit(solution)/shard_map/user_cg/ppermute | solution.py:293
  43.1 5.9 %collective-permute-start.22 = (f32[256,128]{1,0:T(8,128)S(1)}, f32[256,128]{1,0:T(8,128)S(1)}, u32[]{:S(2)}, u32[]{:S(2)}) collective-permute-start(f32[256,128]{1,0:T(8,128)S(1)} %get-tuple-element.84.own_ref), channel_id=1, source_target_pairs={{0,2},{1,3},{2,0},{3,1},{4,6},{5,7},{6,4},{7,5},{8,10},{9,11},{10,... | collective-permute-start | bytes 393224 | tf_op jit(solution)/shard_map/user_cg/ppermute | solution.py:293
  46.4 6.3 %collective-permute-start.18 = (f32[256,128]{1,0:T(8,128)S(1)}, f32[256,128]{1,0:T(8,128)S(1)}, u32[]{:S(2)}, u32[]{:S(2)}) collective-permute-start(f32[256,128]{1,0:T(8,128)S(1)} %get-tuple-element.73.own_ref), channel_id=1, source_target_pairs={{0,2},{1,3},{2,0},{3,1},{4,6},{5,7},{6,4},{7,5},{8,10},{9,11},{10,... | collective-permute-start | bytes 393224 | tf_op jit(solution)/shard_map/user_cg/ppermute | solution.py:293
  50.8 6.4 %collective-permute-start.23 = (f32[256,128]{1,0:T(8,128)S(1)}, f32[256,128]{1,0:T(8,128)S(1)}, u32[]{:S(2)}, u32[]{:S(2)}) collective-permute-start(f32[256,128]{1,0:T(8,128)S(1)} %get-tuple-element.88.own_ref), channel_id=1, source_target_pairs={{0,2},{1,3},{2,0},{3,1},{4,6},{5,7},{6,4},{7,5},{8,10},{9,11},{10,... | collective-permute-start | bytes 393224 | tf_op jit(solution)/shard_map/user_cg/ppermute | solution.py:293
  54.4 5.6 %collective-permute-start.19 = (f32[256,128]{1,0:T(8,128)S(1)}, f32[256,128]{1,0:T(8,128)S(1)}, u32[]{:S(2)}, u32[]{:S(2)}) collective-permute-start(f32[256,128]{1,0:T(8,128)S(1)} %get-tuple-element.77.own_ref), channel_id=1, source_target_pairs={{0,2},{1,3},{2,0},{3,1},{4,6},{5,7},{6,4},{7,5},{8,10},{9,11},{10,... | collective-permute-start | bytes 393224 | tf_op jit(solution)/shard_map/user_cg/ppermute | solution.py:293
  58.2 3.7 %collective-permute-start.24 = (f32[8,256]{1,0:T(8,128)S(1)}, f32[8,256]{1,0:T(8,128)S(1)}, u32[]{:S(2)}, u32[]{:S(2)}) collective-permute-start(f32[8,256]{1,0:T(8,128)S(1)} %get-tuple-element.92.refs_8_), channel_id=1, source_target_pairs={{0,2},{1,3},{2,0},{3,1},{4,6},{5,7},{6,4},{7,5},{8,10},{9,11},{10,... | collective-permute-start | bytes 24584 | tf_op jit(solution)/shard_map/user_cg/ppermute | solution.py:293
  65.2 6.4 %collective-permute-start.29 = (f32[512,128]{1,0:T(8,128)S(1)}, f32[512,128]{1,0:T(8,128)S(1)}, u32[]{:S(2)}, u32[]{:S(2)}) collective-permute-start(f32[512,128]{1,0:T(8,128)S(1)} %get-tuple-element.98.refs_0_), channel_id=1, source_target_pairs={{0,8},{4,12},{8,0},{12,4},{16,24},{20,28},{24,16},{28,20},{1,9},{5... | collective-permute-start | bytes 786440 | tf_op jit(solution)/shard_map/gather_users/ppermute | solution.py:293
  66.9 9.0 %collective-permute-start.27 = (f32[512,128]{1,0:T(8,128)S(1)}, f32[512,128]{1,0:T(8,128)S(1)}, u32[]{:S(2)}, u32[]{:S(2)}) collective-permute-start(f32[512,128]{1,0:T(8,128)S(1)} %get-tuple-element.98.refs_0_), channel_id=1, source_target_pairs={{0,4},{4,0},{8,12},{12,8},{16,20},{20,16},{24,28},{28,24},{1,5},{5... | collective-permute-start | bytes 786440 | tf_op jit(solution)/shard_map/gather_users/ppermute | solution.py:293
  71.6 7.0 %collective-permute-start.31 = (f32[512,128]{1,0:T(8,128)S(1)}, f32[512,128]{1,0:T(8,128)S(1)}, u32[]{:S(2)}, u32[]{:S(2)}) collective-permute-start(f32[512,128]{1,0:T(8,128)S(1)} %collective-permute-done.29.refs_4_), channel_id=1, source_target_pairs={{0,4},{4,0},{8,12},{12,8},{16,20},{20,16},{24,28},{28,24},{1,5},{5... | collective-permute-start | bytes 786440 | tf_op jit(solution)/shard_map/gather_users/ppermute | solution.py:293
  73.2 5.5 %collective-permute-start.26 = (f32[512,128]{1,0:T(8,128)S(1)}, f32[512,128]{1,0:T(8,128)S(1)}, u32[]{:S(2)}, u32[]{:S(2)}) collective-permute-start(f32[512,128]{1,0:T(8,128)S(1)} %get-tuple-element.98.refs_0_), channel_id=1, source_target_pairs={{0,1},{1,0},{2,3},{3,2},{4,5},{5,4},{6,7},{7,6},{8,9},{9,8},{10,11... | collective-permute-start | bytes 786440 | tf_op jit(solution)/shard_map/gather_users/ppermute | solution.py:293
  73.2 5.5 %collective-permute-start.30 = (f32[512,128]{1,0:T(8,128)S(1)}, f32[512,128]{1,0:T(8,128)S(1)}, u32[]{:S(2)}, u32[]{:S(2)}) collective-permute-start(f32[512,128]{1,0:T(8,128)S(1)} %collective-permute-done.29.refs_4_), channel_id=1, source_target_pairs={{0,1},{1,0},{2,3},{3,2},{4,5},{5,4},{6,7},{7,6},{8,9},{9,8},{10,11... | collective-permute-start | bytes 786440 | tf_op jit(solution)/shard_map/gather_users/ppermute | solution.py:293
  81.2 8.3 %collective-permute-start.37 = (f32[128,128]{1,0:T(8,128)S(1)}, f32[128,128]{1,0:T(8,128)S(1)}, u32[]{:S(2)}, u32[]{:S(2)}) collective-permute-start(f32[128,128]{1,0:T(8,128)S(1)} %get-tuple-element.116.own_ref), channel_id=1, source_target_pairs={{0,16},{4,20},{8,24},{12,28},{16,0},{20,4},{24,8},{28,12},{1,17},{... | collective-permute-start | bytes 196616 | tf_op jit(solution)/shard_map/item_cg/ppermute | solution.py:293
  83.1 27.0 %collective-permute-start.25 = (f32[128,128]{1,0:T(8,128)S(1)}, f32[128,128]{1,0:T(8,128)S(1)}, u32[]{:S(2)}, u32[]{:S(2)}) collective-permute-start(f32[128,128]{1,0:T(8,128)S(1)} %get-tuple-element.94), channel_id=1, source_target_pairs={{0,1},{1,0},{2,3},{3,2},{4,5},{5,4},{6,7},{7,6},{8,9},{9,8},{10,11... | collective-permute-start | bytes 196616 | tf_op jit(solution)/shard_map/user_cg/ppermute | solution.py:293
  83.1 8.3 %collective-permute-start.33 = (f32[128,128]{1,0:T(8,128)S(1)}, f32[128,128]{1,0:T(8,128)S(1)}, u32[]{:S(2)}, u32[]{:S(2)}) collective-permute-start(f32[128,128]{1,0:T(8,128)S(1)} %get-tuple-element.103.own_ref), channel_id=1, source_target_pairs={{0,16},{4,20},{8,24},{12,28},{16,0},{20,4},{24,8},{28,12},{1,17},{... | collective-permute-start | bytes 196616 | tf_op jit(solution)/shard_map/item_cg/ppermute | solution.py:293
  91.3 6.1 %collective-permute-start.38 = (f32[128,128]{1,0:T(8,128)S(1)}, f32[128,128]{1,0:T(8,128)S(1)}, u32[]{:S(2)}, u32[]{:S(2)}) collective-permute-start(f32[128,128]{1,0:T(8,128)S(1)} %get-tuple-element.118.own_ref), channel_id=1, source_target_pairs={{0,16},{4,20},{8,24},{12,28},{16,0},{20,4},{24,8},{28,12},{1,17},{... | collective-permute-start | bytes 196616 | tf_op jit(solution)/shard_map/item_cg/ppermute | solution.py:293
  92.9 6.2 %collective-permute-start.34 = (f32[128,128]{1,0:T(8,128)S(1)}, f32[128,128]{1,0:T(8,128)S(1)}, u32[]{:S(2)}, u32[]{:S(2)}) collective-permute-start(f32[128,128]{1,0:T(8,128)S(1)} %get-tuple-element.107.own_ref), channel_id=1, source_target_pairs={{0,16},{4,20},{8,24},{12,28},{16,0},{20,4},{24,8},{28,12},{1,17},{... | collective-permute-start | bytes 196616 | tf_op jit(solution)/shard_map/item_cg/ppermute | solution.py:293
  99.1 5.8 %collective-permute-start.39 = (f32[128,128]{1,0:T(8,128)S(1)}, f32[128,128]{1,0:T(8,128)S(1)}, u32[]{:S(2)}, u32[]{:S(2)}) collective-permute-start(f32[128,128]{1,0:T(8,128)S(1)} %get-tuple-element.122.own_ref), channel_id=1, source_target_pairs={{0,16},{4,20},{8,24},{12,28},{16,0},{20,4},{24,8},{28,12},{1,17},{... | collective-permute-start | bytes 196616 | tf_op jit(solution)/shard_map/item_cg/ppermute | solution.py:293
  100.9 5.9 %collective-permute-start.35 = (f32[128,128]{1,0:T(8,128)S(1)}, f32[128,128]{1,0:T(8,128)S(1)}, u32[]{:S(2)}, u32[]{:S(2)}) collective-permute-start(f32[128,128]{1,0:T(8,128)S(1)} %get-tuple-element.111.own_ref), channel_id=1, source_target_pairs={{0,16},{4,20},{8,24},{12,28},{16,0},{20,4},{24,8},{28,12},{1,17},{... | collective-permute-start | bytes 196616 | tf_op jit(solution)/shard_map/item_cg/ppermute | solution.py:293
  105.8 4.9 %collective-permute-start.40 = (f32[8,128]{1,0:T(8,128)S(1)}, f32[8,128]{1,0:T(8,128)S(1)}, u32[]{:S(2)}, u32[]{:S(2)}) collective-permute-start(f32[8,128]{1,0:T(8,128)S(1)} %get-tuple-element.126.refs_8_), channel_id=1, source_target_pairs={{0,16},{4,20},{8,24},{12,28},{16,0},{20,4},{24,8},{28,12},{1,17},{... | collective-permute-start | bytes 12296 | tf_op jit(solution)/shard_map/item_cg/ppermute | solution.py:293
  107.8 4.6 %collective-permute-start.36 = (f32[8,128]{1,0:T(8,128)S(1)}, f32[8,128]{1,0:T(8,128)S(1)}, u32[]{:S(2)}, u32[]{:S(2)}) collective-permute-start(f32[8,128]{1,0:T(8,128)S(1)} %get-tuple-element.115.refs_3_), channel_id=1, source_target_pairs={{0,16},{4,20},{8,24},{12,28},{16,0},{20,4},{24,8},{28,12},{1,17},{... | collective-permute-start | bytes 12296 | tf_op jit(solution)/shard_map/item_cg/ppermute | solution.py:293
  (18 other events, 73.1 us)

commit v4 on v3

--- a/solution.py
+++ b/solution.py
@@ -93,51 +93,75 @@
     return solution, residual, direction
 
 
-def pack_kernel(slots, ids_ref, conf_ref, given_ref, send_ref):
+def pack_kernel(slots, ids_ref, conf_ref, named_ref, given_ref, send_ref, held, in_sems, sems):
     slot_total, block, _ = conf_ref.shape
     half = block // 2
     owners = slot_total // slots
     near = owners // 2
     core = lax.rem(lax.axis_index("item"), 2)
-    shift = ids_ref[slot_total]
-    count = ids_ref[2 * slot_total]
-    given_ref[...] = conf_ref[:, pl.ds(pl.multiple_of((1 - core) * half, half), half), :]
-    for owner in range(owners):
-        first = lax.rem(owner - shift + owners, owners)
-        for slot in range(slots):
-            place = first + owners * slot
-            used = place < jnp.minimum(count, slot_total)
-            send_ref[owner % near, owner // near * slots + slot] = jnp.where(used, conf_ref[place], 0)
-
-
-def user_tiles_kernel(weight_zero, own_ids, other_ids, conf_ref, half_ref, dense_ref, weight_ref):
+    taken = [
+        pltpu.make_async_copy(conf_ref.at[slot], held.at[slot], in_sems.at[slot]) for slot in range(slot_total)
+    ]
+    for copy in taken:
+        copy.start()
+    copies = []
+    for owner in range(near):
+        target = send_ref.at[owner, 2 * slots * block :, :]
+        copies.append(pltpu.make_async_copy(named_ref, target, sems.at[len(copies)]))
+        copies[-1].start()
+    for slot in range(slot_total):
+        owner = lax.rem(ids_ref[1, 0] + slot, owners)
+        start = pl.multiple_of((owner // near * slots + slot // owners) * block, block)
+        target = send_ref.at[lax.rem(owner, near), pl.ds(start, block), :]
+        taken[slot].wait()
+        copies.append(pltpu.make_async_copy(held.at[slot], target, sems.at[len(copies)]))
+        copies[-1].start()
+    rows = pl.ds(pl.multiple_of((1 - core) * half, half), half)
+    copies.append(pltpu.make_async_copy(held.at[:, rows, :], given_ref, sems.at[len(copies)]))
+    copies[-1].start()
+    for copy in copies:
+        copy.wait()
+
+
+def user_tile(named_ref, slot, base, counts, dense_ref, weight_ref):
+    half, block = counts.shape
+    owners = dense_ref.shape[1] // block // 2
+    owner = lax.rem(named_ref[1, 0] + slot, owners)
+    row = pl.multiple_of(named_ref[0, slot] * half, half)
+    col = pl.multiple_of((base + jnp.bitwise_xor(owner, lax.axis_index("user"))) * block, block)
+    at = (pl.ds(row, half), pl.ds(col, block))
+    value = counts.astype(f32)
+    dense_ref[at] = dense_ref[at] + value
+    weight_ref[at] = weight_ref[at] + jnp.where(value > 0.0, 1.0 + value, 0.0).astype(bf16)
+
+
+def own_tiles_kernel(weight_zero, named_ref, conf_ref, dense_ref, weight_ref, held, sem):
     slot_total, block, _ = conf_ref.shape
     half = block // 2
-    owners = dense_ref.shape[1] // block // 2
-    me = lax.axis_index("user")
     core = lax.rem(lax.axis_index("item"), 2)
+    rows = pl.ds(pl.multiple_of(core * half, half), half)
+    copy = pltpu.make_async_copy(conf_ref.at[:, rows, :], held, sem)
+    copy.start()
     dense_ref[...] = jnp.full(dense_ref.shape, weight_zero, f32)
     weight_ref[...] = jnp.zeros(weight_ref.shape, bf16)
-
-    def place(ids, slot, base, counts):
-        row = pl.multiple_of(ids[slot] * half, half)
-        col = pl.multiple_of((base + jnp.bitwise_xor(ids[slot_total + slot], me)) * block, block)
-        at = (pl.ds(row, half), pl.ds(col, block))
-        value = counts.astype(f32)
-        dense_ref[at] = dense_ref[at] + value
-        weight_ref[at] = weight_ref[at] + jnp.where(value > 0.0, 1.0 + value, 0.0).astype(bf16)
-
-    def own(slot, carry):
-        rows = pl.ds(pl.multiple_of(core * half, half), half)
-        place(own_ids, slot, 0, conf_ref[slot, rows, :])
+    copy.wait()
+
+    def one(slot, carry):
+        user_tile(named_ref, slot, 0, held[slot], dense_ref, weight_ref)
         return carry
 
-    def other(slot, carry):
-        place(other_ids, slot, owners, half_ref[slot])
+    lax.fori_loop(0, jnp.minimum(named_ref[1, 1], slot_total), one, 0)
+
+
+def other_tiles_kernel(named_ref, half_ref, dense_in, weight_in, dense_ref, weight_ref):
+    slot_total, _, block = half_ref.shape
+    owners = dense_ref.shape[1] // block // 2
+
+    def one(slot, carry):
+        user_tile(named_ref, slot, owners, half_ref[slot], dense_ref, weight_ref)
         return carry
 
-    lax.fori_loop(0, jnp.minimum(own_ids[2 * slot_total], slot_total), own, 0)
-    lax.fori_loop(0, jnp.minimum(other_ids[2 * slot_total], slot_total), other, 0)
+    lax.fori_loop(0, jnp.minimum(named_ref[1, 1], slot_total), one, 0)
 
 
 def user_side_kernel(count, *refs):
@@ -207,19 +231,23 @@
     give_ref[...] = out_ref[pl.ds(pl.multiple_of(other * rows, rows), rows), :]
 
 
-def item_tiles_kernel(weight_zero, row_blocks, lists_ref, tiles_ref, dense_ref, weight_ref):
-    near, count, block, _ = tiles_ref.shape
-    slots = count // 2
+def item_tiles_kernel(weight_zero, row_blocks, slots, lists_ref, tiles_ref, dense_ref, weight_ref):
+    near = tiles_ref.shape[0]
+    block = tiles_ref.shape[2]
     me = lax.rem(lax.axis_index("user"), near)
     dense_ref[...] = jnp.full(dense_ref.shape, weight_zero, f32)
     weight_ref[...] = jnp.zeros(weight_ref.shape, bf16)
     for source in range(near):
         mask = jnp.bitwise_xor(source, me)
         for upper in range(2):
-            first = lax.rem(me + upper * near - lists_ref[mask, 1, 0] + 2 * near, 2 * near)
+            first = lax.rem(me + upper * near - lists_ref[source, 1, 0] + 2 * near, 2 * near)
             for slot in range(slots):
-                value = jnp.transpose(tiles_ref[source, upper * slots + slot].astype(f32))
-                row = lists_ref[mask, 0, first + 2 * near * slot]
+                start = (upper * slots + slot) * block
+                place = first + 2 * near * slot
+                used = place < lists_ref[source, 1, 1]
+                tile = jnp.where(used, tiles_ref[source, start : start + block, :], 0)
+                value = jnp.transpose(tile.astype(f32))
+                row = lists_ref[source, 0, place]
                 col = pl.multiple_of((mask * row_blocks + row) * block, block)
                 at = (slice(upper * block, (upper + 1) * block), pl.ds(col, block))
                 dense_ref[at] = dense_ref[at] + value
@@ -260,16 +288,17 @@
 SMEM = pltpu.SMEM
 
 
-def call(kernel, outs, *operands, scalars=0, flops=0, scratch=(), limit=16):
+def call(kernel, outs, *operands, scalars=0, far=0, far_outs=0, flops=0, scratch=(), limit=16, aliases=None):
     size = sum(op.size * op.dtype.itemsize for op in operands)
     size += sum(4 * math.prod(out.shape) for out in outs)
-    spaces = [SMEM] * scalars + [VMEM] * (len(operands) - scalars)
+    spaces = [SMEM] * scalars + [pl.ANY] * far + [VMEM] * (len(operands) - scalars - far)
     return pl.pallas_call(
         kernel,
         out_shape=tuple(outs),
         in_specs=[pl.BlockSpec(memory_space=space) for space in spaces],
-        out_specs=tuple(pl.BlockSpec(memory_space=VMEM) for unused in outs),
+        out_specs=tuple(pl.BlockSpec(memory_space=pl.ANY if place < far_outs else VMEM) for place in range(len(outs))),
         scratch_shapes=scratch,
+        input_output_aliases=aliases or {},
         compiler_params=pltpu.CompilerParams(vmem_limit_bytes=limit * MIB),
         cost_estimate=pl.CostEstimate(flops=flops, bytes_accessed=size, transcendentals=0),
     )(*operands)
@@ -303,38 +332,43 @@
             mask *= 2
 
     conf = conf.reshape(slot_total, block, block)
-    ids = jnp.concatenate(
-        [tile_rows.reshape(-1), tile_cols.reshape(-1), tile_count.reshape(-1)]
-    ).astype(jnp.int32)
-
     def after(value, *tokens):
         return lax.optimization_barrier((value, *tokens))[0]
 
-    named = jnp.concatenate([tile_rows.reshape(1, -1), tile_cols.reshape(1, -1)])
-    named = jnp.pad(named.astype(f32), ((0, 6), (0, rank - slot_total)))
-    sent = jnp.concatenate([item_init, named], axis=0)
+    named = sum(
+        jnp.pad(value.reshape(1, -1), ((row, 7 - row), (lane, rank - lane - size)))
+        for value, row, lane, size in (
+            (tile_rows, 0, 0, slot_total), (tile_cols[..., :1], 1, 0, 1), (tile_count, 1, 1, 1)
+        )
+    )
     near = n_user // 2
     with jax.named_scope("gather_items"):
-        pieces = {0: sent}
+        pieces = {0: item_init}
         for mask in (6, 4, 2, 1):
-            pieces[mask] = swap(sent, "user", mask)
+            pieces[mask] = swap(item_init, "user", mask)
 
     with jax.named_scope("gather_items"):
         for mask in (2, 6, 4):
-            pieces[mask + 1] = swap(pieces[mask], "user", 1)
+            pieces[mask + 1] = swap(after(pieces[mask], named), "user", 1)
         own_items = [pieces[mask] for mask in range(n_user)]
         other_items = [swap(piece, "item", 1) for piece in own_items]
 
     with jax.named_scope("pack_tiles"):
+        far_conf = pltpu.with_memory_space_constraint(conf, pltpu.HBM)
         given, packed = call(
             functools.partial(pack_kernel, slots),
             (
                 pltpu.HBM((slot_total, half, block), jnp.int32),
-                pltpu.HBM((near, 2 * slots, block, block), jnp.int32),
+                pltpu.HBM((near, 2 * slots * block + 8, block), jnp.int32),
             ),
-            after(ids, pieces[3]), conf, scalars=1, flops=10 ** 9,
-        )
-        other_ids = swap(ids, "item", 1)
+            after(named, pieces[3]), far_conf, named, scalars=1, far=1, far_outs=2, limit=16,
+            scratch=(
+                pltpu.VMEM(conf.shape, jnp.int32),
+                pltpu.SemaphoreType.DMA((slot_total,)),
+                pltpu.SemaphoreType.DMA((slot_total + 1 + near,)),
+            ),
+        )
+        other_named = swap(named, "item", 1)
         other_half = swap(given, "item", 1)
 
     with jax.named_scope("send_tiles"):
@@ -342,14 +376,19 @@
         tiles = lax.all_to_all(
             after(packed, *own_items), "user", 0, 0, tiled=True, axis_index_groups=halves
         )
-        ids = after(ids, *own_items)
+        own_named = after(named, *own_items)
 
     with jax.named_scope("user_tiles"):
         columns = 2 * n_user * block
+        dense = (shaped((rows, columns)), shaped((rows, columns), bf16))
         user_conf, user_weight = call(
-            functools.partial(user_tiles_kernel, unobserved / (item_init.shape[0] * n_user * n_item)),
-            (shaped((rows, columns)), shaped((rows, columns), bf16)),
-            ids, other_ids, conf, other_half, scalars=2, flops=10 ** 9,
+            functools.partial(own_tiles_kernel, unobserved / (item_init.shape[0] * n_user * n_item)),
+            dense, own_named, far_conf, scalars=1, far=1, flops=10 ** 9,
+            scratch=(pltpu.VMEM((slot_total, half, block), jnp.int32), pltpu.SemaphoreType.DMA(())),
+        )
+        user_conf, user_weight = call(
+            other_tiles_kernel, dense, other_named, other_half, user_conf, user_weight,
+            scalars=1, flops=10 ** 9, aliases={2: 0, 3: 1},
         )
 
     def iterate(sides, confidence, pairs, both):
@@ -395,11 +434,11 @@
         found = [users, swap(users, "user", 1), swap(users, "user", 2)]
 
     with jax.named_scope("item_tiles"):
-        lists = jnp.stack([pieces[mask][block : block + 2] for mask in range(near)]).astype(jnp.int32)
+        lists = tiles[:, 2 * slots * block : 2 * slots * block + 2]
         columns = near * row_blocks * block
         item_conf, item_weight = call(
             functools.partial(
-                item_tiles_kernel, unobserved / (user_factors.shape[0] * n_user * n_item), row_blocks
+                item_tiles_kernel, unobserved / (user_factors.shape[0] * n_user * n_item), row_blocks, slots
             ),
             (shaped((2 * block, columns)), shaped((2 * block, columns), bf16)),
             lists, tiles, scalars=1, flops=10 ** 9,

time: 114 us -> 112 us (0.982)
  Pallas kernels: 30.6 us -> 33.2 us
  waiting for transfers between devices: 32.9 us -> 30.9 us
  local copies, waits for them, and re-layouts: 3.16 us -> 1.93 us
    pallas_call x20 -> x21, Pallas kernels: 30.6 us -> 33.2 us  [call(): pl.pallas_call(kernel, out_shape=tuple(outs), in_specs=[pl.BlockSpec(memo...]
    ppermute x41, waiting for transfers between devices: 32.9 us -> 30.9 us  [swap(): lax.ppermute(value, axis, [(place, place ^ mask) for place in range(size)])]
    concatenate x2 -> x0, other arithmetic: 1.59 us -> none  [the longest x1 0.85 us: dense_shards(): sent = jnp.concatenate([item_init, named], axis=0)]
    add x0 -> x1, other arithmetic: none -> 1.38 us  [dense_shards(): sum((jnp.pad(value.reshape(1, -1), ((row, 7 - row), (lane, rank - lane -...]
    unnamed x16 -> x14, local copies, waits for them, and re-layouts: 3.15 us -> 1.93 us
  transfers between devices with their start and end apart: 42 -> 42, of which waited for: 16 -> 18; matrix products, arithmetic and copies ran while one was open for 1% -> 1% of each run, Pallas kernels for 25% -> 28%
where the time goes in v4:
time: 112 us; the launch traced here: 111 us
  starting transfers between devices  41.9 us (37%)
  Pallas kernels  33.2 us (30%)
  waiting for transfers between devices  30.9 us (28%)
  local copies, waits for them, and re-layouts  1.93 us (2%)
  between operations  1.55 us (1%)
  other arithmetic  1.38 us (1%)
    ppermute x41, starting transfers between devices, swap(): lax.ppermute(value, axis, [(place, place ^ mask) for place in range(size)])  38.1 us
    pallas_call x21, Pallas kernels, call(): pl.pallas_call(kernel, out_shape=tuple(outs), in_specs=[pl.BlockSpec(memo...  33.2 us
    ppermute x41, waiting for transfers between devices, swap(): lax.ppermute(value, axis, [(place, place ^ mask) for place in range(size)])  30.9 us
    all_to_all x1, starting transfers between devices, dense_shards(): lax.all_to_all(after(packed, *own_items), 'user', 0, 0, tiled=True, axis_...  3.83 us
  transfers between devices with their start and end apart: 42, of which 18 were waited for; matrix products, arithmetic and copies ran while one was open for 1% of the time, Pallas kernels for 28%

profile of v4, /device:TPU:0, one launch (start us, length us, event | category | flops | bytes accessed | tf_op | source)
XLA Modules:
  0.0 110.9 jit_solution(11947148012737682651)
XLA Ops:
  0.6 3.1 %collective-permute-start.1 = (f32[128,128]{1,0:T(8,128)}, f32[128,128]{1,0:T(8,128)S(1)}, u32[]{:S(2)}, u32[]{:S(2)}) collective-permute-start(f32[128,128]{1,0:T(8,128)} %refs_0_.1), channel_id=1, source_target_pairs={{0,8},{4,12},{8,0},{12,4},{16,24},{20,28},{24,16},{28,20},{1,9},{5... | collective-permute-start | bytes 196616 | tf_op jit(solution)/shard_map/gather_items/ppermute | solution.py:322
  3.7 2.6 %collective-permute-start.3 = (f32[128,128]{1,0:T(8,128)}, f32[128,128]{1,0:T(8,128)S(1)}, u32[]{:S(2)}, u32[]{:S(2)}) collective-permute-start(f32[128,128]{1,0:T(8,128)} %refs_0_.1), channel_id=1, source_target_pairs={{0,16},{4,20},{8,24},{12,28},{16,0},{20,4},{24,8},{28,12},{1,17},{... | collective-permute-start | bytes 196616 | tf_op jit(solution)/shard_map/gather_items/ppermute | solution.py:322
  6.3 1.7 %collective-permute-start = (f32[128,128]{1,0:T(8,128)}, f32[128,128]{1,0:T(8,128)S(1)}, u32[]{:S(2)}, u32[]{:S(2)}) collective-permute-start(f32[128,128]{1,0:T(8,128)} %refs_0_.1), channel_id=1, source_target_pairs={{0,4},{4,0},{8,12},{12,8},{16,20},{20,16},{24,28},{28,24},{1,5},{5... | collective-permute-start | bytes 196616 | tf_op jit(solution)/shard_map/gather_items/ppermute | solution.py:322
  11.2 1.5 %collective-permute-start.4 = (f32[128,128]{1,0:T(8,128)S(1)}, f32[128,128]{1,0:T(8,128)S(1)}, u32[]{:S(2)}, u32[]{:S(2)}) collective-permute-start(f32[128,128]{1,0:T(8,128)S(1)} %collective-permute-done.3.refs_4_), channel_id=1, source_target_pairs={{0,4},{4,0},{8,12},{12,8},{16,20},{20,16},{24,28},{28,24},{1,5},{5... | collective-permute-start | bytes 196616 | tf_op jit(solution)/shard_map/gather_items/ppermute | solution.py:322
  14.8 5.0 %pack_tiles.1 = (s32[48,64,128]{2,1,0:T(8,128)}, s32[4,1544,128]{2,1,0:T(8,128)}) custom-call(s32[8,128]{1,0:T(8,128)S(1)} %pad_add_fusion.ids_ref.named_ref, s32[48,128,128]{2,1,0:T(8,128)} %bitcast.4, s32[8,128]{1,0:T(8,128)S(1)} %pad_add_fusion.ids_ref.named_ref), custom_call_target="tpu_custom_call" | custom-call | bytes 7888896 | tf_op jit(solution)/shard_map/pack_tiles/pallas_call | solution.py:295
  21.1 3.8 %all-to-all-start = ((s32[4,1544,128]{2,1,0:T(8,128)}), s32[4,1544,128]{2,1,0:T(8,128)S(1)}, u32[]{:S(2)}, u32[]{:S(2)}) async-start(s32[4,1544,128]{2,1,0:T(8,128)} %get-tuple-element.107), calls=%async_computation | async-start | bytes 6324224 | tf_op jit(solution)/shard_map/send_tiles/all_to_all | solution.py:376
  26.8 3.1 %user_tiles.2 = (f32[512,2048]{1,0:T(8,128)S(1)}, bf16[512,2048]{1,0:T(8,128)(2,1)S(1)}) custom-call(s32[8,128]{1,0:T(8,128)S(1)} %copy-done.6, s32[48,128,128]{2,1,0:T(8,128)} %bitcast.5), custom_call_target="tpu_custom_call" | custom-call | flops 1000000000 | bytes 11538432 | tf_op jit(solution)/shard_map/user_tiles/pallas_call | solution.py:295
  31.5 1.6 %user_tiles.3 = (f32[512,2048]{1,0:T(8,128)S(1)}, bf16[512,2048]{1,0:T(8,128)(2,1)S(1)}) custom-call(s32[8,128]{1,0:T(8,128)S(1)} %collective-permute-done.15.named_ref, s32[48,64,128]{2,1,0:T(8,128)S(1)} %collective-permute-done.16.half_ref, f32[512,2048]{1,0:T(8,128)S(1)} %get-tuple-element.76.dense_in, ...), custom_call_target="tpu_custom_call", output_to_operand_aliasing={{0}: (2, {}), {1}: (3, {})} | custom-call | flops 1000000000 | bytes 16257024 | tf_op jit(solution)/shard_map/user_tiles/pallas_call | solution.py:295
  33.9 2.1 %collective-permute-start.21 = (f32[256,128]{1,0:T(8,128)S(1)}, f32[256,128]{1,0:T(8,128)S(1)}, u32[]{:S(2)}, u32[]{:S(2)}) collective-permute-start(f32[256,128]{1,0:T(8,128)S(1)} %get-tuple-element.92.own_ref), channel_id=1, source_target_pairs={{0,2},{1,3},{2,0},{3,1},{4,6},{5,7},{6,4},{7,5},{8,10},{9,11},{10,... | collective-permute-start | bytes 393224 | tf_op jit(solution)/shard_map/user_cg/ppermute | solution.py:322
  36.1 4.3 %collective-permute-done.21.other_ref = f32[256,128]{1,0:T(8,128)S(1)} collective-permute-done((f32[256,128]{1,0:T(8,128)S(1)}, f32[256,128]{1,0:T(8,128)S(1)}, u32[]{:S(2)}, u32[]{:S(2)}) %collective-permute-start.21) | collective-permute-done | bytes 131104 | tf_op jit(solution)/shard_map/user_cg/ppermute | solution.py:322
  40.4 1.6 %user_cg.13 = (f32[256,128]{1,0:T(8,128)S(1)}, f32[256,128]{1,0:T(8,128)S(1)}) custom-call(f32[256,128]{1,0:T(8,128)S(1)} %get-tuple-element.92.own_ref, f32[256,128]{1,0:T(8,128)S(1)} %collective-permute-done.21.other_ref, f32[512,2048]{1,0:T(8,128)S(1)} %get-tuple-element.80.conf_ref, bf16[2048,256]{1,0:T(8,128)(2,1)S(1)} %get-tuple-element.81.pairs_ref), custom_call_target="tpu_custom_call" | custom-call | flops 805306368 | bytes 5767168 | tf_op jit(solution)/shard_map/user_cg/pallas_call | solution.py:295
  42.0 2.1 %collective-permute-start.22 = (f32[256,128]{1,0:T(8,128)S(1)}, f32[256,128]{1,0:T(8,128)S(1)}, u32[]{:S(2)}, u32[]{:S(2)}) collective-permute-start(f32[256,128]{1,0:T(8,128)S(1)} %get-tuple-element.94.own_ref), channel_id=1, source_target_pairs={{0,2},{1,3},{2,0},{3,1},{4,6},{5,7},{6,4},{7,5},{8,10},{9,11},{10,... | collective-permute-start | bytes 393224 | tf_op jit(solution)/shard_map/user_cg/ppermute | solution.py:322
  44.2 1.6 %user_cg.10 = (f32[256,128]{1,0:T(8,128)S(1)}, f32[256,128]{1,0:T(8,128)S(1)}) custom-call(f32[256,128]{1,0:T(8,128)S(1)} %get-tuple-element.79.own_ref, f32[256,128]{1,0:T(8,128)S(1)} %collective-permute-done.17.other_ref, f32[512,2048]{1,0:T(8,128)S(1)} %get-tuple-element.80.conf_ref, bf16[2048,256]{1,0:T(8,128)(2,1)S(1)} %get-tuple-element.81.pairs_ref), custom_call_target="tpu_custom_call" | custom-call | flops 805306368 | bytes 5767168 | tf_op jit(solution)/shard_map/user_cg/pallas_call | solution.py:295
  45.9 2.6 %collective-permute-done.22.other_ref = f32[256,128]{1,0:T(8,128)S(1)} collective-permute-done((f32[256,128]{1,0:T(8,128)S(1)}, f32[256,128]{1,0:T(8,128)S(1)}, u32[]{:S(2)}, u32[]{:S(2)}) %collective-permute-start.22) | collective-permute-done | bytes 131104 | tf_op jit(solution)/shard_map/user_cg/ppermute | solution.py:322
  48.5 1.8 %user_cg.14 = (f32[256,128]{1,0:T(8,128)S(1)}, f32[256,128]{1,0:T(8,128)S(1)}, f32[256,128]{1,0:T(8,128)S(1)}, f32[256,128]{1,0:T(8,128)S(1)}) custom-call(f32[256,128]{1,0:T(8,128)S(1)} %get-tuple-element.93.side_ref, f32[256,128]{1,0:T(8,128)S(1)} %get-tuple-element.94.own_ref, f32[256,128]{1,0:T(8,128)S(1)} %collective-permute-done.22.other_ref, ...), custom_call_target="tpu_custom_call" | custom-call | flops 805306368 | bytes 6160384 | tf_op jit(solution)/shard_map/user_cg/pallas_call | solution.py:295
  51.6 1.8 %user_cg.11 = (f32[256,128]{1,0:T(8,128)S(1)}, f32[256,128]{1,0:T(8,128)S(1)}, f32[256,128]{1,0:T(8,128)S(1)}, f32[256,128]{1,0:T(8,128)S(1)}) custom-call(f32[256,128]{1,0:T(8,128)S(1)} %get-tuple-element.82.side_ref, f32[256,128]{1,0:T(8,128)S(1)} %get-tuple-element.83.own_ref, f32[256,128]{1,0:T(8,128)S(1)} %collective-permute-done.18.other_ref, ...), custom_call_target="tpu_custom_call" | custom-call | flops 805306368 | bytes 6160384 | tf_op jit(solution)/shard_map/user_cg/pallas_call | solution.py:295
  54.2 1.7 %collective-permute-done.23.other_ref = f32[256,128]{1,0:T(8,128)S(1)} collective-permute-done((f32[256,128]{1,0:T(8,128)S(1)}, f32[256,128]{1,0:T(8,128)S(1)}, u32[]{:S(2)}, u32[]{:S(2)}) %collective-permute-start.23) | collective-permute-done | bytes 131104 | tf_op jit(solution)/shard_map/user_cg/ppermute | solution.py:322
  60.6 2.5 %collective-permute-done.20.refs_4_ = f32[8,256]{1,0:T(8,128)S(1)} collective-permute-done((f32[8,256]{1,0:T(8,128)S(1)}, f32[8,256]{1,0:T(8,128)S(1)}, u32[]{:S(2)}, u32[]{:S(2)}) %collective-permute-start.20) | collective-permute-done | bytes 8224 | tf_op jit(solution)/shard_map/user_cg/ppermute | solution.py:322
  63.6 2.0 %collective-permute-start.29 = (f32[512,128]{1,0:T(8,128)S(1)}, f32[512,128]{1,0:T(8,128)S(1)}, u32[]{:S(2)}, u32[]{:S(2)}) collective-permute-start(f32[512,128]{1,0:T(8,128)S(1)} %get-tuple-element.108.refs_0_), channel_id=1, source_target_pairs={{0,8},{4,12},{8,0},{12,4},{16,24},{20,28},{24,16},{28,20},{1,9},{5... | collective-permute-start | bytes 786440 | tf_op jit(solution)/shard_map/gather_users/ppermute | solution.py:322
  67.1 2.3 %item_tiles.1 = (f32[256,4096]{1,0:T(8,128)S(1)}, bf16[256,4096]{1,0:T(8,128)(2,1)S(1)}) custom-call(s32[4,2,128]{2,1,0:T(2,128)S(1)} %slice.7.lists_ref, s32[4,1544,128]{2,1,0:T(8,128)S(1)} %all-to-all-done.tiles_ref), custom_call_target="tpu_custom_call" | custom-call | flops 1000000000 | bytes 11554816 | tf_op jit(solution)/shard_map/item_tiles/pallas_call | solution.py:295
  72.9 3.5 %collective-permute-done.31.refs_6_ = f32[512,128]{1,0:T(8,128)S(1)} collective-permute-done((f32[512,128]{1,0:T(8,128)S(1)}, f32[512,128]{1,0:T(8,128)S(1)}, u32[]{:S(2)}, u32[]{:S(2)}) %collective-permute-start.31) | collective-permute-done | bytes 262176 | tf_op jit(solution)/shard_map/gather_users/ppermute | solution.py:322
  76.4 1.5 %collective-permute-done.32.refs_7_ = f32[512,128]{1,0:T(8,128)S(1)} collective-permute-done((f32[512,128]{1,0:T(8,128)S(1)}, f32[512,128]{1,0:T(8,128)S(1)}, u32[]{:S(2)}, u32[]{:S(2)}) %collective-permute-start.32) | collective-permute-done | bytes 262176 | tf_op jit(solution)/shard_map/gather_users/ppermute | solution.py:322
  78.9 2.8 %collective-permute-start.37 = (f32[128,128]{1,0:T(8,128)S(1)}, f32[128,128]{1,0:T(8,128)S(1)}, u32[]{:S(2)}, u32[]{:S(2)}) collective-permute-start(f32[128,128]{1,0:T(8,128)S(1)} %get-tuple-element.126.own_ref), channel_id=1, source_target_pairs={{0,16},{4,20},{8,24},{12,28},{16,0},{20,4},{24,8},{28,12},{1,17},{... | collective-permute-start | bytes 196616 | tf_op jit(solution)/shard_map/item_cg/ppermute | solution.py:322
  81.9 2.9 %collective-permute-done.37.other_ref = f32[128,128]{1,0:T(8,128)S(1)} collective-permute-done((f32[128,128]{1,0:T(8,128)S(1)}, f32[128,128]{1,0:T(8,128)S(1)}, u32[]{:S(2)}, u32[]{:S(2)}) %collective-permute-start.37) | collective-permute-done | bytes 65568 | tf_op jit(solution)/shard_map/item_cg/ppermute | solution.py:322
  84.8 1.8 %item_cg.12 = (f32[128,128]{1,0:T(8,128)S(1)}, f32[128,128]{1,0:T(8,128)S(1)}) custom-call(f32[128,128]{1,0:T(8,128)S(1)} %get-tuple-element.126.own_ref, f32[128,128]{1,0:T(8,128)S(1)} %collective-permute-done.37.other_ref, f32[256,4096]{1,0:T(8,128)S(1)} %get-tuple-element.114.conf_ref, bf16[4096,256]{1,0:T(8,128)(2,1)S(1)} %get-tuple-element.115.pairs_ref), custom_call_target="tpu_custom_call" | custom-call | flops 805306368 | bytes 6553600 | tf_op jit(solution)/shard_map/item_cg/pallas_call | solution.py:295
  86.6 2.8 %collective-permute-start.38 = (f32[128,128]{1,0:T(8,128)S(1)}, f32[128,128]{1,0:T(8,128)S(1)}, u32[]{:S(2)}, u32[]{:S(2)}) collective-permute-start(f32[128,128]{1,0:T(8,128)S(1)} %get-tuple-element.128.own_ref), channel_id=1, source_target_pairs={{0,16},{4,20},{8,24},{12,28},{16,0},{20,4},{24,8},{28,12},{1,17},{... | collective-permute-start | bytes 196616 | tf_op jit(solution)/shard_map/item_cg/ppermute | solution.py:322
  89.4 1.6 %item_cg.9 = (f32[128,128]{1,0:T(8,128)S(1)}, f32[128,128]{1,0:T(8,128)S(1)}) custom-call(f32[128,128]{1,0:T(8,128)S(1)} %get-tuple-element.113.own_ref, f32[128,128]{1,0:T(8,128)S(1)} %collective-permute-done.33.other_ref, f32[256,4096]{1,0:T(8,128)S(1)} %get-tuple-element.114.conf_ref, bf16[4096,256]{1,0:T(8,128)(2,1)S(1)} %get-tuple-element.115.pairs_ref), custom_call_target="tpu_custom_call" | custom-call | flops 805306368 | bytes 6553600 | tf_op jit(solution)/shard_map/item_cg/pallas_call | solution.py:295
  91.8 1.7 %item_cg.13 = (f32[128,128]{1,0:T(8,128)S(1)}, f32[128,128]{1,0:T(8,128)S(1)}, f32[128,128]{1,0:T(8,128)S(1)}, f32[128,128]{1,0:T(8,128)S(1)}) custom-call(f32[128,128]{1,0:T(8,128)S(1)} %get-tuple-element.127.side_ref, f32[128,128]{1,0:T(8,128)S(1)} %get-tuple-element.128.own_ref, f32[128,128]{1,0:T(8,128)S(1)} %collective-permute-done.38.other_ref, ...), custom_call_target="tpu_custom_call" | custom-call | flops 805306368 | bytes 6750208 | tf_op jit(solution)/shard_map/item_cg/pallas_call | solution.py:295
  93.5 3.3 %collective-permute-start.39 = (f32[128,128]{1,0:T(8,128)S(1)}, f32[128,128]{1,0:T(8,128)S(1)}, u32[]{:S(2)}, u32[]{:S(2)}) collective-permute-start(f32[128,128]{1,0:T(8,128)S(1)} %get-tuple-element.132.own_ref), channel_id=1, source_target_pairs={{0,16},{4,20},{8,24},{12,28},{16,0},{20,4},{24,8},{28,12},{1,17},{... | collective-permute-start | bytes 196616 | tf_op jit(solution)/shard_map/item_cg/ppermute | solution.py:322
  96.8 1.7 %item_cg.10 = (f32[128,128]{1,0:T(8,128)S(1)}, f32[128,128]{1,0:T(8,128)S(1)}, f32[128,128]{1,0:T(8,128)S(1)}, f32[128,128]{1,0:T(8,128)S(1)}) custom-call(f32[128,128]{1,0:T(8,128)S(1)} %get-tuple-element.116.side_ref, f32[128,128]{1,0:T(8,128)S(1)} %get-tuple-element.117.own_ref, f32[128,128]{1,0:T(8,128)S(1)} %collective-permute-done.34.other_ref, ...), custom_call_target="tpu_custom_call" | custom-call | flops 805306368 | bytes 6750208 | tf_op jit(solution)/shard_map/item_cg/pallas_call | solution.py:295
  98.6 2.1 %collective-permute-done.39.other_ref = f32[128,128]{1,0:T(8,128)S(1)} collective-permute-done((f32[128,128]{1,0:T(8,128)S(1)}, f32[128,128]{1,0:T(8,128)S(1)}, u32[]{:S(2)}, u32[]{:S(2)}) %collective-permute-start.39) | collective-permute-done | bytes 65568 | tf_op jit(solution)/shard_map/item_cg/ppermute | solution.py:322
  106.3 3.6 %collective-permute-done.36.refs_4_ = f32[8,128]{1,0:T(8,128)S(1)} collective-permute-done((f32[8,128]{1,0:T(8,128)S(1)}, f32[8,128]{1,0:T(8,128)S(1)}, u32[]{:S(2)}, u32[]{:S(2)}) %collective-permute-start.36) | collective-permute-done | bytes 4128 | tf_op jit(solution)/shard_map/item_cg/ppermute | solution.py:322
  (89 shorter events, 31.1 us)
Async XLA Ops:
  0.6 9.5 %collective-permute-start.1 = (f32[128,128]{1,0:T(8,128)}, f32[128,128]{1,0:T(8,128)S(1)}, u32[]{:S(2)}, u32[]{:S(2)}) collective-permute-start(f32[128,128]{1,0:T(8,128)} %refs_0_.1), channel_id=1, source_target_pairs={{0,8},{4,12},{8,0},{12,4},{16,24},{20,28},{24,16},{28,20},{1,9},{5... | collective-permute-start | bytes 196616 | tf_op jit(solution)/shard_map/gather_items/ppermute | solution.py:322
  3.7 7.5 %collective-permute-start.3 = (f32[128,128]{1,0:T(8,128)}, f32[128,128]{1,0:T(8,128)S(1)}, u32[]{:S(2)}, u32[]{:S(2)}) collective-permute-start(f32[128,128]{1,0:T(8,128)} %refs_0_.1), channel_id=1, source_target_pairs={{0,16},{4,20},{8,24},{12,28},{16,0},{20,4},{24,8},{28,12},{1,17},{... | collective-permute-start | bytes 196616 | tf_op jit(solution)/shard_map/gather_items/ppermute | solution.py:322
  6.3 6.4 %collective-permute-start.5 = (f32[128,128]{1,0:T(8,128)}, f32[128,128]{1,0:T(8,128)S(1)}, u32[]{:S(2)}, u32[]{:S(2)}) collective-permute-start(f32[128,128]{1,0:T(8,128)} %refs_0_.1), channel_id=1, source_target_pairs={{0,24},{4,28},{8,16},{12,20},{16,8},{20,12},{24,0},{28,4},{1,25},{... | collective-permute-start | bytes 196616 | tf_op jit(solution)/shard_map/gather_items/ppermute | solution.py:322
  6.3 13.5 %collective-permute-start = (f32[128,128]{1,0:T(8,128)}, f32[128,128]{1,0:T(8,128)S(1)}, u32[]{:S(2)}, u32[]{:S(2)}) collective-permute-start(f32[128,128]{1,0:T(8,128)} %refs_0_.1), channel_id=1, source_target_pairs={{0,4},{4,0},{8,12},{12,8},{16,20},{20,16},{24,28},{28,24},{1,5},{5... | collective-permute-start | bytes 196616 | tf_op jit(solution)/shard_map/gather_items/ppermute | solution.py:322
  10.1 4.7 %collective-permute-start.2 = (f32[128,128]{1,0:T(8,128)S(1)}, f32[128,128]{1,0:T(8,128)S(1)}, u32[]{:S(2)}, u32[]{:S(2)}) collective-permute-start(f32[128,128]{1,0:T(8,128)S(1)} %collective-permute-done.1.refs_2_), channel_id=1, source_target_pairs={{0,4},{4,0},{8,12},{12,8},{16,20},{20,16},{24,28},{28,24},{1,5},{5... | collective-permute-start | bytes 196616 | tf_op jit(solution)/shard_map/gather_items/ppermute | solution.py:322
  11.2 8.6 %collective-permute-start.4 = (f32[128,128]{1,0:T(8,128)S(1)}, f32[128,128]{1,0:T(8,128)S(1)}, u32[]{:S(2)}, u32[]{:S(2)}) collective-permute-start(f32[128,128]{1,0:T(8,128)S(1)} %collective-permute-done.3.refs_4_), channel_id=1, source_target_pairs={{0,4},{4,0},{8,12},{12,8},{16,20},{20,16},{24,28},{28,24},{1,5},{5... | collective-permute-start | bytes 196616 | tf_op jit(solution)/shard_map/gather_items/ppermute | solution.py:322
  12.7 7.1 %collective-permute-start.6 = (f32[128,128]{1,0:T(8,128)S(1)}, f32[128,128]{1,0:T(8,128)S(1)}, u32[]{:S(2)}, u32[]{:S(2)}) collective-permute-start(f32[128,128]{1,0:T(8,128)S(1)} %collective-permute-done.5.refs_6_), channel_id=1, source_target_pairs={{0,4},{4,0},{8,12},{12,8},{16,20},{20,16},{24,28},{28,24},{1,5},{5... | collective-permute-start | bytes 196616 | tf_op jit(solution)/shard_map/gather_items/ppermute | solution.py:322
  21.1 42.5 %all-to-all-start = ((s32[4,1544,128]{2,1,0:T(8,128)}), s32[4,1544,128]{2,1,0:T(8,128)S(1)}, u32[]{:S(2)}, u32[]{:S(2)}) async-start(s32[4,1544,128]{2,1,0:T(8,128)} %get-tuple-element.107), calls=%async_computation | async-start | bytes 6324224 | tf_op jit(solution)/shard_map/send_tiles/all_to_all | solution.py:376
  25.0 6.1 %collective-permute-start.16 = (s32[48,64,128]{2,1,0:T(8,128)}, s32[48,64,128]{2,1,0:T(8,128)S(1)}, u32[]{:S(2)}, u32[]{:S(2)}) collective-permute-start(s32[48,64,128]{2,1,0:T(8,128)} %get-tuple-element.74), channel_id=1, source_target_pairs={{0,1},{1,0},{2,3},{3,2},{4,5},{5,4},{6,7},{7,6},{8,9},{9,8},{10,11... | collective-permute-start | bytes 4718600 | tf_op jit(solution)/shard_map/pack_tiles/ppermute | solution.py:322
  25.1 4.8 %collective-permute-start.15 = (s32[8,128]{1,0:T(8,128)}, s32[8,128]{1,0:T(8,128)S(1)}, u32[]{:S(2)}, u32[]{:S(2)}) collective-permute-start(s32[8,128]{1,0:T(8,128)} %copy-done.5), channel_id=1, source_target_pairs={{0,1},{1,0},{2,3},{3,2},{4,5},{5,4},{6,7},{7,6},{8,9},{9,8},{10,11... | collective-permute-start | bytes 12296 | tf_op jit(solution)/shard_map/pack_tiles/ppermute | solution.py:322
  25.6 4.9 %collective-permute-start.7 = (f32[128,128]{1,0:T(8,128)S(1)}, f32[128,128]{1,0:T(8,128)S(1)}, u32[]{:S(2)}, u32[]{:S(2)}) collective-permute-start(f32[128,128]{1,0:T(8,128)S(1)} %copy-done), channel_id=1, source_target_pairs={{0,1},{1,0},{2,3},{3,2},{4,5},{5,4},{6,7},{7,6},{8,9},{9,8},{10,11... | collective-permute-start | bytes 196616 | tf_op jit(solution)/shard_map/gather_items/ppermute | solution.py:322
  25.6 4.9 %collective-permute-start.11 = (f32[128,128]{1,0:T(8,128)S(1)}, f32[128,128]{1,0:T(8,128)S(1)}, u32[]{:S(2)}, u32[]{:S(2)}) collective-permute-start(f32[128,128]{1,0:T(8,128)S(1)} %collective-permute-done.3.refs_4_), channel_id=1, source_target_pairs={{0,1},{1,0},{2,3},{3,2},{4,5},{5,4},{6,7},{7,6},{8,9},{9,8},{10,11... | collective-permute-start | bytes 196616 | tf_op jit(solution)/shard_map/gather_items/ppermute | solution.py:322
  26.1 4.9 %collective-permute-start.13 = (f32[128,128]{1,0:T(8,128)S(1)}, f32[128,128]{1,0:T(8,128)S(1)}, u32[]{:S(2)}, u32[]{:S(2)}) collective-permute-start(f32[128,128]{1,0:T(8,128)S(1)} %collective-permute-done.5.refs_6_), channel_id=1, source_target_pairs={{0,1},{1,0},{2,3},{3,2},{4,5},{5,4},{6,7},{7,6},{8,9},{9,8},{10,11... | collective-permute-start | bytes 196616 | tf_op jit(solution)/shard_map/gather_items/ppermute | solution.py:322
  33.9 6.5 %collective-permute-start.21 = (f32[256,128]{1,0:T(8,128)S(1)}, f32[256,128]{1,0:T(8,128)S(1)}, u32[]{:S(2)}, u32[]{:S(2)}) collective-permute-start(f32[256,128]{1,0:T(8,128)S(1)} %get-tuple-element.92.own_ref), channel_id=1, source_target_pairs={{0,2},{1,3},{2,0},{3,1},{4,6},{5,7},{6,4},{7,5},{8,10},{9,11},{10,... | collective-permute-start | bytes 393224 | tf_op jit(solution)/shard_map/user_cg/ppermute | solution.py:322
  36.0 8.1 %collective-permute-start.17 = (f32[256,128]{1,0:T(8,128)S(1)}, f32[256,128]{1,0:T(8,128)S(1)}, u32[]{:S(2)}, u32[]{:S(2)}) collective-permute-start(f32[256,128]{1,0:T(8,128)S(1)} %get-tuple-element.79.own_ref), channel_id=1, source_target_pairs={{0,2},{1,3},{2,0},{3,1},{4,6},{5,7},{6,4},{7,5},{8,10},{9,11},{10,... | collective-permute-start | bytes 393224 | tf_op jit(solution)/shard_map/user_cg/ppermute | solution.py:322
  42.0 6.5 %collective-permute-start.22 = (f32[256,128]{1,0:T(8,128)S(1)}, f32[256,128]{1,0:T(8,128)S(1)}, u32[]{:S(2)}, u32[]{:S(2)}) collective-permute-start(f32[256,128]{1,0:T(8,128)S(1)} %get-tuple-element.94.own_ref), channel_id=1, source_target_pairs={{0,2},{1,3},{2,0},{3,1},{4,6},{5,7},{6,4},{7,5},{8,10},{9,11},{10,... | collective-permute-start | bytes 393224 | tf_op jit(solution)/shard_map/user_cg/ppermute | solution.py:322
  45.8 5.8 %collective-permute-start.18 = (f32[256,128]{1,0:T(8,128)S(1)}, f32[256,128]{1,0:T(8,128)S(1)}, u32[]{:S(2)}, u32[]{:S(2)}) collective-permute-start(f32[256,128]{1,0:T(8,128)S(1)} %get-tuple-element.83.own_ref), channel_id=1, source_target_pairs={{0,2},{1,3},{2,0},{3,1},{4,6},{5,7},{6,4},{7,5},{8,10},{9,11},{10,... | collective-permute-start | bytes 393224 | tf_op jit(solution)/shard_map/user_cg/ppermute | solution.py:322
  50.3 5.6 %collective-permute-start.23 = (f32[256,128]{1,0:T(8,128)S(1)}, f32[256,128]{1,0:T(8,128)S(1)}, u32[]{:S(2)}, u32[]{:S(2)}) collective-permute-start(f32[256,128]{1,0:T(8,128)S(1)} %get-tuple-element.98.own_ref), channel_id=1, source_target_pairs={{0,2},{1,3},{2,0},{3,1},{4,6},{5,7},{6,4},{7,5},{8,10},{9,11},{10,... | collective-permute-start | bytes 393224 | tf_op jit(solution)/shard_map/user_cg/ppermute | solution.py:322
  53.4 5.0 %collective-permute-start.19 = (f32[256,128]{1,0:T(8,128)S(1)}, f32[256,128]{1,0:T(8,128)S(1)}, u32[]{:S(2)}, u32[]{:S(2)}) collective-permute-start(f32[256,128]{1,0:T(8,128)S(1)} %get-tuple-element.87.own_ref), channel_id=1, source_target_pairs={{0,2},{1,3},{2,0},{3,1},{4,6},{5,7},{6,4},{7,5},{8,10},{9,11},{10,... | collective-permute-start | bytes 393224 | tf_op jit(solution)/shard_map/user_cg/ppermute | solution.py:322
  63.6 6.4 %collective-permute-start.29 = (f32[512,128]{1,0:T(8,128)S(1)}, f32[512,128]{1,0:T(8,128)S(1)}, u32[]{:S(2)}, u32[]{:S(2)}) collective-permute-start(f32[512,128]{1,0:T(8,128)S(1)} %get-tuple-element.108.refs_0_), channel_id=1, source_target_pairs={{0,8},{4,12},{8,0},{12,4},{16,24},{20,28},{24,16},{28,20},{1,9},{5... | collective-permute-start | bytes 786440 | tf_op jit(solution)/shard_map/gather_users/ppermute | solution.py:322
  65.6 7.3 %collective-permute-start.27 = (f32[512,128]{1,0:T(8,128)S(1)}, f32[512,128]{1,0:T(8,128)S(1)}, u32[]{:S(2)}, u32[]{:S(2)}) collective-permute-start(f32[512,128]{1,0:T(8,128)S(1)} %get-tuple-element.108.refs_0_), channel_id=1, source_target_pairs={{0,4},{4,0},{8,12},{12,8},{16,20},{20,16},{24,28},{28,24},{1,5},{5... | collective-permute-start | bytes 786440 | tf_op jit(solution)/shard_map/gather_users/ppermute | solution.py:322
  70.0 6.4 %collective-permute-start.31 = (f32[512,128]{1,0:T(8,128)S(1)}, f32[512,128]{1,0:T(8,128)S(1)}, u32[]{:S(2)}, u32[]{:S(2)}) collective-permute-start(f32[512,128]{1,0:T(8,128)S(1)} %collective-permute-done.29.refs_4_), channel_id=1, source_target_pairs={{0,4},{4,0},{8,12},{12,8},{16,20},{20,16},{24,28},{28,24},{1,5},{5... | collective-permute-start | bytes 786440 | tf_op jit(solution)/shard_map/gather_users/ppermute | solution.py:322
  71.5 4.9 %collective-permute-start.26 = (f32[512,128]{1,0:T(8,128)S(1)}, f32[512,128]{1,0:T(8,128)S(1)}, u32[]{:S(2)}, u32[]{:S(2)}) collective-permute-start(f32[512,128]{1,0:T(8,128)S(1)} %get-tuple-element.108.refs_0_), channel_id=1, source_target_pairs={{0,1},{1,0},{2,3},{3,2},{4,5},{5,4},{6,7},{7,6},{8,9},{9,8},{10,11... | collective-permute-start | bytes 786440 | tf_op jit(solution)/shard_map/gather_users/ppermute | solution.py:322
  71.5 4.9 %collective-permute-start.30 = (f32[512,128]{1,0:T(8,128)S(1)}, f32[512,128]{1,0:T(8,128)S(1)}, u32[]{:S(2)}, u32[]{:S(2)}) collective-permute-start(f32[512,128]{1,0:T(8,128)S(1)} %collective-permute-done.29.refs_4_), channel_id=1, source_target_pairs={{0,1},{1,0},{2,3},{3,2},{4,5},{5,4},{6,7},{7,6},{8,9},{9,8},{10,11... | collective-permute-start | bytes 786440 | tf_op jit(solution)/shard_map/gather_users/ppermute | solution.py:322
  78.9 5.9 %collective-permute-start.37 = (f32[128,128]{1,0:T(8,128)S(1)}, f32[128,128]{1,0:T(8,128)S(1)}, u32[]{:S(2)}, u32[]{:S(2)}) collective-permute-start(f32[128,128]{1,0:T(8,128)S(1)} %get-tuple-element.126.own_ref), channel_id=1, source_target_pairs={{0,16},{4,20},{8,24},{12,28},{16,0},{20,4},{24,8},{28,12},{1,17},{... | collective-permute-start | bytes 196616 | tf_op jit(solution)/shard_map/item_cg/ppermute | solution.py:322
  81.7 24.0 %collective-permute-start.25 = (f32[128,128]{1,0:T(8,128)S(1)}, f32[128,128]{1,0:T(8,128)S(1)}, u32[]{:S(2)}, u32[]{:S(2)}) collective-permute-start(f32[128,128]{1,0:T(8,128)S(1)} %get-tuple-element.104), channel_id=1, source_target_pairs={{0,1},{1,0},{2,3},{3,2},{4,5},{5,4},{6,7},{7,6},{8,9},{9,8},{10,11... | collective-permute-start | bytes 196616 | tf_op jit(solution)/shard_map/user_cg/ppermute | solution.py:322
  81.7 7.7 %collective-permute-start.33 = (f32[128,128]{1,0:T(8,128)S(1)}, f32[128,128]{1,0:T(8,128)S(1)}, u32[]{:S(2)}, u32[]{:S(2)}) collective-permute-start(f32[128,128]{1,0:T(8,128)S(1)} %get-tuple-element.113.own_ref), channel_id=1, source_target_pairs={{0,16},{4,20},{8,24},{12,28},{16,0},{20,4},{24,8},{28,12},{1,17},{... | collective-permute-start | bytes 196616 | tf_op jit(solution)/shard_map/item_cg/ppermute | solution.py:322
  86.6 5.2 %collective-permute-start.38 = (f32[128,128]{1,0:T(8,128)S(1)}, f32[128,128]{1,0:T(8,128)S(1)}, u32[]{:S(2)}, u32[]{:S(2)}) collective-permute-start(f32[128,128]{1,0:T(8,128)S(1)} %get-tuple-element.128.own_ref), channel_id=1, source_target_pairs={{0,16},{4,20},{8,24},{12,28},{16,0},{20,4},{24,8},{28,12},{1,17},{... | collective-permute-start | bytes 196616 | tf_op jit(solution)/shard_map/item_cg/ppermute | solution.py:322
  90.9 5.9 %collective-permute-start.34 = (f32[128,128]{1,0:T(8,128)S(1)}, f32[128,128]{1,0:T(8,128)S(1)}, u32[]{:S(2)}, u32[]{:S(2)}) collective-permute-start(f32[128,128]{1,0:T(8,128)S(1)} %get-tuple-element.117.own_ref), channel_id=1, source_target_pairs={{0,16},{4,20},{8,24},{12,28},{16,0},{20,4},{24,8},{28,12},{1,17},{... | collective-permute-start | bytes 196616 | tf_op jit(solution)/shard_map/item_cg/ppermute | solution.py:322
  93.5 7.2 %collective-permute-start.39 = (f32[128,128]{1,0:T(8,128)S(1)}, f32[128,128]{1,0:T(8,128)S(1)}, u32[]{:S(2)}, u32[]{:S(2)}) collective-permute-start(f32[128,128]{1,0:T(8,128)S(1)} %get-tuple-element.132.own_ref), channel_id=1, source_target_pairs={{0,16},{4,20},{8,24},{12,28},{16,0},{20,4},{24,8},{28,12},{1,17},{... | collective-permute-start | bytes 196616 | tf_op jit(solution)/shard_map/item_cg/ppermute | solution.py:322
  98.5 5.9 %collective-permute-start.35 = (f32[128,128]{1,0:T(8,128)S(1)}, f32[128,128]{1,0:T(8,128)S(1)}, u32[]{:S(2)}, u32[]{:S(2)}) collective-permute-start(f32[128,128]{1,0:T(8,128)S(1)} %get-tuple-element.121.own_ref), channel_id=1, source_target_pairs={{0,16},{4,20},{8,24},{12,28},{16,0},{20,4},{24,8},{28,12},{1,17},{... | collective-permute-start | bytes 196616 | tf_op jit(solution)/shard_map/item_cg/ppermute | solution.py:322
  101.6 4.7 %collective-permute-start.40 = (f32[8,128]{1,0:T(8,128)S(1)}, f32[8,128]{1,0:T(8,128)S(1)}, u32[]{:S(2)}, u32[]{:S(2)}) collective-permute-start(f32[8,128]{1,0:T(8,128)S(1)} %get-tuple-element.136.refs_8_), channel_id=1, source_target_pairs={{0,16},{4,20},{8,24},{12,28},{16,0},{20,4},{24,8},{28,12},{1,17},{... | collective-permute-start | bytes 12296 | tf_op jit(solution)/shard_map/item_cg/ppermute | solution.py:322
  (17 other events, 58.1 us)

commit v5 on v4

--- a/solution.py
+++ b/solution.py
@@ -316,7 +316,7 @@
     row_blocks = UB * n_item
     rows = row_blocks * half
     slots = -(-slot_total // n_user)
-    width = 2 * rank
+    width = 4 * rank
     def swap(value, axis, mask):
         size = n_item if axis == "item" else n_user
         return lax.ppermute(value, axis, [(place, place ^ mask) for place in range(size)])

time: 112 us -> 112 us (level); the launches traced: 111 us -> 110 us
  starting transfers between devices: 41.9 us -> 39.4 us
  waiting for transfers between devices: 30.9 us -> 33.3 us
    ppermute x41, starting transfers between devices: 38.1 us -> 35.5 us  [swap(): lax.ppermute(value, axis, [(place, place ^ mask) for place in range(size)])]
    ppermute x41, waiting for transfers between devices: 30.9 us -> 33.3 us  [swap(): lax.ppermute(value, axis, [(place, place ^ mask) for place in range(size)])]
  transfers between devices with their start and end apart: 42 -> 42, of which waited for: 18 -> 19; matrix products, arithmetic and copies ran while one was open for 1% -> 1% of each run, Pallas kernels for 28% -> 28%
where the time goes in v5:
time: 112 us; the launch traced here: 110 us
  starting transfers between devices  39.4 us (35%)
  waiting for transfers between devices  33.3 us (30%)
  Pallas kernels  32.1 us (29%)
  local copies, waits for them, and re-layouts  1.93 us (2%)
  between operations  1.58 us (1%)
  other arithmetic  1.38 us (1%)
    ppermute x41, starting transfers between devices, swap(): lax.ppermute(value, axis, [(place, place ^ mask) for place in range(size)])  35.5 us
    ppermute x41, waiting for transfers between devices, swap(): lax.ppermute(value, axis, [(place, place ^ mask) for place in range(size)])  33.3 us
    pallas_call x21, Pallas kernels, call(): pl.pallas_call(kernel, out_shape=tuple(outs), in_specs=[pl.BlockSpec(memo...  32.1 us
    all_to_all x1, starting transfers between devices, dense_shards(): lax.all_to_all(after(packed, *own_items), 'user', 0, 0, tiled=True, axis_...  3.83 us
  transfers between devices with their start and end apart: 42, of which 19 were waited for; matrix products, arithmetic and copies ran while one was open for 1% of the time, Pallas kernels for 28%

profile of v5, /device:TPU:0, one launch (start us, length us, event | category | flops | bytes accessed | tf_op | source)
XLA Modules:
  0.0 109.7 jit_solution(6223771500771871956)
XLA Ops:
  0.6 3.1 %collective-permute-start.1 = (f32[128,128]{1,0:T(8,128)}, f32[128,128]{1,0:T(8,128)S(1)}, u32[]{:S(2)}, u32[]{:S(2)}) collective-permute-start(f32[128,128]{1,0:T(8,128)} %refs_0_.1), channel_id=1, source_target_pairs={{0,8},{4,12},{8,0},{12,4},{16,24},{20,28},{24,16},{28,20},{1,9},{5... | collective-permute-start | bytes 196616 | tf_op jit(solution)/shard_map/gather_items/ppermute | solution.py:322
  3.7 2.6 %collective-permute-start.3 = (f32[128,128]{1,0:T(8,128)}, f32[128,128]{1,0:T(8,128)S(1)}, u32[]{:S(2)}, u32[]{:S(2)}) collective-permute-start(f32[128,128]{1,0:T(8,128)} %refs_0_.1), channel_id=1, source_target_pairs={{0,16},{4,20},{8,24},{12,28},{16,0},{20,4},{24,8},{28,12},{1,17},{... | collective-permute-start | bytes 196616 | tf_op jit(solution)/shard_map/gather_items/ppermute | solution.py:322
  6.3 1.7 %collective-permute-start = (f32[128,128]{1,0:T(8,128)}, f32[128,128]{1,0:T(8,128)S(1)}, u32[]{:S(2)}, u32[]{:S(2)}) collective-permute-start(f32[128,128]{1,0:T(8,128)} %refs_0_.1), channel_id=1, source_target_pairs={{0,4},{4,0},{8,12},{12,8},{16,20},{20,16},{24,28},{28,24},{1,5},{5... | collective-permute-start | bytes 196616 | tf_op jit(solution)/shard_map/gather_items/ppermute | solution.py:322
  11.2 1.5 %collective-permute-start.4 = (f32[128,128]{1,0:T(8,128)S(1)}, f32[128,128]{1,0:T(8,128)S(1)}, u32[]{:S(2)}, u32[]{:S(2)}) collective-permute-start(f32[128,128]{1,0:T(8,128)S(1)} %collective-permute-done.3.refs_4_), channel_id=1, source_target_pairs={{0,4},{4,0},{8,12},{12,8},{16,20},{20,16},{24,28},{28,24},{1,5},{5... | collective-permute-start | bytes 196616 | tf_op jit(solution)/shard_map/gather_items/ppermute | solution.py:322
  14.8 5.0 %pack_tiles.1 = (s32[48,64,128]{2,1,0:T(8,128)}, s32[4,1544,128]{2,1,0:T(8,128)}) custom-call(s32[8,128]{1,0:T(8,128)S(1)} %pad_add_fusion.ids_ref.named_ref, s32[48,128,128]{2,1,0:T(8,128)} %bitcast.4, s32[8,128]{1,0:T(8,128)S(1)} %pad_add_fusion.ids_ref.named_ref), custom_call_target="tpu_custom_call" | custom-call | bytes 7888896 | tf_op jit(solution)/shard_map/pack_tiles/pallas_call | solution.py:295
  21.1 3.8 %all-to-all-start = ((s32[4,1544,128]{2,1,0:T(8,128)}), s32[4,1544,128]{2,1,0:T(8,128)S(1)}, u32[]{:S(2)}, u32[]{:S(2)}) async-start(s32[4,1544,128]{2,1,0:T(8,128)} %get-tuple-element.107), calls=%async_computation | async-start | bytes 6324224 | tf_op jit(solution)/shard_map/send_tiles/all_to_all | solution.py:376
  26.8 3.1 %user_tiles.2 = (f32[512,2048]{1,0:T(8,128)S(1)}, bf16[512,2048]{1,0:T(8,128)(2,1)S(1)}) custom-call(s32[8,128]{1,0:T(8,128)S(1)} %copy-done.6, s32[48,128,128]{2,1,0:T(8,128)} %bitcast.5), custom_call_target="tpu_custom_call" | custom-call | flops 1000000000 | bytes 11538432 | tf_op jit(solution)/shard_map/user_tiles/pallas_call | solution.py:295
  31.6 1.8 %user_tiles.3 = (f32[512,2048]{1,0:T(8,128)S(1)}, bf16[512,2048]{1,0:T(8,128)(2,1)S(1)}) custom-call(s32[8,128]{1,0:T(8,128)S(1)} %collective-permute-done.15.named_ref, s32[48,64,128]{2,1,0:T(8,128)S(1)} %collective-permute-done.16.half_ref, f32[512,2048]{1,0:T(8,128)S(1)} %get-tuple-element.76.dense_in, ...), custom_call_target="tpu_custom_call", output_to_operand_aliasing={{0}: (2, {}), {1}: (3, {})} | custom-call | flops 1000000000 | bytes 16257024 | tf_op jit(solution)/shard_map/user_tiles/pallas_call | solution.py:295
  36.3 4.3 %collective-permute-done.21.other_ref = f32[256,128]{1,0:T(8,128)S(1)} collective-permute-done((f32[256,128]{1,0:T(8,128)S(1)}, f32[256,128]{1,0:T(8,128)S(1)}, u32[]{:S(2)}, u32[]{:S(2)}) %collective-permute-start.21) | collective-permute-done | bytes 131104 | tf_op jit(solution)/shard_map/user_cg/ppermute | solution.py:322
  40.6 1.5 %user_cg.13 = (f32[256,128]{1,0:T(8,128)S(1)}, f32[256,128]{1,0:T(8,128)S(1)}) custom-call(f32[256,128]{1,0:T(8,128)S(1)} %get-tuple-element.92.own_ref, f32[256,128]{1,0:T(8,128)S(1)} %collective-permute-done.21.other_ref, f32[512,2048]{1,0:T(8,128)S(1)} %get-tuple-element.80.conf_ref, bf16[2048,256]{1,0:T(8,128)(2,1)S(1)} %get-tuple-element.81.pairs_ref), custom_call_target="tpu_custom_call" | custom-call | flops 805306368 | bytes 5767168 | tf_op jit(solution)/shard_map/user_cg/pallas_call | solution.py:295
  43.4 1.5 %user_cg.10 = (f32[256,128]{1,0:T(8,128)S(1)}, f32[256,128]{1,0:T(8,128)S(1)}) custom-call(f32[256,128]{1,0:T(8,128)S(1)} %get-tuple-element.79.own_ref, f32[256,128]{1,0:T(8,128)S(1)} %collective-permute-done.17.other_ref, f32[512,2048]{1,0:T(8,128)S(1)} %get-tuple-element.80.conf_ref, bf16[2048,256]{1,0:T(8,128)(2,1)S(1)} %get-tuple-element.81.pairs_ref), custom_call_target="tpu_custom_call" | custom-call | flops 805306368 | bytes 5767168 | tf_op jit(solution)/shard_map/user_cg/pallas_call | solution.py:295
  45.7 2.7 %collective-permute-done.22.other_ref = f32[256,128]{1,0:T(8,128)S(1)} collective-permute-done((f32[256,128]{1,0:T(8,128)S(1)}, f32[256,128]{1,0:T(8,128)S(1)}, u32[]{:S(2)}, u32[]{:S(2)}) %collective-permute-start.22) | collective-permute-done | bytes 131104 | tf_op jit(solution)/shard_map/user_cg/ppermute | solution.py:322
  48.4 1.6 %user_cg.14 = (f32[256,128]{1,0:T(8,128)S(1)}, f32[256,128]{1,0:T(8,128)S(1)}, f32[256,128]{1,0:T(8,128)S(1)}, f32[256,128]{1,0:T(8,128)S(1)}) custom-call(f32[256,128]{1,0:T(8,128)S(1)} %get-tuple-element.93.side_ref, f32[256,128]{1,0:T(8,128)S(1)} %get-tuple-element.94.own_ref, f32[256,128]{1,0:T(8,128)S(1)} %collective-permute-done.22.other_ref, ...), custom_call_target="tpu_custom_call" | custom-call | flops 805306368 | bytes 6160384 | tf_op jit(solution)/shard_map/user_cg/pallas_call | solution.py:295
  51.2 1.6 %user_cg.11 = (f32[256,128]{1,0:T(8,128)S(1)}, f32[256,128]{1,0:T(8,128)S(1)}, f32[256,128]{1,0:T(8,128)S(1)}, f32[256,128]{1,0:T(8,128)S(1)}) custom-call(f32[256,128]{1,0:T(8,128)S(1)} %get-tuple-element.82.side_ref, f32[256,128]{1,0:T(8,128)S(1)} %get-tuple-element.83.own_ref, f32[256,128]{1,0:T(8,128)S(1)} %collective-permute-done.18.other_ref, ...), custom_call_target="tpu_custom_call" | custom-call | flops 805306368 | bytes 6160384 | tf_op jit(solution)/shard_map/user_cg/pallas_call | solution.py:295
  53.8 1.8 %collective-permute-done.23.other_ref = f32[256,128]{1,0:T(8,128)S(1)} collective-permute-done((f32[256,128]{1,0:T(8,128)S(1)}, f32[256,128]{1,0:T(8,128)S(1)}, u32[]{:S(2)}, u32[]{:S(2)}) %collective-permute-start.23) | collective-permute-done | bytes 131104 | tf_op jit(solution)/shard_map/user_cg/ppermute | solution.py:322
  60.3 2.3 %collective-permute-done.20.refs_4_ = f32[8,256]{1,0:T(8,128)S(1)} collective-permute-done((f32[8,256]{1,0:T(8,128)S(1)}, f32[8,256]{1,0:T(8,128)S(1)}, u32[]{:S(2)}, u32[]{:S(2)}) %collective-permute-start.20) | collective-permute-done | bytes 8224 | tf_op jit(solution)/shard_map/user_cg/ppermute | solution.py:322
  63.0 3.0 %collective-permute-start.29 = (f32[512,128]{1,0:T(8,128)S(1)}, f32[512,128]{1,0:T(8,128)S(1)}, u32[]{:S(2)}, u32[]{:S(2)}) collective-permute-start(f32[512,128]{1,0:T(8,128)S(1)} %get-tuple-element.108.refs_0_), channel_id=1, source_target_pairs={{0,8},{4,12},{8,0},{12,4},{16,24},{20,28},{24,16},{28,20},{1,9},{5... | collective-permute-start | bytes 786440 | tf_op jit(solution)/shard_map/gather_users/ppermute | solution.py:322
  66.6 2.3 %item_tiles.1 = (f32[256,4096]{1,0:T(8,128)S(1)}, bf16[256,4096]{1,0:T(8,128)(2,1)S(1)}) custom-call(s32[4,2,128]{2,1,0:T(2,128)S(1)} %slice.7.lists_ref, s32[4,1544,128]{2,1,0:T(8,128)S(1)} %all-to-all-done.tiles_ref), custom_call_target="tpu_custom_call" | custom-call | flops 1000000000 | bytes 11554816 | tf_op jit(solution)/shard_map/item_tiles/pallas_call | solution.py:295
  68.9 1.4 %collective-permute-done.29.refs_4_ = f32[512,128]{1,0:T(8,128)S(1)} collective-permute-done((f32[512,128]{1,0:T(8,128)S(1)}, f32[512,128]{1,0:T(8,128)S(1)}, u32[]{:S(2)}, u32[]{:S(2)}) %collective-permute-start.29) | collective-permute-done | bytes 262176 | tf_op jit(solution)/shard_map/gather_users/ppermute | solution.py:322
  71.8 2.0 %collective-permute-done.27.refs_2_ = f32[512,128]{1,0:T(8,128)S(1)} collective-permute-done((f32[512,128]{1,0:T(8,128)S(1)}, f32[512,128]{1,0:T(8,128)S(1)}, u32[]{:S(2)}, u32[]{:S(2)}) %collective-permute-start.27) | collective-permute-done | bytes 262176 | tf_op jit(solution)/shard_map/gather_users/ppermute | solution.py:322
  73.8 3.0 %collective-permute-done.31.refs_6_ = f32[512,128]{1,0:T(8,128)S(1)} collective-permute-done((f32[512,128]{1,0:T(8,128)S(1)}, f32[512,128]{1,0:T(8,128)S(1)}, u32[]{:S(2)}, u32[]{:S(2)}) %collective-permute-start.31) | collective-permute-done | bytes 262176 | tf_op jit(solution)/shard_map/gather_users/ppermute | solution.py:322
  76.7 1.5 %collective-permute-done.32.refs_7_ = f32[512,128]{1,0:T(8,128)S(1)} collective-permute-done((f32[512,128]{1,0:T(8,128)S(1)}, f32[512,128]{1,0:T(8,128)S(1)}, u32[]{:S(2)}, u32[]{:S(2)}) %collective-permute-start.32) | collective-permute-done | bytes 262176 | tf_op jit(solution)/shard_map/gather_users/ppermute | solution.py:322
  79.2 1.7 %collective-permute-start.37 = (f32[128,128]{1,0:T(8,128)S(1)}, f32[128,128]{1,0:T(8,128)S(1)}, u32[]{:S(2)}, u32[]{:S(2)}) collective-permute-start(f32[128,128]{1,0:T(8,128)S(1)} %get-tuple-element.126.own_ref), channel_id=1, source_target_pairs={{0,16},{4,20},{8,24},{12,28},{16,0},{20,4},{24,8},{28,12},{1,17},{... | collective-permute-start | bytes 196616 | tf_op jit(solution)/shard_map/item_cg/ppermute | solution.py:322
  82.2 2.2 %collective-permute-done.37.other_ref = f32[128,128]{1,0:T(8,128)S(1)} collective-permute-done((f32[128,128]{1,0:T(8,128)S(1)}, f32[128,128]{1,0:T(8,128)S(1)}, u32[]{:S(2)}, u32[]{:S(2)}) %collective-permute-start.37) | collective-permute-done | bytes 65568 | tf_op jit(solution)/shard_map/item_cg/ppermute | solution.py:322
  84.4 1.7 %item_cg.12 = (f32[128,128]{1,0:T(8,128)S(1)}, f32[128,128]{1,0:T(8,128)S(1)}) custom-call(f32[128,128]{1,0:T(8,128)S(1)} %get-tuple-element.126.own_ref, f32[128,128]{1,0:T(8,128)S(1)} %collective-permute-done.37.other_ref, f32[256,4096]{1,0:T(8,128)S(1)} %get-tuple-element.114.conf_ref, bf16[4096,256]{1,0:T(8,128)(2,1)S(1)} %get-tuple-element.115.pairs_ref), custom_call_target="tpu_custom_call" | custom-call | flops 805306368 | bytes 6553600 | tf_op jit(solution)/shard_map/item_cg/pallas_call | solution.py:295
  86.1 1.7 %collective-permute-start.38 = (f32[128,128]{1,0:T(8,128)S(1)}, f32[128,128]{1,0:T(8,128)S(1)}, u32[]{:S(2)}, u32[]{:S(2)}) collective-permute-start(f32[128,128]{1,0:T(8,128)S(1)} %get-tuple-element.128.own_ref), channel_id=1, source_target_pairs={{0,16},{4,20},{8,24},{12,28},{16,0},{20,4},{24,8},{28,12},{1,17},{... | collective-permute-start | bytes 196616 | tf_op jit(solution)/shard_map/item_cg/ppermute | solution.py:322
  91.3 1.5 %item_cg.13 = (f32[128,128]{1,0:T(8,128)S(1)}, f32[128,128]{1,0:T(8,128)S(1)}, f32[128,128]{1,0:T(8,128)S(1)}, f32[128,128]{1,0:T(8,128)S(1)}) custom-call(f32[128,128]{1,0:T(8,128)S(1)} %get-tuple-element.127.side_ref, f32[128,128]{1,0:T(8,128)S(1)} %get-tuple-element.128.own_ref, f32[128,128]{1,0:T(8,128)S(1)} %collective-permute-done.38.other_ref, ...), custom_call_target="tpu_custom_call" | custom-call | flops 805306368 | bytes 6750208 | tf_op jit(solution)/shard_map/item_cg/pallas_call | solution.py:295
  92.9 1.8 %collective-permute-start.39 = (f32[128,128]{1,0:T(8,128)S(1)}, f32[128,128]{1,0:T(8,128)S(1)}, u32[]{:S(2)}, u32[]{:S(2)}) collective-permute-start(f32[128,128]{1,0:T(8,128)S(1)} %get-tuple-element.132.own_ref), channel_id=1, source_target_pairs={{0,16},{4,20},{8,24},{12,28},{16,0},{20,4},{24,8},{28,12},{1,17},{... | collective-permute-start | bytes 196616 | tf_op jit(solution)/shard_map/item_cg/ppermute | solution.py:322
  95.3 1.5 %item_cg.10 = (f32[128,128]{1,0:T(8,128)S(1)}, f32[128,128]{1,0:T(8,128)S(1)}, f32[128,128]{1,0:T(8,128)S(1)}, f32[128,128]{1,0:T(8,128)S(1)}) custom-call(f32[128,128]{1,0:T(8,128)S(1)} %get-tuple-element.116.side_ref, f32[128,128]{1,0:T(8,128)S(1)} %get-tuple-element.117.own_ref, f32[128,128]{1,0:T(8,128)S(1)} %collective-permute-done.34.other_ref, ...), custom_call_target="tpu_custom_call" | custom-call | flops 805306368 | bytes 6750208 | tf_op jit(solution)/shard_map/item_cg/pallas_call | solution.py:295
  97.5 1.9 %collective-permute-done.39.other_ref = f32[128,128]{1,0:T(8,128)S(1)} collective-permute-done((f32[128,128]{1,0:T(8,128)S(1)}, f32[128,128]{1,0:T(8,128)S(1)}, u32[]{:S(2)}, u32[]{:S(2)}) %collective-permute-start.39) | collective-permute-done | bytes 65568 | tf_op jit(solution)/shard_map/item_cg/ppermute | solution.py:322
  101.1 2.0 %collective-permute-done.35.other_ref = f32[128,128]{1,0:T(8,128)S(1)} collective-permute-done((f32[128,128]{1,0:T(8,128)S(1)}, f32[128,128]{1,0:T(8,128)S(1)}, u32[]{:S(2)}, u32[]{:S(2)}) %collective-permute-start.35) | collective-permute-done | bytes 65568 | tf_op jit(solution)/shard_map/item_cg/ppermute | solution.py:322
  105.0 3.7 %collective-permute-done.36.refs_4_ = f32[8,128]{1,0:T(8,128)S(1)} collective-permute-done((f32[8,128]{1,0:T(8,128)S(1)}, f32[8,128]{1,0:T(8,128)S(1)}, u32[]{:S(2)}, u32[]{:S(2)}) %collective-permute-start.36) | collective-permute-done | bytes 4128 | tf_op jit(solution)/shard_map/item_cg/ppermute | solution.py:322
  (89 shorter events, 35.3 us)
Async XLA Ops:
  0.6 9.5 %collective-permute-start.1 = (f32[128,128]{1,0:T(8,128)}, f32[128,128]{1,0:T(8,128)S(1)}, u32[]{:S(2)}, u32[]{:S(2)}) collective-permute-start(f32[128,128]{1,0:T(8,128)} %refs_0_.1), channel_id=1, source_target_pairs={{0,8},{4,12},{8,0},{12,4},{16,24},{20,28},{24,16},{28,20},{1,9},{5... | collective-permute-start | bytes 196616 | tf_op jit(solution)/shard_map/gather_items/ppermute | solution.py:322
  3.7 7.5 %collective-permute-start.3 = (f32[128,128]{1,0:T(8,128)}, f32[128,128]{1,0:T(8,128)S(1)}, u32[]{:S(2)}, u32[]{:S(2)}) collective-permute-start(f32[128,128]{1,0:T(8,128)} %refs_0_.1), channel_id=1, source_target_pairs={{0,16},{4,20},{8,24},{12,28},{16,0},{20,4},{24,8},{28,12},{1,17},{... | collective-permute-start | bytes 196616 | tf_op jit(solution)/shard_map/gather_items/ppermute | solution.py:322
  6.3 6.4 %collective-permute-start.5 = (f32[128,128]{1,0:T(8,128)}, f32[128,128]{1,0:T(8,128)S(1)}, u32[]{:S(2)}, u32[]{:S(2)}) collective-permute-start(f32[128,128]{1,0:T(8,128)} %refs_0_.1), channel_id=1, source_target_pairs={{0,24},{4,28},{8,16},{12,20},{16,8},{20,12},{24,0},{28,4},{1,25},{... | collective-permute-start | bytes 196616 | tf_op jit(solution)/shard_map/gather_items/ppermute | solution.py:322
  6.3 13.5 %collective-permute-start = (f32[128,128]{1,0:T(8,128)}, f32[128,128]{1,0:T(8,128)S(1)}, u32[]{:S(2)}, u32[]{:S(2)}) collective-permute-start(f32[128,128]{1,0:T(8,128)} %refs_0_.1), channel_id=1, source_target_pairs={{0,4},{4,0},{8,12},{12,8},{16,20},{20,16},{24,28},{28,24},{1,5},{5... | collective-permute-start | bytes 196616 | tf_op jit(solution)/shard_map/gather_items/ppermute | solution.py:322
  10.1 4.7 %collective-permute-start.2 = (f32[128,128]{1,0:T(8,128)S(1)}, f32[128,128]{1,0:T(8,128)S(1)}, u32[]{:S(2)}, u32[]{:S(2)}) collective-permute-start(f32[128,128]{1,0:T(8,128)S(1)} %collective-permute-done.1.refs_2_), channel_id=1, source_target_pairs={{0,4},{4,0},{8,12},{12,8},{16,20},{20,16},{24,28},{28,24},{1,5},{5... | collective-permute-start | bytes 196616 | tf_op jit(solution)/shard_map/gather_items/ppermute | solution.py:322
  11.2 8.6 %collective-permute-start.4 = (f32[128,128]{1,0:T(8,128)S(1)}, f32[128,128]{1,0:T(8,128)S(1)}, u32[]{:S(2)}, u32[]{:S(2)}) collective-permute-start(f32[128,128]{1,0:T(8,128)S(1)} %collective-permute-done.3.refs_4_), channel_id=1, source_target_pairs={{0,4},{4,0},{8,12},{12,8},{16,20},{20,16},{24,28},{28,24},{1,5},{5... | collective-permute-start | bytes 196616 | tf_op jit(solution)/shard_map/gather_items/ppermute | solution.py:322
  12.7 7.1 %collective-permute-start.6 = (f32[128,128]{1,0:T(8,128)S(1)}, f32[128,128]{1,0:T(8,128)S(1)}, u32[]{:S(2)}, u32[]{:S(2)}) collective-permute-start(f32[128,128]{1,0:T(8,128)S(1)} %collective-permute-done.5.refs_6_), channel_id=1, source_target_pairs={{0,4},{4,0},{8,12},{12,8},{16,20},{20,16},{24,28},{28,24},{1,5},{5... | collective-permute-start | bytes 196616 | tf_op jit(solution)/shard_map/gather_items/ppermute | solution.py:322
  21.1 41.9 %all-to-all-start = ((s32[4,1544,128]{2,1,0:T(8,128)}), s32[4,1544,128]{2,1,0:T(8,128)S(1)}, u32[]{:S(2)}, u32[]{:S(2)}) async-start(s32[4,1544,128]{2,1,0:T(8,128)} %get-tuple-element.107), calls=%async_computation | async-start | bytes 6324224 | tf_op jit(solution)/shard_map/send_tiles/all_to_all | solution.py:376
  25.0 6.2 %collective-permute-start.16 = (s32[48,64,128]{2,1,0:T(8,128)}, s32[48,64,128]{2,1,0:T(8,128)S(1)}, u32[]{:S(2)}, u32[]{:S(2)}) collective-permute-start(s32[48,64,128]{2,1,0:T(8,128)} %get-tuple-element.74), channel_id=1, source_target_pairs={{0,1},{1,0},{2,3},{3,2},{4,5},{5,4},{6,7},{7,6},{8,9},{9,8},{10,11... | collective-permute-start | bytes 4718600 | tf_op jit(solution)/shard_map/pack_tiles/ppermute | solution.py:322
  25.1 4.9 %collective-permute-start.15 = (s32[8,128]{1,0:T(8,128)}, s32[8,128]{1,0:T(8,128)S(1)}, u32[]{:S(2)}, u32[]{:S(2)}) collective-permute-start(s32[8,128]{1,0:T(8,128)} %copy-done.5), channel_id=1, source_target_pairs={{0,1},{1,0},{2,3},{3,2},{4,5},{5,4},{6,7},{7,6},{8,9},{9,8},{10,11... | collective-permute-start | bytes 12296 | tf_op jit(solution)/shard_map/pack_tiles/ppermute | solution.py:322
  25.6 5.0 %collective-permute-start.7 = (f32[128,128]{1,0:T(8,128)S(1)}, f32[128,128]{1,0:T(8,128)S(1)}, u32[]{:S(2)}, u32[]{:S(2)}) collective-permute-start(f32[128,128]{1,0:T(8,128)S(1)} %copy-done), channel_id=1, source_target_pairs={{0,1},{1,0},{2,3},{3,2},{4,5},{5,4},{6,7},{7,6},{8,9},{9,8},{10,11... | collective-permute-start | bytes 196616 | tf_op jit(solution)/shard_map/gather_items/ppermute | solution.py:322
  25.6 5.0 %collective-permute-start.11 = (f32[128,128]{1,0:T(8,128)S(1)}, f32[128,128]{1,0:T(8,128)S(1)}, u32[]{:S(2)}, u32[]{:S(2)}) collective-permute-start(f32[128,128]{1,0:T(8,128)S(1)} %collective-permute-done.3.refs_4_), channel_id=1, source_target_pairs={{0,1},{1,0},{2,3},{3,2},{4,5},{5,4},{6,7},{7,6},{8,9},{9,8},{10,11... | collective-permute-start | bytes 196616 | tf_op jit(solution)/shard_map/gather_items/ppermute | solution.py:322
  26.1 5.0 %collective-permute-start.13 = (f32[128,128]{1,0:T(8,128)S(1)}, f32[128,128]{1,0:T(8,128)S(1)}, u32[]{:S(2)}, u32[]{:S(2)}) collective-permute-start(f32[128,128]{1,0:T(8,128)S(1)} %collective-permute-done.5.refs_6_), channel_id=1, source_target_pairs={{0,1},{1,0},{2,3},{3,2},{4,5},{5,4},{6,7},{7,6},{8,9},{9,8},{10,11... | collective-permute-start | bytes 196616 | tf_op jit(solution)/shard_map/gather_items/ppermute | solution.py:322
  34.2 6.4 %collective-permute-start.21 = (f32[256,128]{1,0:T(8,128)S(1)}, f32[256,128]{1,0:T(8,128)S(1)}, u32[]{:S(2)}, u32[]{:S(2)}) collective-permute-start(f32[256,128]{1,0:T(8,128)S(1)} %get-tuple-element.92.own_ref), channel_id=1, source_target_pairs={{0,2},{1,3},{2,0},{3,1},{4,6},{5,7},{6,4},{7,5},{8,10},{9,11},{10,... | collective-permute-start | bytes 393224 | tf_op jit(solution)/shard_map/user_cg/ppermute | solution.py:322
  35.5 7.9 %collective-permute-start.17 = (f32[256,128]{1,0:T(8,128)S(1)}, f32[256,128]{1,0:T(8,128)S(1)}, u32[]{:S(2)}, u32[]{:S(2)}) collective-permute-start(f32[256,128]{1,0:T(8,128)S(1)} %get-tuple-element.79.own_ref), channel_id=1, source_target_pairs={{0,2},{1,3},{2,0},{3,1},{4,6},{5,7},{6,4},{7,5},{8,10},{9,11},{10,... | collective-permute-start | bytes 393224 | tf_op jit(solution)/shard_map/user_cg/ppermute | solution.py:322
  42.1 6.3 %collective-permute-start.22 = (f32[256,128]{1,0:T(8,128)S(1)}, f32[256,128]{1,0:T(8,128)S(1)}, u32[]{:S(2)}, u32[]{:S(2)}) collective-permute-start(f32[256,128]{1,0:T(8,128)S(1)} %get-tuple-element.94.own_ref), channel_id=1, source_target_pairs={{0,2},{1,3},{2,0},{3,1},{4,6},{5,7},{6,4},{7,5},{8,10},{9,11},{10,... | collective-permute-start | bytes 393224 | tf_op jit(solution)/shard_map/user_cg/ppermute | solution.py:322
  44.9 6.4 %collective-permute-start.18 = (f32[256,128]{1,0:T(8,128)S(1)}, f32[256,128]{1,0:T(8,128)S(1)}, u32[]{:S(2)}, u32[]{:S(2)}) collective-permute-start(f32[256,128]{1,0:T(8,128)S(1)} %get-tuple-element.83.own_ref), channel_id=1, source_target_pairs={{0,2},{1,3},{2,0},{3,1},{4,6},{5,7},{6,4},{7,5},{8,10},{9,11},{10,... | collective-permute-start | bytes 393224 | tf_op jit(solution)/shard_map/user_cg/ppermute | solution.py:322
  50.0 5.6 %collective-permute-start.23 = (f32[256,128]{1,0:T(8,128)S(1)}, f32[256,128]{1,0:T(8,128)S(1)}, u32[]{:S(2)}, u32[]{:S(2)}) collective-permute-start(f32[256,128]{1,0:T(8,128)S(1)} %get-tuple-element.98.own_ref), channel_id=1, source_target_pairs={{0,2},{1,3},{2,0},{3,1},{4,6},{5,7},{6,4},{7,5},{8,10},{9,11},{10,... | collective-permute-start | bytes 393224 | tf_op jit(solution)/shard_map/user_cg/ppermute | solution.py:322
  52.8 5.0 %collective-permute-start.19 = (f32[256,128]{1,0:T(8,128)S(1)}, f32[256,128]{1,0:T(8,128)S(1)}, u32[]{:S(2)}, u32[]{:S(2)}) collective-permute-start(f32[256,128]{1,0:T(8,128)S(1)} %get-tuple-element.87.own_ref), channel_id=1, source_target_pairs={{0,2},{1,3},{2,0},{3,1},{4,6},{5,7},{6,4},{7,5},{8,10},{9,11},{10,... | collective-permute-start | bytes 393224 | tf_op jit(solution)/shard_map/user_cg/ppermute | solution.py:322
  63.0 7.4 %collective-permute-start.29 = (f32[512,128]{1,0:T(8,128)S(1)}, f32[512,128]{1,0:T(8,128)S(1)}, u32[]{:S(2)}, u32[]{:S(2)}) collective-permute-start(f32[512,128]{1,0:T(8,128)S(1)} %get-tuple-element.108.refs_0_), channel_id=1, source_target_pairs={{0,8},{4,12},{8,0},{12,4},{16,24},{20,28},{24,16},{28,20},{1,9},{5... | collective-permute-start | bytes 786440 | tf_op jit(solution)/shard_map/gather_users/ppermute | solution.py:322
  66.0 7.8 %collective-permute-start.27 = (f32[512,128]{1,0:T(8,128)S(1)}, f32[512,128]{1,0:T(8,128)S(1)}, u32[]{:S(2)}, u32[]{:S(2)}) collective-permute-start(f32[512,128]{1,0:T(8,128)S(1)} %get-tuple-element.108.refs_0_), channel_id=1, source_target_pairs={{0,4},{4,0},{8,12},{12,8},{16,20},{20,16},{24,28},{28,24},{1,5},{5... | collective-permute-start | bytes 786440 | tf_op jit(solution)/shard_map/gather_users/ppermute | solution.py:322
  70.3 6.4 %collective-permute-start.31 = (f32[512,128]{1,0:T(8,128)S(1)}, f32[512,128]{1,0:T(8,128)S(1)}, u32[]{:S(2)}, u32[]{:S(2)}) collective-permute-start(f32[512,128]{1,0:T(8,128)S(1)} %collective-permute-done.29.refs_4_), channel_id=1, source_target_pairs={{0,4},{4,0},{8,12},{12,8},{16,20},{20,16},{24,28},{28,24},{1,5},{5... | collective-permute-start | bytes 786440 | tf_op jit(solution)/shard_map/gather_users/ppermute | solution.py:322
  71.3 5.5 %collective-permute-start.26 = (f32[512,128]{1,0:T(8,128)S(1)}, f32[512,128]{1,0:T(8,128)S(1)}, u32[]{:S(2)}, u32[]{:S(2)}) collective-permute-start(f32[512,128]{1,0:T(8,128)S(1)} %get-tuple-element.108.refs_0_), channel_id=1, source_target_pairs={{0,1},{1,0},{2,3},{3,2},{4,5},{5,4},{6,7},{7,6},{8,9},{9,8},{10,11... | collective-permute-start | bytes 786440 | tf_op jit(solution)/shard_map/gather_users/ppermute | solution.py:322
  71.3 5.5 %collective-permute-start.30 = (f32[512,128]{1,0:T(8,128)S(1)}, f32[512,128]{1,0:T(8,128)S(1)}, u32[]{:S(2)}, u32[]{:S(2)}) collective-permute-start(f32[512,128]{1,0:T(8,128)S(1)} %collective-permute-done.29.refs_4_), channel_id=1, source_target_pairs={{0,1},{1,0},{2,3},{3,2},{4,5},{5,4},{6,7},{7,6},{8,9},{9,8},{10,11... | collective-permute-start | bytes 786440 | tf_op jit(solution)/shard_map/gather_users/ppermute | solution.py:322
  79.2 5.2 %collective-permute-start.37 = (f32[128,128]{1,0:T(8,128)S(1)}, f32[128,128]{1,0:T(8,128)S(1)}, u32[]{:S(2)}, u32[]{:S(2)}) collective-permute-start(f32[128,128]{1,0:T(8,128)S(1)} %get-tuple-element.126.own_ref), channel_id=1, source_target_pairs={{0,16},{4,20},{8,24},{12,28},{16,0},{20,4},{24,8},{28,12},{1,17},{... | collective-permute-start | bytes 196616 | tf_op jit(solution)/shard_map/item_cg/ppermute | solution.py:322
  80.9 23.5 %collective-permute-start.25 = (f32[128,128]{1,0:T(8,128)S(1)}, f32[128,128]{1,0:T(8,128)S(1)}, u32[]{:S(2)}, u32[]{:S(2)}) collective-permute-start(f32[128,128]{1,0:T(8,128)S(1)} %get-tuple-element.104), channel_id=1, source_target_pairs={{0,1},{1,0},{2,3},{3,2},{4,5},{5,4},{6,7},{7,6},{8,9},{9,8},{10,11... | collective-permute-start | bytes 196616 | tf_op jit(solution)/shard_map/user_cg/ppermute | solution.py:322
  80.9 7.8 %collective-permute-start.33 = (f32[128,128]{1,0:T(8,128)S(1)}, f32[128,128]{1,0:T(8,128)S(1)}, u32[]{:S(2)}, u32[]{:S(2)}) collective-permute-start(f32[128,128]{1,0:T(8,128)S(1)} %get-tuple-element.113.own_ref), channel_id=1, source_target_pairs={{0,16},{4,20},{8,24},{12,28},{16,0},{20,4},{24,8},{28,12},{1,17},{... | collective-permute-start | bytes 196616 | tf_op jit(solution)/shard_map/item_cg/ppermute | solution.py:322
  86.1 5.2 %collective-permute-start.38 = (f32[128,128]{1,0:T(8,128)S(1)}, f32[128,128]{1,0:T(8,128)S(1)}, u32[]{:S(2)}, u32[]{:S(2)}) collective-permute-start(f32[128,128]{1,0:T(8,128)S(1)} %get-tuple-element.128.own_ref), channel_id=1, source_target_pairs={{0,16},{4,20},{8,24},{12,28},{16,0},{20,4},{24,8},{28,12},{1,17},{... | collective-permute-start | bytes 196616 | tf_op jit(solution)/shard_map/item_cg/ppermute | solution.py:322
  90.1 5.2 %collective-permute-start.34 = (f32[128,128]{1,0:T(8,128)S(1)}, f32[128,128]{1,0:T(8,128)S(1)}, u32[]{:S(2)}, u32[]{:S(2)}) collective-permute-start(f32[128,128]{1,0:T(8,128)S(1)} %get-tuple-element.117.own_ref), channel_id=1, source_target_pairs={{0,16},{4,20},{8,24},{12,28},{16,0},{20,4},{24,8},{28,12},{1,17},{... | collective-permute-start | bytes 196616 | tf_op jit(solution)/shard_map/item_cg/ppermute | solution.py:322
  92.9 6.5 %collective-permute-start.39 = (f32[128,128]{1,0:T(8,128)S(1)}, f32[128,128]{1,0:T(8,128)S(1)}, u32[]{:S(2)}, u32[]{:S(2)}) collective-permute-start(f32[128,128]{1,0:T(8,128)S(1)} %get-tuple-element.132.own_ref), channel_id=1, source_target_pairs={{0,16},{4,20},{8,24},{12,28},{16,0},{20,4},{24,8},{28,12},{1,17},{... | collective-permute-start | bytes 196616 | tf_op jit(solution)/shard_map/item_cg/ppermute | solution.py:322
  96.8 6.4 %collective-permute-start.35 = (f32[128,128]{1,0:T(8,128)S(1)}, f32[128,128]{1,0:T(8,128)S(1)}, u32[]{:S(2)}, u32[]{:S(2)}) collective-permute-start(f32[128,128]{1,0:T(8,128)S(1)} %get-tuple-element.121.own_ref), channel_id=1, source_target_pairs={{0,16},{4,20},{8,24},{12,28},{16,0},{20,4},{24,8},{28,12},{1,17},{... | collective-permute-start | bytes 196616 | tf_op jit(solution)/shard_map/item_cg/ppermute | solution.py:322
  100.3 4.7 %collective-permute-start.40 = (f32[8,128]{1,0:T(8,128)S(1)}, f32[8,128]{1,0:T(8,128)S(1)}, u32[]{:S(2)}, u32[]{:S(2)}) collective-permute-start(f32[8,128]{1,0:T(8,128)S(1)} %get-tuple-element.136.refs_8_), channel_id=1, source_target_pairs={{0,16},{4,20},{8,24},{12,28},{16,0},{20,4},{24,8},{28,12},{1,17},{... | collective-permute-start | bytes 12296 | tf_op jit(solution)/shard_map/item_cg/ppermute | solution.py:322
  (17 other events, 58.6 us)

commit v6 on v5

--- a/solution.py
+++ b/solution.py
@@ -140,28 +140,28 @@
     half = block // 2
     core = lax.rem(lax.axis_index("item"), 2)
     rows = pl.ds(pl.multiple_of(core * half, half), half)
-    copy = pltpu.make_async_copy(conf_ref.at[:, rows, :], held, sem)
-    copy.start()
+    step = slot_total // sem.shape[0]
+    copies = []
+    for place in range(sem.shape[0]):
+        slots = pl.ds(place * step, step)
+        copies.append(pltpu.make_async_copy(conf_ref.at[slots, rows, :], held.at[slots], sem.at[place]))
+        copies[-1].start()
     dense_ref[...] = jnp.full(dense_ref.shape, weight_zero, f32)
     weight_ref[...] = jnp.zeros(weight_ref.shape, bf16)
-    copy.wait()
-
-    def one(slot, carry):
-        user_tile(named_ref, slot, 0, held[slot], dense_ref, weight_ref)
-        return carry
-
-    lax.fori_loop(0, jnp.minimum(named_ref[1, 1], slot_total), one, 0)
+    for slot in range(slot_total):
+        if slot % step == 0:
+            copies[slot // step].wait()
+        counts = jnp.where(slot < named_ref[1, 1], held[slot], 0)
+        user_tile(named_ref, slot, 0, counts, dense_ref, weight_ref)
 
 
 def other_tiles_kernel(named_ref, half_ref, dense_in, weight_in, dense_ref, weight_ref):
     slot_total, _, block = half_ref.shape
     owners = dense_ref.shape[1] // block // 2
 
-    def one(slot, carry):
-        user_tile(named_ref, slot, owners, half_ref[slot], dense_ref, weight_ref)
-        return carry
-
-    lax.fori_loop(0, jnp.minimum(named_ref[1, 1], slot_total), one, 0)
+    for slot in range(slot_total):
+        counts = jnp.where(slot < named_ref[1, 1], half_ref[slot], 0)
+        user_tile(named_ref, slot, owners, counts, dense_ref, weight_ref)
 
 
 def user_side_kernel(count, *refs):
@@ -384,7 +384,7 @@
         user_conf, user_weight = call(
             functools.partial(own_tiles_kernel, unobserved / (item_init.shape[0] * n_user * n_item)),
             dense, own_named, far_conf, scalars=1, far=1, flops=10 ** 9,
-            scratch=(pltpu.VMEM((slot_total, half, block), jnp.int32), pltpu.SemaphoreType.DMA(())),
+            scratch=(pltpu.VMEM((slot_total, half, block), jnp.int32), pltpu.SemaphoreType.DMA((8,))),
         )
         user_conf, user_weight = call(
             other_tiles_kernel, dense, other_named, other_half, user_conf, user_weight,

time: 112 us -> 109 us (0.973)
  waiting for transfers between devices: 33.3 us -> 28.5 us
  starting transfers between devices: 39.4 us -> 43.4 us
  Pallas kernels: 32.1 us -> 30.9 us
    ppermute x41, waiting for transfers between devices: 33.3 us -> 28.5 us  [swap(): lax.ppermute(value, axis, [(place, place ^ mask) for place in range(size)])]
    ppermute x41, starting transfers between devices: 35.5 us -> 39.5 us  [swap(): lax.ppermute(value, axis, [(place, place ^ mask) for place in range(size)])]
    pallas_call x21, Pallas kernels: 32.1 us -> 30.9 us  [call(): pl.pallas_call(kernel, out_shape=tuple(outs), in_specs=[pl.BlockSpec(memo...]
  transfers between devices with their start and end apart: 42 -> 42, of which waited for: 19 -> 17; matrix products, arithmetic and copies ran while one was open for 1% -> 1% of each run, Pallas kernels for 28% -> 27%
where the time goes in v6:
time: 109 us; the launch traced here: 108 us
  starting transfers between devices  43.4 us (40%)
  Pallas kernels  30.9 us (28%)
  waiting for transfers between devices  28.5 us (26%)
  local copies, waits for them, and re-layouts  1.93 us (2%)
  between operations  1.59 us (1%)
  other arithmetic  1.38 us (1%)
    ppermute x41, starting transfers between devices, swap(): lax.ppermute(value, axis, [(place, place ^ mask) for place in range(size)])  39.5 us
    pallas_call x21, Pallas kernels, call(): pl.pallas_call(kernel, out_shape=tuple(outs), in_specs=[pl.BlockSpec(memo...  30.9 us
    ppermute x41, waiting for transfers between devices, swap(): lax.ppermute(value, axis, [(place, place ^ mask) for place in range(size)])  28.5 us
    all_to_all x1, starting transfers between devices, dense_shards(): lax.all_to_all(after(packed, *own_items), 'user', 0, 0, tiled=True, axis_...  3.83 us
  transfers between devices with their start and end apart: 42, of which 17 were waited for; matrix products, arithmetic and copies ran while one was open for 1% of the time, Pallas kernels for 27%

profile of v6, /device:TPU:0, one launch (start us, length us, event | category | flops | bytes accessed | tf_op | source)
XLA Modules:
  0.0 107.7 jit_solution(5700222995693883661)
XLA Ops:
  0.6 3.1 %collective-permute-start.1 = (f32[128,128]{1,0:T(8,128)}, f32[128,128]{1,0:T(8,128)S(1)}, u32[]{:S(2)}, u32[]{:S(2)}) collective-permute-start(f32[128,128]{1,0:T(8,128)} %refs_0_.1), channel_id=1, source_target_pairs={{0,8},{4,12},{8,0},{12,4},{16,24},{20,28},{24,16},{28,20},{1,9},{5... | collective-permute-start | bytes 196616 | tf_op jit(solution)/shard_map/gather_items/ppermute | solution.py:322
  3.7 2.6 %collective-permute-start.3 = (f32[128,128]{1,0:T(8,128)}, f32[128,128]{1,0:T(8,128)S(1)}, u32[]{:S(2)}, u32[]{:S(2)}) collective-permute-start(f32[128,128]{1,0:T(8,128)} %refs_0_.1), channel_id=1, source_target_pairs={{0,16},{4,20},{8,24},{12,28},{16,0},{20,4},{24,8},{28,12},{1,17},{... | collective-permute-start | bytes 196616 | tf_op jit(solution)/shard_map/gather_items/ppermute | solution.py:322
  6.3 1.7 %collective-permute-start = (f32[128,128]{1,0:T(8,128)}, f32[128,128]{1,0:T(8,128)S(1)}, u32[]{:S(2)}, u32[]{:S(2)}) collective-permute-start(f32[128,128]{1,0:T(8,128)} %refs_0_.1), channel_id=1, source_target_pairs={{0,4},{4,0},{8,12},{12,8},{16,20},{20,16},{24,28},{28,24},{1,5},{5... | collective-permute-start | bytes 196616 | tf_op jit(solution)/shard_map/gather_items/ppermute | solution.py:322
  11.2 1.5 %collective-permute-start.4 = (f32[128,128]{1,0:T(8,128)S(1)}, f32[128,128]{1,0:T(8,128)S(1)}, u32[]{:S(2)}, u32[]{:S(2)}) collective-permute-start(f32[128,128]{1,0:T(8,128)S(1)} %collective-permute-done.3.refs_4_), channel_id=1, source_target_pairs={{0,4},{4,0},{8,12},{12,8},{16,20},{20,16},{24,28},{28,24},{1,5},{5... | collective-permute-start | bytes 196616 | tf_op jit(solution)/shard_map/gather_items/ppermute | solution.py:322
  14.8 5.0 %pack_tiles.1 = (s32[48,64,128]{2,1,0:T(8,128)}, s32[4,1544,128]{2,1,0:T(8,128)}) custom-call(s32[8,128]{1,0:T(8,128)S(1)} %pad_add_fusion.ids_ref.named_ref, s32[48,128,128]{2,1,0:T(8,128)} %bitcast.4, s32[8,128]{1,0:T(8,128)S(1)} %pad_add_fusion.ids_ref.named_ref), custom_call_target="tpu_custom_call" | custom-call | bytes 7888896 | tf_op jit(solution)/shard_map/pack_tiles/pallas_call | solution.py:295
  21.1 3.8 %all-to-all-start = ((s32[4,1544,128]{2,1,0:T(8,128)}), s32[4,1544,128]{2,1,0:T(8,128)S(1)}, u32[]{:S(2)}, u32[]{:S(2)}) async-start(s32[4,1544,128]{2,1,0:T(8,128)} %get-tuple-element.107), calls=%async_computation | async-start | bytes 6324224 | tf_op jit(solution)/shard_map/send_tiles/all_to_all | solution.py:376
  26.8 2.6 %user_tiles.2 = (f32[512,2048]{1,0:T(8,128)S(1)}, bf16[512,2048]{1,0:T(8,128)(2,1)S(1)}) custom-call(s32[8,128]{1,0:T(8,128)S(1)} %copy-done.6, s32[48,128,128]{2,1,0:T(8,128)} %bitcast.5), custom_call_target="tpu_custom_call" | custom-call | flops 1000000000 | bytes 11538432 | tf_op jit(solution)/shard_map/user_tiles/pallas_call | solution.py:295
  33.0 1.6 %collective-permute-start.21 = (f32[256,128]{1,0:T(8,128)S(1)}, f32[256,128]{1,0:T(8,128)S(1)}, u32[]{:S(2)}, u32[]{:S(2)}) collective-permute-start(f32[256,128]{1,0:T(8,128)S(1)} %get-tuple-element.92.own_ref), channel_id=1, source_target_pairs={{0,2},{1,3},{2,0},{3,1},{4,6},{5,7},{6,4},{7,5},{8,10},{9,11},{10,... | collective-permute-start | bytes 393224 | tf_op jit(solution)/shard_map/user_cg/ppermute | solution.py:322
  35.0 4.3 %collective-permute-done.21.other_ref = f32[256,128]{1,0:T(8,128)S(1)} collective-permute-done((f32[256,128]{1,0:T(8,128)S(1)}, f32[256,128]{1,0:T(8,128)S(1)}, u32[]{:S(2)}, u32[]{:S(2)}) %collective-permute-start.21) | collective-permute-done | bytes 131104 | tf_op jit(solution)/shard_map/user_cg/ppermute | solution.py:322
  40.8 1.6 %collective-permute-start.22 = (f32[256,128]{1,0:T(8,128)S(1)}, f32[256,128]{1,0:T(8,128)S(1)}, u32[]{:S(2)}, u32[]{:S(2)}) collective-permute-start(f32[256,128]{1,0:T(8,128)S(1)} %get-tuple-element.94.own_ref), channel_id=1, source_target_pairs={{0,2},{1,3},{2,0},{3,1},{4,6},{5,7},{6,4},{7,5},{8,10},{9,11},{10,... | collective-permute-start | bytes 393224 | tf_op jit(solution)/shard_map/user_cg/ppermute | solution.py:322
  42.4 1.5 %user_cg.10 = (f32[256,128]{1,0:T(8,128)S(1)}, f32[256,128]{1,0:T(8,128)S(1)}) custom-call(f32[256,128]{1,0:T(8,128)S(1)} %get-tuple-element.79.own_ref, f32[256,128]{1,0:T(8,128)S(1)} %collective-permute-done.17.other_ref, f32[512,2048]{1,0:T(8,128)S(1)} %get-tuple-element.80.conf_ref, bf16[2048,256]{1,0:T(8,128)(2,1)S(1)} %get-tuple-element.81.pairs_ref), custom_call_target="tpu_custom_call" | custom-call | flops 805306368 | bytes 5767168 | tf_op jit(solution)/shard_map/user_cg/pallas_call | solution.py:295
  44.5 2.6 %collective-permute-done.22.other_ref = f32[256,128]{1,0:T(8,128)S(1)} collective-permute-done((f32[256,128]{1,0:T(8,128)S(1)}, f32[256,128]{1,0:T(8,128)S(1)}, u32[]{:S(2)}, u32[]{:S(2)}) %collective-permute-start.22) | collective-permute-done | bytes 131104 | tf_op jit(solution)/shard_map/user_cg/ppermute | solution.py:322
  47.1 1.6 %user_cg.14 = (f32[256,128]{1,0:T(8,128)S(1)}, f32[256,128]{1,0:T(8,128)S(1)}, f32[256,128]{1,0:T(8,128)S(1)}, f32[256,128]{1,0:T(8,128)S(1)}) custom-call(f32[256,128]{1,0:T(8,128)S(1)} %get-tuple-element.93.side_ref, f32[256,128]{1,0:T(8,128)S(1)} %get-tuple-element.94.own_ref, f32[256,128]{1,0:T(8,128)S(1)} %collective-permute-done.22.other_ref, ...), custom_call_target="tpu_custom_call" | custom-call | flops 805306368 | bytes 6160384 | tf_op jit(solution)/shard_map/user_cg/pallas_call | solution.py:295
  48.7 1.6 %collective-permute-start.23 = (f32[256,128]{1,0:T(8,128)S(1)}, f32[256,128]{1,0:T(8,128)S(1)}, u32[]{:S(2)}, u32[]{:S(2)}) collective-permute-start(f32[256,128]{1,0:T(8,128)S(1)} %get-tuple-element.98.own_ref), channel_id=1, source_target_pairs={{0,2},{1,3},{2,0},{3,1},{4,6},{5,7},{6,4},{7,5},{8,10},{9,11},{10,... | collective-permute-start | bytes 393224 | tf_op jit(solution)/shard_map/user_cg/ppermute | solution.py:322
  50.2 1.6 %user_cg.11 = (f32[256,128]{1,0:T(8,128)S(1)}, f32[256,128]{1,0:T(8,128)S(1)}, f32[256,128]{1,0:T(8,128)S(1)}, f32[256,128]{1,0:T(8,128)S(1)}) custom-call(f32[256,128]{1,0:T(8,128)S(1)} %get-tuple-element.82.side_ref, f32[256,128]{1,0:T(8,128)S(1)} %get-tuple-element.83.own_ref, f32[256,128]{1,0:T(8,128)S(1)} %collective-permute-done.18.other_ref, ...), custom_call_target="tpu_custom_call" | custom-call | flops 805306368 | bytes 6160384 | tf_op jit(solution)/shard_map/user_cg/pallas_call | solution.py:295
  52.8 1.7 %collective-permute-done.23.other_ref = f32[256,128]{1,0:T(8,128)S(1)} collective-permute-done((f32[256,128]{1,0:T(8,128)S(1)}, f32[256,128]{1,0:T(8,128)S(1)}, u32[]{:S(2)}, u32[]{:S(2)}) %collective-permute-start.23) | collective-permute-done | bytes 131104 | tf_op jit(solution)/shard_map/user_cg/ppermute | solution.py:322
  55.6 1.7 %collective-permute-start.24 = (f32[8,256]{1,0:T(8,128)S(1)}, f32[8,256]{1,0:T(8,128)S(1)}, u32[]{:S(2)}, u32[]{:S(2)}) collective-permute-start(f32[8,256]{1,0:T(8,128)S(1)} %get-tuple-element.102.refs_8_), channel_id=1, source_target_pairs={{0,2},{1,3},{2,0},{3,1},{4,6},{5,7},{6,4},{7,5},{8,10},{9,11},{10,... | collective-permute-start | bytes 24584 | tf_op jit(solution)/shard_map/user_cg/ppermute | solution.py:322
  59.3 2.7 %collective-permute-done.20.refs_4_ = f32[8,256]{1,0:T(8,128)S(1)} collective-permute-done((f32[8,256]{1,0:T(8,128)S(1)}, f32[8,256]{1,0:T(8,128)S(1)}, u32[]{:S(2)}, u32[]{:S(2)}) %collective-permute-start.20) | collective-permute-done | bytes 8224 | tf_op jit(solution)/shard_map/user_cg/ppermute | solution.py:322
  62.4 2.0 %collective-permute-start.29 = (f32[512,128]{1,0:T(8,128)S(1)}, f32[512,128]{1,0:T(8,128)S(1)}, u32[]{:S(2)}, u32[]{:S(2)}) collective-permute-start(f32[512,128]{1,0:T(8,128)S(1)} %get-tuple-element.108.refs_0_), channel_id=1, source_target_pairs={{0,8},{4,12},{8,0},{12,4},{16,24},{20,28},{24,16},{28,20},{1,9},{5... | collective-permute-start | bytes 786440 | tf_op jit(solution)/shard_map/gather_users/ppermute | solution.py:322
  64.4 1.5 %collective-permute-start.27 = (f32[512,128]{1,0:T(8,128)S(1)}, f32[512,128]{1,0:T(8,128)S(1)}, u32[]{:S(2)}, u32[]{:S(2)}) collective-permute-start(f32[512,128]{1,0:T(8,128)S(1)} %get-tuple-element.108.refs_0_), channel_id=1, source_target_pairs={{0,4},{4,0},{8,12},{12,8},{16,20},{20,16},{24,28},{28,24},{1,5},{5... | collective-permute-start | bytes 786440 | tf_op jit(solution)/shard_map/gather_users/ppermute | solution.py:322
  65.9 2.5 %item_tiles.1 = (f32[256,4096]{1,0:T(8,128)S(1)}, bf16[256,4096]{1,0:T(8,128)(2,1)S(1)}) custom-call(s32[4,2,128]{2,1,0:T(2,128)S(1)} %slice.7.lists_ref, s32[4,1544,128]{2,1,0:T(8,128)S(1)} %all-to-all-done.tiles_ref), custom_call_target="tpu_custom_call" | custom-call | flops 1000000000 | bytes 11554816 | tf_op jit(solution)/shard_map/item_tiles/pallas_call | solution.py:295
  68.9 1.9 %collective-permute-start.31 = (f32[512,128]{1,0:T(8,128)S(1)}, f32[512,128]{1,0:T(8,128)S(1)}, u32[]{:S(2)}, u32[]{:S(2)}) collective-permute-start(f32[512,128]{1,0:T(8,128)S(1)} %collective-permute-done.29.refs_4_), channel_id=1, source_target_pairs={{0,4},{4,0},{8,12},{12,8},{16,20},{20,16},{24,28},{28,24},{1,5},{5... | collective-permute-start | bytes 786440 | tf_op jit(solution)/shard_map/gather_users/ppermute | solution.py:322
  72.3 3.0 %collective-permute-done.31.refs_6_ = f32[512,128]{1,0:T(8,128)S(1)} collective-permute-done((f32[512,128]{1,0:T(8,128)S(1)}, f32[512,128]{1,0:T(8,128)S(1)}, u32[]{:S(2)}, u32[]{:S(2)}) %collective-permute-start.31) | collective-permute-done | bytes 262176 | tf_op jit(solution)/shard_map/gather_users/ppermute | solution.py:322
  75.3 1.5 %collective-permute-done.32.refs_7_ = f32[512,128]{1,0:T(8,128)S(1)} collective-permute-done((f32[512,128]{1,0:T(8,128)S(1)}, f32[512,128]{1,0:T(8,128)S(1)}, u32[]{:S(2)}, u32[]{:S(2)}) %collective-permute-start.32) | collective-permute-done | bytes 262176 | tf_op jit(solution)/shard_map/gather_users/ppermute | solution.py:322
  77.7 2.0 %collective-permute-start.37 = (f32[128,128]{1,0:T(8,128)S(1)}, f32[128,128]{1,0:T(8,128)S(1)}, u32[]{:S(2)}, u32[]{:S(2)}) collective-permute-start(f32[128,128]{1,0:T(8,128)S(1)} %get-tuple-element.126.own_ref), channel_id=1, source_target_pairs={{0,16},{4,20},{8,24},{12,28},{16,0},{20,4},{24,8},{28,12},{1,17},{... | collective-permute-start | bytes 196616 | tf_op jit(solution)/shard_map/item_cg/ppermute | solution.py:322
  80.7 3.6 %collective-permute-done.37.other_ref = f32[128,128]{1,0:T(8,128)S(1)} collective-permute-done((f32[128,128]{1,0:T(8,128)S(1)}, f32[128,128]{1,0:T(8,128)S(1)}, u32[]{:S(2)}, u32[]{:S(2)}) %collective-permute-start.37) | collective-permute-done | bytes 65568 | tf_op jit(solution)/shard_map/item_cg/ppermute | solution.py:322
  88.6 1.7 %collective-permute-start.34 = (f32[128,128]{1,0:T(8,128)S(1)}, f32[128,128]{1,0:T(8,128)S(1)}, u32[]{:S(2)}, u32[]{:S(2)}) collective-permute-start(f32[128,128]{1,0:T(8,128)S(1)} %get-tuple-element.117.own_ref), channel_id=1, source_target_pairs={{0,16},{4,20},{8,24},{12,28},{16,0},{20,4},{24,8},{28,12},{1,17},{... | collective-permute-start | bytes 196616 | tf_op jit(solution)/shard_map/item_cg/ppermute | solution.py:322
  90.3 2.2 %collective-permute-done.38.other_ref = f32[128,128]{1,0:T(8,128)S(1)} collective-permute-done((f32[128,128]{1,0:T(8,128)S(1)}, f32[128,128]{1,0:T(8,128)S(1)}, u32[]{:S(2)}, u32[]{:S(2)}) %collective-permute-start.38) | collective-permute-done | bytes 65568 | tf_op jit(solution)/shard_map/item_cg/ppermute | solution.py:322
  92.5 1.5 %item_cg.13 = (f32[128,128]{1,0:T(8,128)S(1)}, f32[128,128]{1,0:T(8,128)S(1)}, f32[128,128]{1,0:T(8,128)S(1)}, f32[128,128]{1,0:T(8,128)S(1)}) custom-call(f32[128,128]{1,0:T(8,128)S(1)} %get-tuple-element.127.side_ref, f32[128,128]{1,0:T(8,128)S(1)} %get-tuple-element.128.own_ref, f32[128,128]{1,0:T(8,128)S(1)} %collective-permute-done.38.other_ref, ...), custom_call_target="tpu_custom_call" | custom-call | flops 805306368 | bytes 6750208 | tf_op jit(solution)/shard_map/item_cg/pallas_call | solution.py:295
  94.1 1.5 %item_cg.10 = (f32[128,128]{1,0:T(8,128)S(1)}, f32[128,128]{1,0:T(8,128)S(1)}, f32[128,128]{1,0:T(8,128)S(1)}, f32[128,128]{1,0:T(8,128)S(1)}) custom-call(f32[128,128]{1,0:T(8,128)S(1)} %get-tuple-element.116.side_ref, f32[128,128]{1,0:T(8,128)S(1)} %get-tuple-element.117.own_ref, f32[128,128]{1,0:T(8,128)S(1)} %collective-permute-done.34.other_ref, ...), custom_call_target="tpu_custom_call" | custom-call | flops 805306368 | bytes 6750208 | tf_op jit(solution)/shard_map/item_cg/pallas_call | solution.py:295
  95.7 3.0 %collective-permute-start.35 = (f32[128,128]{1,0:T(8,128)S(1)}, f32[128,128]{1,0:T(8,128)S(1)}, u32[]{:S(2)}, u32[]{:S(2)}) collective-permute-start(f32[128,128]{1,0:T(8,128)S(1)} %get-tuple-element.121.own_ref), channel_id=1, source_target_pairs={{0,16},{4,20},{8,24},{12,28},{16,0},{20,4},{24,8},{28,12},{1,17},{... | collective-permute-start | bytes 196616 | tf_op jit(solution)/shard_map/item_cg/ppermute | solution.py:322
  102.2 2.7 %collective-permute-start.36 = (f32[8,128]{1,0:T(8,128)S(1)}, f32[8,128]{1,0:T(8,128)S(1)}, u32[]{:S(2)}, u32[]{:S(2)}) collective-permute-start(f32[8,128]{1,0:T(8,128)S(1)} %get-tuple-element.125.refs_3_), channel_id=1, source_target_pairs={{0,16},{4,20},{8,24},{12,28},{16,0},{20,4},{24,8},{28,12},{1,17},{... | collective-permute-start | bytes 12296 | tf_op jit(solution)/shard_map/item_cg/ppermute | solution.py:322
  (89 shorter events, 32.7 us)
Async XLA Ops:
  0.6 9.5 %collective-permute-start.1 = (f32[128,128]{1,0:T(8,128)}, f32[128,128]{1,0:T(8,128)S(1)}, u32[]{:S(2)}, u32[]{:S(2)}) collective-permute-start(f32[128,128]{1,0:T(8,128)} %refs_0_.1), channel_id=1, source_target_pairs={{0,8},{4,12},{8,0},{12,4},{16,24},{20,28},{24,16},{28,20},{1,9},{5... | collective-permute-start | bytes 196616 | tf_op jit(solution)/shard_map/gather_items/ppermute | solution.py:322
  3.7 7.5 %collective-permute-start.3 = (f32[128,128]{1,0:T(8,128)}, f32[128,128]{1,0:T(8,128)S(1)}, u32[]{:S(2)}, u32[]{:S(2)}) collective-permute-start(f32[128,128]{1,0:T(8,128)} %refs_0_.1), channel_id=1, source_target_pairs={{0,16},{4,20},{8,24},{12,28},{16,0},{20,4},{24,8},{28,12},{1,17},{... | collective-permute-start | bytes 196616 | tf_op jit(solution)/shard_map/gather_items/ppermute | solution.py:322
  6.3 6.4 %collective-permute-start.5 = (f32[128,128]{1,0:T(8,128)}, f32[128,128]{1,0:T(8,128)S(1)}, u32[]{:S(2)}, u32[]{:S(2)}) collective-permute-start(f32[128,128]{1,0:T(8,128)} %refs_0_.1), channel_id=1, source_target_pairs={{0,24},{4,28},{8,16},{12,20},{16,8},{20,12},{24,0},{28,4},{1,25},{... | collective-permute-start | bytes 196616 | tf_op jit(solution)/shard_map/gather_items/ppermute | solution.py:322
  6.3 13.5 %collective-permute-start = (f32[128,128]{1,0:T(8,128)}, f32[128,128]{1,0:T(8,128)S(1)}, u32[]{:S(2)}, u32[]{:S(2)}) collective-permute-start(f32[128,128]{1,0:T(8,128)} %refs_0_.1), channel_id=1, source_target_pairs={{0,4},{4,0},{8,12},{12,8},{16,20},{20,16},{24,28},{28,24},{1,5},{5... | collective-permute-start | bytes 196616 | tf_op jit(solution)/shard_map/gather_items/ppermute | solution.py:322
  10.1 4.7 %collective-permute-start.2 = (f32[128,128]{1,0:T(8,128)S(1)}, f32[128,128]{1,0:T(8,128)S(1)}, u32[]{:S(2)}, u32[]{:S(2)}) collective-permute-start(f32[128,128]{1,0:T(8,128)S(1)} %collective-permute-done.1.refs_2_), channel_id=1, source_target_pairs={{0,4},{4,0},{8,12},{12,8},{16,20},{20,16},{24,28},{28,24},{1,5},{5... | collective-permute-start | bytes 196616 | tf_op jit(solution)/shard_map/gather_items/ppermute | solution.py:322
  11.2 8.6 %collective-permute-start.4 = (f32[128,128]{1,0:T(8,128)S(1)}, f32[128,128]{1,0:T(8,128)S(1)}, u32[]{:S(2)}, u32[]{:S(2)}) collective-permute-start(f32[128,128]{1,0:T(8,128)S(1)} %collective-permute-done.3.refs_4_), channel_id=1, source_target_pairs={{0,4},{4,0},{8,12},{12,8},{16,20},{20,16},{24,28},{28,24},{1,5},{5... | collective-permute-start | bytes 196616 | tf_op jit(solution)/shard_map/gather_items/ppermute | solution.py:322
  12.7 7.1 %collective-permute-start.6 = (f32[128,128]{1,0:T(8,128)S(1)}, f32[128,128]{1,0:T(8,128)S(1)}, u32[]{:S(2)}, u32[]{:S(2)}) collective-permute-start(f32[128,128]{1,0:T(8,128)S(1)} %collective-permute-done.5.refs_6_), channel_id=1, source_target_pairs={{0,4},{4,0},{8,12},{12,8},{16,20},{20,16},{24,28},{28,24},{1,5},{5... | collective-permute-start | bytes 196616 | tf_op jit(solution)/shard_map/gather_items/ppermute | solution.py:322
  21.1 41.3 %all-to-all-start = ((s32[4,1544,128]{2,1,0:T(8,128)}), s32[4,1544,128]{2,1,0:T(8,128)S(1)}, u32[]{:S(2)}, u32[]{:S(2)}) async-start(s32[4,1544,128]{2,1,0:T(8,128)} %get-tuple-element.107), calls=%async_computation | async-start | bytes 6324224 | tf_op jit(solution)/shard_map/send_tiles/all_to_all | solution.py:376
  25.0 5.6 %collective-permute-start.16 = (s32[48,64,128]{2,1,0:T(8,128)}, s32[48,64,128]{2,1,0:T(8,128)S(1)}, u32[]{:S(2)}, u32[]{:S(2)}) collective-permute-start(s32[48,64,128]{2,1,0:T(8,128)} %get-tuple-element.74), channel_id=1, source_target_pairs={{0,1},{1,0},{2,3},{3,2},{4,5},{5,4},{6,7},{7,6},{8,9},{9,8},{10,11... | collective-permute-start | bytes 4718600 | tf_op jit(solution)/shard_map/pack_tiles/ppermute | solution.py:322
  25.6 4.4 %collective-permute-start.7 = (f32[128,128]{1,0:T(8,128)S(1)}, f32[128,128]{1,0:T(8,128)S(1)}, u32[]{:S(2)}, u32[]{:S(2)}) collective-permute-start(f32[128,128]{1,0:T(8,128)S(1)} %copy-done), channel_id=1, source_target_pairs={{0,1},{1,0},{2,3},{3,2},{4,5},{5,4},{6,7},{7,6},{8,9},{9,8},{10,11... | collective-permute-start | bytes 196616 | tf_op jit(solution)/shard_map/gather_items/ppermute | solution.py:322
  25.6 4.4 %collective-permute-start.11 = (f32[128,128]{1,0:T(8,128)S(1)}, f32[128,128]{1,0:T(8,128)S(1)}, u32[]{:S(2)}, u32[]{:S(2)}) collective-permute-start(f32[128,128]{1,0:T(8,128)S(1)} %collective-permute-done.3.refs_4_), channel_id=1, source_target_pairs={{0,1},{1,0},{2,3},{3,2},{4,5},{5,4},{6,7},{7,6},{8,9},{9,8},{10,11... | collective-permute-start | bytes 196616 | tf_op jit(solution)/shard_map/gather_items/ppermute | solution.py:322
  26.1 4.4 %collective-permute-start.13 = (f32[128,128]{1,0:T(8,128)S(1)}, f32[128,128]{1,0:T(8,128)S(1)}, u32[]{:S(2)}, u32[]{:S(2)}) collective-permute-start(f32[128,128]{1,0:T(8,128)S(1)} %collective-permute-done.5.refs_6_), channel_id=1, source_target_pairs={{0,1},{1,0},{2,3},{3,2},{4,5},{5,4},{6,7},{7,6},{8,9},{9,8},{10,11... | collective-permute-start | bytes 196616 | tf_op jit(solution)/shard_map/gather_items/ppermute | solution.py:322
  33.0 6.4 %collective-permute-start.21 = (f32[256,128]{1,0:T(8,128)S(1)}, f32[256,128]{1,0:T(8,128)S(1)}, u32[]{:S(2)}, u32[]{:S(2)}) collective-permute-start(f32[256,128]{1,0:T(8,128)S(1)} %get-tuple-element.92.own_ref), channel_id=1, source_target_pairs={{0,2},{1,3},{2,0},{3,1},{4,6},{5,7},{6,4},{7,5},{8,10},{9,11},{10,... | collective-permute-start | bytes 393224 | tf_op jit(solution)/shard_map/user_cg/ppermute | solution.py:322
  34.5 7.9 %collective-permute-start.17 = (f32[256,128]{1,0:T(8,128)S(1)}, f32[256,128]{1,0:T(8,128)S(1)}, u32[]{:S(2)}, u32[]{:S(2)}) collective-permute-start(f32[256,128]{1,0:T(8,128)S(1)} %get-tuple-element.79.own_ref), channel_id=1, source_target_pairs={{0,2},{1,3},{2,0},{3,1},{4,6},{5,7},{6,4},{7,5},{8,10},{9,11},{10,... | collective-permute-start | bytes 393224 | tf_op jit(solution)/shard_map/user_cg/ppermute | solution.py:322
  40.8 6.2 %collective-permute-start.22 = (f32[256,128]{1,0:T(8,128)S(1)}, f32[256,128]{1,0:T(8,128)S(1)}, u32[]{:S(2)}, u32[]{:S(2)}) collective-permute-start(f32[256,128]{1,0:T(8,128)S(1)} %get-tuple-element.94.own_ref), channel_id=1, source_target_pairs={{0,2},{1,3},{2,0},{3,1},{4,6},{5,7},{6,4},{7,5},{8,10},{9,11},{10,... | collective-permute-start | bytes 393224 | tf_op jit(solution)/shard_map/user_cg/ppermute | solution.py:322
  43.9 6.4 %collective-permute-start.18 = (f32[256,128]{1,0:T(8,128)S(1)}, f32[256,128]{1,0:T(8,128)S(1)}, u32[]{:S(2)}, u32[]{:S(2)}) collective-permute-start(f32[256,128]{1,0:T(8,128)S(1)} %get-tuple-element.83.own_ref), channel_id=1, source_target_pairs={{0,2},{1,3},{2,0},{3,1},{4,6},{5,7},{6,4},{7,5},{8,10},{9,11},{10,... | collective-permute-start | bytes 393224 | tf_op jit(solution)/shard_map/user_cg/ppermute | solution.py:322
  48.7 5.9 %collective-permute-start.23 = (f32[256,128]{1,0:T(8,128)S(1)}, f32[256,128]{1,0:T(8,128)S(1)}, u32[]{:S(2)}, u32[]{:S(2)}) collective-permute-start(f32[256,128]{1,0:T(8,128)S(1)} %get-tuple-element.98.own_ref), channel_id=1, source_target_pairs={{0,2},{1,3},{2,0},{3,1},{4,6},{5,7},{6,4},{7,5},{8,10},{9,11},{10,... | collective-permute-start | bytes 393224 | tf_op jit(solution)/shard_map/user_cg/ppermute | solution.py:322
  51.9 5.4 %collective-permute-start.19 = (f32[256,128]{1,0:T(8,128)S(1)}, f32[256,128]{1,0:T(8,128)S(1)}, u32[]{:S(2)}, u32[]{:S(2)}) collective-permute-start(f32[256,128]{1,0:T(8,128)S(1)} %get-tuple-element.87.own_ref), channel_id=1, source_target_pairs={{0,2},{1,3},{2,0},{3,1},{4,6},{5,7},{6,4},{7,5},{8,10},{9,11},{10,... | collective-permute-start | bytes 393224 | tf_op jit(solution)/shard_map/user_cg/ppermute | solution.py:322
  62.4 6.4 %collective-permute-start.29 = (f32[512,128]{1,0:T(8,128)S(1)}, f32[512,128]{1,0:T(8,128)S(1)}, u32[]{:S(2)}, u32[]{:S(2)}) collective-permute-start(f32[512,128]{1,0:T(8,128)S(1)} %get-tuple-element.108.refs_0_), channel_id=1, source_target_pairs={{0,8},{4,12},{8,0},{12,4},{16,24},{20,28},{24,16},{28,20},{1,9},{5... | collective-permute-start | bytes 786440 | tf_op jit(solution)/shard_map/gather_users/ppermute | solution.py:322
  64.4 7.8 %collective-permute-start.27 = (f32[512,128]{1,0:T(8,128)S(1)}, f32[512,128]{1,0:T(8,128)S(1)}, u32[]{:S(2)}, u32[]{:S(2)}) collective-permute-start(f32[512,128]{1,0:T(8,128)S(1)} %get-tuple-element.108.refs_0_), channel_id=1, source_target_pairs={{0,4},{4,0},{8,12},{12,8},{16,20},{20,16},{24,28},{28,24},{1,5},{5... | collective-permute-start | bytes 786440 | tf_op jit(solution)/shard_map/gather_users/ppermute | solution.py:322
  68.9 6.4 %collective-permute-start.31 = (f32[512,128]{1,0:T(8,128)S(1)}, f32[512,128]{1,0:T(8,128)S(1)}, u32[]{:S(2)}, u32[]{:S(2)}) collective-permute-start(f32[512,128]{1,0:T(8,128)S(1)} %collective-permute-done.29.refs_4_), channel_id=1, source_target_pairs={{0,4},{4,0},{8,12},{12,8},{16,20},{20,16},{24,28},{28,24},{1,5},{5... | collective-permute-start | bytes 786440 | tf_op jit(solution)/shard_map/gather_users/ppermute | solution.py:322
  70.8 4.5 %collective-permute-start.26 = (f32[512,128]{1,0:T(8,128)S(1)}, f32[512,128]{1,0:T(8,128)S(1)}, u32[]{:S(2)}, u32[]{:S(2)}) collective-permute-start(f32[512,128]{1,0:T(8,128)S(1)} %get-tuple-element.108.refs_0_), channel_id=1, source_target_pairs={{0,1},{1,0},{2,3},{3,2},{4,5},{5,4},{6,7},{7,6},{8,9},{9,8},{10,11... | collective-permute-start | bytes 786440 | tf_op jit(solution)/shard_map/gather_users/ppermute | solution.py:322
  70.8 4.5 %collective-permute-start.30 = (f32[512,128]{1,0:T(8,128)S(1)}, f32[512,128]{1,0:T(8,128)S(1)}, u32[]{:S(2)}, u32[]{:S(2)}) collective-permute-start(f32[512,128]{1,0:T(8,128)S(1)} %collective-permute-done.29.refs_4_), channel_id=1, source_target_pairs={{0,1},{1,0},{2,3},{3,2},{4,5},{5,4},{6,7},{7,6},{8,9},{9,8},{10,11... | collective-permute-start | bytes 786440 | tf_op jit(solution)/shard_map/gather_users/ppermute | solution.py:322
  77.7 6.6 %collective-permute-start.37 = (f32[128,128]{1,0:T(8,128)S(1)}, f32[128,128]{1,0:T(8,128)S(1)}, u32[]{:S(2)}, u32[]{:S(2)}) collective-permute-start(f32[128,128]{1,0:T(8,128)S(1)} %get-tuple-element.126.own_ref), channel_id=1, source_target_pairs={{0,16},{4,20},{8,24},{12,28},{16,0},{20,4},{24,8},{28,12},{1,17},{... | collective-permute-start | bytes 196616 | tf_op jit(solution)/shard_map/item_cg/ppermute | solution.py:322
  79.7 25.2 %collective-permute-start.25 = (f32[128,128]{1,0:T(8,128)S(1)}, f32[128,128]{1,0:T(8,128)S(1)}, u32[]{:S(2)}, u32[]{:S(2)}) collective-permute-start(f32[128,128]{1,0:T(8,128)S(1)} %get-tuple-element.104), channel_id=1, source_target_pairs={{0,1},{1,0},{2,3},{3,2},{4,5},{5,4},{6,7},{7,6},{8,9},{9,8},{10,11... | collective-permute-start | bytes 196616 | tf_op jit(solution)/shard_map/user_cg/ppermute | solution.py:322
  79.7 7.5 %collective-permute-start.33 = (f32[128,128]{1,0:T(8,128)S(1)}, f32[128,128]{1,0:T(8,128)S(1)}, u32[]{:S(2)}, u32[]{:S(2)}) collective-permute-start(f32[128,128]{1,0:T(8,128)S(1)} %get-tuple-element.113.own_ref), channel_id=1, source_target_pairs={{0,16},{4,20},{8,24},{12,28},{16,0},{20,4},{24,8},{28,12},{1,17},{... | collective-permute-start | bytes 196616 | tf_op jit(solution)/shard_map/item_cg/ppermute | solution.py:322
  85.8 6.7 %collective-permute-start.38 = (f32[128,128]{1,0:T(8,128)S(1)}, f32[128,128]{1,0:T(8,128)S(1)}, u32[]{:S(2)}, u32[]{:S(2)}) collective-permute-start(f32[128,128]{1,0:T(8,128)S(1)} %get-tuple-element.128.own_ref), channel_id=1, source_target_pairs={{0,16},{4,20},{8,24},{12,28},{16,0},{20,4},{24,8},{28,12},{1,17},{... | collective-permute-start | bytes 196616 | tf_op jit(solution)/shard_map/item_cg/ppermute | solution.py:322
  88.6 5.5 %collective-permute-start.34 = (f32[128,128]{1,0:T(8,128)S(1)}, f32[128,128]{1,0:T(8,128)S(1)}, u32[]{:S(2)}, u32[]{:S(2)}) collective-permute-start(f32[128,128]{1,0:T(8,128)S(1)} %get-tuple-element.117.own_ref), channel_id=1, source_target_pairs={{0,16},{4,20},{8,24},{12,28},{16,0},{20,4},{24,8},{28,12},{1,17},{... | collective-permute-start | bytes 196616 | tf_op jit(solution)/shard_map/item_cg/ppermute | solution.py:322
  94.0 5.8 %collective-permute-start.39 = (f32[128,128]{1,0:T(8,128)S(1)}, f32[128,128]{1,0:T(8,128)S(1)}, u32[]{:S(2)}, u32[]{:S(2)}) collective-permute-start(f32[128,128]{1,0:T(8,128)S(1)} %get-tuple-element.132.own_ref), channel_id=1, source_target_pairs={{0,16},{4,20},{8,24},{12,28},{16,0},{20,4},{24,8},{28,12},{1,17},{... | collective-permute-start | bytes 196616 | tf_op jit(solution)/shard_map/item_cg/ppermute | solution.py:322
  95.7 5.6 %collective-permute-start.35 = (f32[128,128]{1,0:T(8,128)S(1)}, f32[128,128]{1,0:T(8,128)S(1)}, u32[]{:S(2)}, u32[]{:S(2)}) collective-permute-start(f32[128,128]{1,0:T(8,128)S(1)} %get-tuple-element.121.own_ref), channel_id=1, source_target_pairs={{0,16},{4,20},{8,24},{12,28},{16,0},{20,4},{24,8},{28,12},{1,17},{... | collective-permute-start | bytes 196616 | tf_op jit(solution)/shard_map/item_cg/ppermute | solution.py:322
  100.8 4.7 %collective-permute-start.40 = (f32[8,128]{1,0:T(8,128)S(1)}, f32[8,128]{1,0:T(8,128)S(1)}, u32[]{:S(2)}, u32[]{:S(2)}) collective-permute-start(f32[8,128]{1,0:T(8,128)S(1)} %get-tuple-element.136.refs_8_), channel_id=1, source_target_pairs={{0,16},{4,20},{8,24},{12,28},{16,0},{20,4},{24,8},{28,12},{1,17},{... | collective-permute-start | bytes 12296 | tf_op jit(solution)/shard_map/item_cg/ppermute | solution.py:322
  102.2 4.6 %collective-permute-start.36 = (f32[8,128]{1,0:T(8,128)S(1)}, f32[8,128]{1,0:T(8,128)S(1)}, u32[]{:S(2)}, u32[]{:S(2)}) collective-permute-start(f32[8,128]{1,0:T(8,128)S(1)} %get-tuple-element.125.refs_3_), channel_id=1, source_target_pairs={{0,16},{4,20},{8,24},{12,28},{16,0},{20,4},{24,8},{28,12},{1,17},{... | collective-permute-start | bytes 12296 | tf_op jit(solution)/shard_map/item_cg/ppermute | solution.py:322
  (17 other events, 54.0 us)

commit v7 on v6

--- a/solution.py
+++ b/solution.py
@@ -104,6 +104,7 @@
     ]
     for copy in taken:
         copy.start()
+    rows = pl.ds(pl.multiple_of((1 - core) * half, half), half)
     copies = []
     for owner in range(near):
         target = send_ref.at[owner, 2 * slots * block :, :]
@@ -116,9 +117,13 @@
         taken[slot].wait()
         copies.append(pltpu.make_async_copy(held.at[slot], target, sems.at[len(copies)]))
         copies[-1].start()
-    rows = pl.ds(pl.multiple_of((1 - core) * half, half), half)
-    copies.append(pltpu.make_async_copy(held.at[:, rows, :], given_ref, sems.at[len(copies)]))
-    copies[-1].start()
+        if (slot + 1) % owners == 0:
+            slots_in = pl.ds(slot + 1 - owners, owners)
+            part = pltpu.make_async_copy(
+                held.at[slots_in, rows, :], given_ref.at[slots_in], sems.at[len(copies)]
+            )
+            copies.append(part)
+            part.start()
     for copy in copies:
         copy.wait()
 
@@ -365,7 +370,7 @@
             scratch=(
                 pltpu.VMEM(conf.shape, jnp.int32),
                 pltpu.SemaphoreType.DMA((slot_total,)),
-                pltpu.SemaphoreType.DMA((slot_total + 1 + near,)),
+                pltpu.SemaphoreType.DMA((slot_total + slots + near,)),
             ),
         )
         other_named = swap(named, "item", 1)

time: 109 us -> 109 us (level)
  no operation moved by 1% of the time
where the time goes in v7:
time: 109 us; the launch traced here: 107 us
  starting transfers between devices  43.2 us (40%)
  Pallas kernels  30.6 us (28%)
  waiting for transfers between devices  28.7 us (26%)
  local copies, waits for them, and re-layouts  1.93 us (2%)
  between operations  1.6 us (1%)
  other arithmetic  1.38 us (1%)
    ppermute x41, starting transfers between devices, swap(): lax.ppermute(value, axis, [(place, place ^ mask) for place in range(size)])  39.3 us
    pallas_call x21, Pallas kernels, call(): pl.pallas_call(kernel, out_shape=tuple(outs), in_specs=[pl.BlockSpec(memo...  30.6 us
    ppermute x41, waiting for transfers between devices, swap(): lax.ppermute(value, axis, [(place, place ^ mask) for place in range(size)])  28.7 us
    all_to_all x1, starting transfers between devices, dense_shards(): lax.all_to_all(after(packed, *own_items), 'user', 0, 0, tiled=True, axis_...  3.83 us
  transfers between devices with their start and end apart: 42, of which 17 were waited for; matrix products, arithmetic and copies ran while one was open for 1% of the time, Pallas kernels for 27%

profile of v7, /device:TPU:0, one launch (start us, length us, event | category | flops | bytes accessed | tf_op | source)
XLA Modules:
  0.0 107.4 jit_solution(16277925667360933873)
XLA Ops:
  0.6 3.1 %collective-permute-start.1 = (f32[128,128]{1,0:T(8,128)}, f32[128,128]{1,0:T(8,128)S(1)}, u32[]{:S(2)}, u32[]{:S(2)}) collective-permute-start(f32[128,128]{1,0:T(8,128)} %refs_0_.1), channel_id=1, source_target_pairs={{0,8},{4,12},{8,0},{12,4},{16,24},{20,28},{24,16},{28,20},{1,9},{5... | collective-permute-start | bytes 196616 | tf_op jit(solution)/shard_map/gather_items/ppermute | solution.py:327
  3.7 2.6 %collective-permute-start.3 = (f32[128,128]{1,0:T(8,128)}, f32[128,128]{1,0:T(8,128)S(1)}, u32[]{:S(2)}, u32[]{:S(2)}) collective-permute-start(f32[128,128]{1,0:T(8,128)} %refs_0_.1), channel_id=1, source_target_pairs={{0,16},{4,20},{8,24},{12,28},{16,0},{20,4},{24,8},{28,12},{1,17},{... | collective-permute-start | bytes 196616 | tf_op jit(solution)/shard_map/gather_items/ppermute | solution.py:327
  6.3 1.7 %collective-permute-start = (f32[128,128]{1,0:T(8,128)}, f32[128,128]{1,0:T(8,128)S(1)}, u32[]{:S(2)}, u32[]{:S(2)}) collective-permute-start(f32[128,128]{1,0:T(8,128)} %refs_0_.1), channel_id=1, source_target_pairs={{0,4},{4,0},{8,12},{12,8},{16,20},{20,16},{24,28},{28,24},{1,5},{5... | collective-permute-start | bytes 196616 | tf_op jit(solution)/shard_map/gather_items/ppermute | solution.py:327
  11.2 1.5 %collective-permute-start.4 = (f32[128,128]{1,0:T(8,128)S(1)}, f32[128,128]{1,0:T(8,128)S(1)}, u32[]{:S(2)}, u32[]{:S(2)}) collective-permute-start(f32[128,128]{1,0:T(8,128)S(1)} %collective-permute-done.3.refs_4_), channel_id=1, source_target_pairs={{0,4},{4,0},{8,12},{12,8},{16,20},{20,16},{24,28},{28,24},{1,5},{5... | collective-permute-start | bytes 196616 | tf_op jit(solution)/shard_map/gather_items/ppermute | solution.py:327
  14.8 4.7 %pack_tiles.1 = (s32[48,64,128]{2,1,0:T(8,128)}, s32[4,1544,128]{2,1,0:T(8,128)}) custom-call(s32[8,128]{1,0:T(8,128)S(1)} %pad_add_fusion.ids_ref.named_ref, s32[48,128,128]{2,1,0:T(8,128)} %bitcast.4, s32[8,128]{1,0:T(8,128)S(1)} %pad_add_fusion.ids_ref.named_ref), custom_call_target="tpu_custom_call" | custom-call | bytes 7888896 | tf_op jit(solution)/shard_map/pack_tiles/pallas_call | solution.py:300
  20.8 3.8 %all-to-all-start = ((s32[4,1544,128]{2,1,0:T(8,128)}), s32[4,1544,128]{2,1,0:T(8,128)S(1)}, u32[]{:S(2)}, u32[]{:S(2)}) async-start(s32[4,1544,128]{2,1,0:T(8,128)} %get-tuple-element.107), calls=%async_computation | async-start | bytes 6324224 | tf_op jit(solution)/shard_map/send_tiles/all_to_all | solution.py:381
  26.5 2.6 %user_tiles.2 = (f32[512,2048]{1,0:T(8,128)S(1)}, bf16[512,2048]{1,0:T(8,128)(2,1)S(1)}) custom-call(s32[8,128]{1,0:T(8,128)S(1)} %copy-done.6, s32[48,128,128]{2,1,0:T(8,128)} %bitcast.5), custom_call_target="tpu_custom_call" | custom-call | flops 1000000000 | bytes 11538432 | tf_op jit(solution)/shard_map/user_tiles/pallas_call | solution.py:300
  32.6 1.6 %collective-permute-start.21 = (f32[256,128]{1,0:T(8,128)S(1)}, f32[256,128]{1,0:T(8,128)S(1)}, u32[]{:S(2)}, u32[]{:S(2)}) collective-permute-start(f32[256,128]{1,0:T(8,128)S(1)} %get-tuple-element.92.own_ref), channel_id=1, source_target_pairs={{0,2},{1,3},{2,0},{3,1},{4,6},{5,7},{6,4},{7,5},{8,10},{9,11},{10,... | collective-permute-start | bytes 393224 | tf_op jit(solution)/shard_map/user_cg/ppermute | solution.py:327
  34.7 4.3 %collective-permute-done.21.other_ref = f32[256,128]{1,0:T(8,128)S(1)} collective-permute-done((f32[256,128]{1,0:T(8,128)S(1)}, f32[256,128]{1,0:T(8,128)S(1)}, u32[]{:S(2)}, u32[]{:S(2)}) %collective-permute-start.21) | collective-permute-done | bytes 131104 | tf_op jit(solution)/shard_map/user_cg/ppermute | solution.py:327
  39.0 1.5 %user_cg.13 = (f32[256,128]{1,0:T(8,128)S(1)}, f32[256,128]{1,0:T(8,128)S(1)}) custom-call(f32[256,128]{1,0:T(8,128)S(1)} %get-tuple-element.92.own_ref, f32[256,128]{1,0:T(8,128)S(1)} %collective-permute-done.21.other_ref, f32[512,2048]{1,0:T(8,128)S(1)} %get-tuple-element.80.conf_ref, bf16[2048,256]{1,0:T(8,128)(2,1)S(1)} %get-tuple-element.81.pairs_ref), custom_call_target="tpu_custom_call" | custom-call | flops 805306368 | bytes 5767168 | tf_op jit(solution)/shard_map/user_cg/pallas_call | solution.py:300
  40.5 1.6 %collective-permute-start.22 = (f32[256,128]{1,0:T(8,128)S(1)}, f32[256,128]{1,0:T(8,128)S(1)}, u32[]{:S(2)}, u32[]{:S(2)}) collective-permute-start(f32[256,128]{1,0:T(8,128)S(1)} %get-tuple-element.94.own_ref), channel_id=1, source_target_pairs={{0,2},{1,3},{2,0},{3,1},{4,6},{5,7},{6,4},{7,5},{8,10},{9,11},{10,... | collective-permute-start | bytes 393224 | tf_op jit(solution)/shard_map/user_cg/ppermute | solution.py:327
  42.0 1.5 %user_cg.10 = (f32[256,128]{1,0:T(8,128)S(1)}, f32[256,128]{1,0:T(8,128)S(1)}) custom-call(f32[256,128]{1,0:T(8,128)S(1)} %get-tuple-element.79.own_ref, f32[256,128]{1,0:T(8,128)S(1)} %collective-permute-done.17.other_ref, f32[512,2048]{1,0:T(8,128)S(1)} %get-tuple-element.80.conf_ref, bf16[2048,256]{1,0:T(8,128)(2,1)S(1)} %get-tuple-element.81.pairs_ref), custom_call_target="tpu_custom_call" | custom-call | flops 805306368 | bytes 5767168 | tf_op jit(solution)/shard_map/user_cg/pallas_call | solution.py:300
  44.1 2.6 %collective-permute-done.22.other_ref = f32[256,128]{1,0:T(8,128)S(1)} collective-permute-done((f32[256,128]{1,0:T(8,128)S(1)}, f32[256,128]{1,0:T(8,128)S(1)}, u32[]{:S(2)}, u32[]{:S(2)}) %collective-permute-start.22) | collective-permute-done | bytes 131104 | tf_op jit(solution)/shard_map/user_cg/ppermute | solution.py:327
  46.7 1.6 %user_cg.14 = (f32[256,128]{1,0:T(8,128)S(1)}, f32[256,128]{1,0:T(8,128)S(1)}, f32[256,128]{1,0:T(8,128)S(1)}, f32[256,128]{1,0:T(8,128)S(1)}) custom-call(f32[256,128]{1,0:T(8,128)S(1)} %get-tuple-element.93.side_ref, f32[256,128]{1,0:T(8,128)S(1)} %get-tuple-element.94.own_ref, f32[256,128]{1,0:T(8,128)S(1)} %collective-permute-done.22.other_ref, ...), custom_call_target="tpu_custom_call" | custom-call | flops 805306368 | bytes 6160384 | tf_op jit(solution)/shard_map/user_cg/pallas_call | solution.py:300
  48.3 1.6 %collective-permute-start.23 = (f32[256,128]{1,0:T(8,128)S(1)}, f32[256,128]{1,0:T(8,128)S(1)}, u32[]{:S(2)}, u32[]{:S(2)}) collective-permute-start(f32[256,128]{1,0:T(8,128)S(1)} %get-tuple-element.98.own_ref), channel_id=1, source_target_pairs={{0,2},{1,3},{2,0},{3,1},{4,6},{5,7},{6,4},{7,5},{8,10},{9,11},{10,... | collective-permute-start | bytes 393224 | tf_op jit(solution)/shard_map/user_cg/ppermute | solution.py:327
  49.9 1.6 %user_cg.11 = (f32[256,128]{1,0:T(8,128)S(1)}, f32[256,128]{1,0:T(8,128)S(1)}, f32[256,128]{1,0:T(8,128)S(1)}, f32[256,128]{1,0:T(8,128)S(1)}) custom-call(f32[256,128]{1,0:T(8,128)S(1)} %get-tuple-element.82.side_ref, f32[256,128]{1,0:T(8,128)S(1)} %get-tuple-element.83.own_ref, f32[256,128]{1,0:T(8,128)S(1)} %collective-permute-done.18.other_ref, ...), custom_call_target="tpu_custom_call" | custom-call | flops 805306368 | bytes 6160384 | tf_op jit(solution)/shard_map/user_cg/pallas_call | solution.py:300
  52.4 1.7 %collective-permute-done.23.other_ref = f32[256,128]{1,0:T(8,128)S(1)} collective-permute-done((f32[256,128]{1,0:T(8,128)S(1)}, f32[256,128]{1,0:T(8,128)S(1)}, u32[]{:S(2)}, u32[]{:S(2)}) %collective-permute-start.23) | collective-permute-done | bytes 131104 | tf_op jit(solution)/shard_map/user_cg/ppermute | solution.py:327
  55.2 1.8 %collective-permute-start.24 = (f32[8,256]{1,0:T(8,128)S(1)}, f32[8,256]{1,0:T(8,128)S(1)}, u32[]{:S(2)}, u32[]{:S(2)}) collective-permute-start(f32[8,256]{1,0:T(8,128)S(1)} %get-tuple-element.102.refs_8_), channel_id=1, source_target_pairs={{0,2},{1,3},{2,0},{3,1},{4,6},{5,7},{6,4},{7,5},{8,10},{9,11},{10,... | collective-permute-start | bytes 24584 | tf_op jit(solution)/shard_map/user_cg/ppermute | solution.py:327
  58.9 2.8 %collective-permute-done.20.refs_4_ = f32[8,256]{1,0:T(8,128)S(1)} collective-permute-done((f32[8,256]{1,0:T(8,128)S(1)}, f32[8,256]{1,0:T(8,128)S(1)}, u32[]{:S(2)}, u32[]{:S(2)}) %collective-permute-start.20) | collective-permute-done | bytes 8224 | tf_op jit(solution)/shard_map/user_cg/ppermute | solution.py:327
  62.1 2.0 %collective-permute-start.29 = (f32[512,128]{1,0:T(8,128)S(1)}, f32[512,128]{1,0:T(8,128)S(1)}, u32[]{:S(2)}, u32[]{:S(2)}) collective-permute-start(f32[512,128]{1,0:T(8,128)S(1)} %get-tuple-element.108.refs_0_), channel_id=1, source_target_pairs={{0,8},{4,12},{8,0},{12,4},{16,24},{20,28},{24,16},{28,20},{1,9},{5... | collective-permute-start | bytes 786440 | tf_op jit(solution)/shard_map/gather_users/ppermute | solution.py:327
  65.5 2.6 %item_tiles.1 = (f32[256,4096]{1,0:T(8,128)S(1)}, bf16[256,4096]{1,0:T(8,128)(2,1)S(1)}) custom-call(s32[4,2,128]{2,1,0:T(2,128)S(1)} %slice.7.lists_ref, s32[4,1544,128]{2,1,0:T(8,128)S(1)} %all-to-all-done.tiles_ref), custom_call_target="tpu_custom_call" | custom-call | flops 1000000000 | bytes 11554816 | tf_op jit(solution)/shard_map/item_tiles/pallas_call | solution.py:300
  68.5 1.9 %collective-permute-start.31 = (f32[512,128]{1,0:T(8,128)S(1)}, f32[512,128]{1,0:T(8,128)S(1)}, u32[]{:S(2)}, u32[]{:S(2)}) collective-permute-start(f32[512,128]{1,0:T(8,128)S(1)} %collective-permute-done.29.refs_4_), channel_id=1, source_target_pairs={{0,4},{4,0},{8,12},{12,8},{16,20},{20,16},{24,28},{28,24},{1,5},{5... | collective-permute-start | bytes 786440 | tf_op jit(solution)/shard_map/gather_users/ppermute | solution.py:327
  71.9 3.0 %collective-permute-done.31.refs_6_ = f32[512,128]{1,0:T(8,128)S(1)} collective-permute-done((f32[512,128]{1,0:T(8,128)S(1)}, f32[512,128]{1,0:T(8,128)S(1)}, u32[]{:S(2)}, u32[]{:S(2)}) %collective-permute-start.31) | collective-permute-done | bytes 262176 | tf_op jit(solution)/shard_map/gather_users/ppermute | solution.py:327
  74.9 1.5 %collective-permute-done.32.refs_7_ = f32[512,128]{1,0:T(8,128)S(1)} collective-permute-done((f32[512,128]{1,0:T(8,128)S(1)}, f32[512,128]{1,0:T(8,128)S(1)}, u32[]{:S(2)}, u32[]{:S(2)}) %collective-permute-start.32) | collective-permute-done | bytes 262176 | tf_op jit(solution)/shard_map/gather_users/ppermute | solution.py:327
  77.4 1.9 %collective-permute-start.37 = (f32[128,128]{1,0:T(8,128)S(1)}, f32[128,128]{1,0:T(8,128)S(1)}, u32[]{:S(2)}, u32[]{:S(2)}) collective-permute-start(f32[128,128]{1,0:T(8,128)S(1)} %get-tuple-element.126.own_ref), channel_id=1, source_target_pairs={{0,16},{4,20},{8,24},{12,28},{16,0},{20,4},{24,8},{28,12},{1,17},{... | collective-permute-start | bytes 196616 | tf_op jit(solution)/shard_map/item_cg/ppermute | solution.py:327
  80.4 3.6 %collective-permute-done.37.other_ref = f32[128,128]{1,0:T(8,128)S(1)} collective-permute-done((f32[128,128]{1,0:T(8,128)S(1)}, f32[128,128]{1,0:T(8,128)S(1)}, u32[]{:S(2)}, u32[]{:S(2)}) %collective-permute-start.37) | collective-permute-done | bytes 65568 | tf_op jit(solution)/shard_map/item_cg/ppermute | solution.py:327
  88.3 1.7 %collective-permute-start.34 = (f32[128,128]{1,0:T(8,128)S(1)}, f32[128,128]{1,0:T(8,128)S(1)}, u32[]{:S(2)}, u32[]{:S(2)}) collective-permute-start(f32[128,128]{1,0:T(8,128)S(1)} %get-tuple-element.117.own_ref), channel_id=1, source_target_pairs={{0,16},{4,20},{8,24},{12,28},{16,0},{20,4},{24,8},{28,12},{1,17},{... | collective-permute-start | bytes 196616 | tf_op jit(solution)/shard_map/item_cg/ppermute | solution.py:327
  89.9 2.2 %collective-permute-done.38.other_ref = f32[128,128]{1,0:T(8,128)S(1)} collective-permute-done((f32[128,128]{1,0:T(8,128)S(1)}, f32[128,128]{1,0:T(8,128)S(1)}, u32[]{:S(2)}, u32[]{:S(2)}) %collective-permute-start.38) | collective-permute-done | bytes 65568 | tf_op jit(solution)/shard_map/item_cg/ppermute | solution.py:327
  92.2 1.5 %item_cg.13 = (f32[128,128]{1,0:T(8,128)S(1)}, f32[128,128]{1,0:T(8,128)S(1)}, f32[128,128]{1,0:T(8,128)S(1)}, f32[128,128]{1,0:T(8,128)S(1)}) custom-call(f32[128,128]{1,0:T(8,128)S(1)} %get-tuple-element.127.side_ref, f32[128,128]{1,0:T(8,128)S(1)} %get-tuple-element.128.own_ref, f32[128,128]{1,0:T(8,128)S(1)} %collective-permute-done.38.other_ref, ...), custom_call_target="tpu_custom_call" | custom-call | flops 805306368 | bytes 6750208 | tf_op jit(solution)/shard_map/item_cg/pallas_call | solution.py:300
  93.8 1.5 %item_cg.10 = (f32[128,128]{1,0:T(8,128)S(1)}, f32[128,128]{1,0:T(8,128)S(1)}, f32[128,128]{1,0:T(8,128)S(1)}, f32[128,128]{1,0:T(8,128)S(1)}) custom-call(f32[128,128]{1,0:T(8,128)S(1)} %get-tuple-element.116.side_ref, f32[128,128]{1,0:T(8,128)S(1)} %get-tuple-element.117.own_ref, f32[128,128]{1,0:T(8,128)S(1)} %collective-permute-done.34.other_ref, ...), custom_call_target="tpu_custom_call" | custom-call | flops 805306368 | bytes 6750208 | tf_op jit(solution)/shard_map/item_cg/pallas_call | solution.py:300
  95.3 3.0 %collective-permute-start.35 = (f32[128,128]{1,0:T(8,128)S(1)}, f32[128,128]{1,0:T(8,128)S(1)}, u32[]{:S(2)}, u32[]{:S(2)}) collective-permute-start(f32[128,128]{1,0:T(8,128)S(1)} %get-tuple-element.121.own_ref), channel_id=1, source_target_pairs={{0,16},{4,20},{8,24},{12,28},{16,0},{20,4},{24,8},{28,12},{1,17},{... | collective-permute-start | bytes 196616 | tf_op jit(solution)/shard_map/item_cg/ppermute | solution.py:327
  101.8 2.7 %collective-permute-start.36 = (f32[8,128]{1,0:T(8,128)S(1)}, f32[8,128]{1,0:T(8,128)S(1)}, u32[]{:S(2)}, u32[]{:S(2)}) collective-permute-start(f32[8,128]{1,0:T(8,128)S(1)} %get-tuple-element.125.refs_3_), channel_id=1, source_target_pairs={{0,16},{4,20},{8,24},{12,28},{16,0},{20,4},{24,8},{28,12},{1,17},{... | collective-permute-start | bytes 12296 | tf_op jit(solution)/shard_map/item_cg/ppermute | solution.py:327
  (89 shorter events, 32.5 us)
Async XLA Ops:
  0.6 9.5 %collective-permute-start.1 = (f32[128,128]{1,0:T(8,128)}, f32[128,128]{1,0:T(8,128)S(1)}, u32[]{:S(2)}, u32[]{:S(2)}) collective-permute-start(f32[128,128]{1,0:T(8,128)} %refs_0_.1), channel_id=1, source_target_pairs={{0,8},{4,12},{8,0},{12,4},{16,24},{20,28},{24,16},{28,20},{1,9},{5... | collective-permute-start | bytes 196616 | tf_op jit(solution)/shard_map/gather_items/ppermute | solution.py:327
  3.7 7.5 %collective-permute-start.3 = (f32[128,128]{1,0:T(8,128)}, f32[128,128]{1,0:T(8,128)S(1)}, u32[]{:S(2)}, u32[]{:S(2)}) collective-permute-start(f32[128,128]{1,0:T(8,128)} %refs_0_.1), channel_id=1, source_target_pairs={{0,16},{4,20},{8,24},{12,28},{16,0},{20,4},{24,8},{28,12},{1,17},{... | collective-permute-start | bytes 196616 | tf_op jit(solution)/shard_map/gather_items/ppermute | solution.py:327
  6.3 6.4 %collective-permute-start.5 = (f32[128,128]{1,0:T(8,128)}, f32[128,128]{1,0:T(8,128)S(1)}, u32[]{:S(2)}, u32[]{:S(2)}) collective-permute-start(f32[128,128]{1,0:T(8,128)} %refs_0_.1), channel_id=1, source_target_pairs={{0,24},{4,28},{8,16},{12,20},{16,8},{20,12},{24,0},{28,4},{1,25},{... | collective-permute-start | bytes 196616 | tf_op jit(solution)/shard_map/gather_items/ppermute | solution.py:327
  6.3 13.2 %collective-permute-start = (f32[128,128]{1,0:T(8,128)}, f32[128,128]{1,0:T(8,128)S(1)}, u32[]{:S(2)}, u32[]{:S(2)}) collective-permute-start(f32[128,128]{1,0:T(8,128)} %refs_0_.1), channel_id=1, source_target_pairs={{0,4},{4,0},{8,12},{12,8},{16,20},{20,16},{24,28},{28,24},{1,5},{5... | collective-permute-start | bytes 196616 | tf_op jit(solution)/shard_map/gather_items/ppermute | solution.py:327
  10.1 4.7 %collective-permute-start.2 = (f32[128,128]{1,0:T(8,128)S(1)}, f32[128,128]{1,0:T(8,128)S(1)}, u32[]{:S(2)}, u32[]{:S(2)}) collective-permute-start(f32[128,128]{1,0:T(8,128)S(1)} %collective-permute-done.1.refs_2_), channel_id=1, source_target_pairs={{0,4},{4,0},{8,12},{12,8},{16,20},{20,16},{24,28},{28,24},{1,5},{5... | collective-permute-start | bytes 196616 | tf_op jit(solution)/shard_map/gather_items/ppermute | solution.py:327
  11.2 8.3 %collective-permute-start.4 = (f32[128,128]{1,0:T(8,128)S(1)}, f32[128,128]{1,0:T(8,128)S(1)}, u32[]{:S(2)}, u32[]{:S(2)}) collective-permute-start(f32[128,128]{1,0:T(8,128)S(1)} %collective-permute-done.3.refs_4_), channel_id=1, source_target_pairs={{0,4},{4,0},{8,12},{12,8},{16,20},{20,16},{24,28},{28,24},{1,5},{5... | collective-permute-start | bytes 196616 | tf_op jit(solution)/shard_map/gather_items/ppermute | solution.py:327
  12.7 6.8 %collective-permute-start.6 = (f32[128,128]{1,0:T(8,128)S(1)}, f32[128,128]{1,0:T(8,128)S(1)}, u32[]{:S(2)}, u32[]{:S(2)}) collective-permute-start(f32[128,128]{1,0:T(8,128)S(1)} %collective-permute-done.5.refs_6_), channel_id=1, source_target_pairs={{0,4},{4,0},{8,12},{12,8},{16,20},{20,16},{24,28},{28,24},{1,5},{5... | collective-permute-start | bytes 196616 | tf_op jit(solution)/shard_map/gather_items/ppermute | solution.py:327
  20.8 41.3 %all-to-all-start = ((s32[4,1544,128]{2,1,0:T(8,128)}), s32[4,1544,128]{2,1,0:T(8,128)S(1)}, u32[]{:S(2)}, u32[]{:S(2)}) async-start(s32[4,1544,128]{2,1,0:T(8,128)} %get-tuple-element.107), calls=%async_computation | async-start | bytes 6324224 | tf_op jit(solution)/shard_map/send_tiles/all_to_all | solution.py:381
  24.6 5.6 %collective-permute-start.16 = (s32[48,64,128]{2,1,0:T(8,128)}, s32[48,64,128]{2,1,0:T(8,128)S(1)}, u32[]{:S(2)}, u32[]{:S(2)}) collective-permute-start(s32[48,64,128]{2,1,0:T(8,128)} %get-tuple-element.74), channel_id=1, source_target_pairs={{0,1},{1,0},{2,3},{3,2},{4,5},{5,4},{6,7},{7,6},{8,9},{9,8},{10,11... | collective-permute-start | bytes 4718600 | tf_op jit(solution)/shard_map/pack_tiles/ppermute | solution.py:327
  25.2 4.4 %collective-permute-start.7 = (f32[128,128]{1,0:T(8,128)S(1)}, f32[128,128]{1,0:T(8,128)S(1)}, u32[]{:S(2)}, u32[]{:S(2)}) collective-permute-start(f32[128,128]{1,0:T(8,128)S(1)} %copy-done), channel_id=1, source_target_pairs={{0,1},{1,0},{2,3},{3,2},{4,5},{5,4},{6,7},{7,6},{8,9},{9,8},{10,11... | collective-permute-start | bytes 196616 | tf_op jit(solution)/shard_map/gather_items/ppermute | solution.py:327
  25.3 4.4 %collective-permute-start.11 = (f32[128,128]{1,0:T(8,128)S(1)}, f32[128,128]{1,0:T(8,128)S(1)}, u32[]{:S(2)}, u32[]{:S(2)}) collective-permute-start(f32[128,128]{1,0:T(8,128)S(1)} %collective-permute-done.3.refs_4_), channel_id=1, source_target_pairs={{0,1},{1,0},{2,3},{3,2},{4,5},{5,4},{6,7},{7,6},{8,9},{9,8},{10,11... | collective-permute-start | bytes 196616 | tf_op jit(solution)/shard_map/gather_items/ppermute | solution.py:327
  25.7 4.4 %collective-permute-start.13 = (f32[128,128]{1,0:T(8,128)S(1)}, f32[128,128]{1,0:T(8,128)S(1)}, u32[]{:S(2)}, u32[]{:S(2)}) collective-permute-start(f32[128,128]{1,0:T(8,128)S(1)} %collective-permute-done.5.refs_6_), channel_id=1, source_target_pairs={{0,1},{1,0},{2,3},{3,2},{4,5},{5,4},{6,7},{7,6},{8,9},{9,8},{10,11... | collective-permute-start | bytes 196616 | tf_op jit(solution)/shard_map/gather_items/ppermute | solution.py:327
  32.6 6.4 %collective-permute-start.21 = (f32[256,128]{1,0:T(8,128)S(1)}, f32[256,128]{1,0:T(8,128)S(1)}, u32[]{:S(2)}, u32[]{:S(2)}) collective-permute-start(f32[256,128]{1,0:T(8,128)S(1)} %get-tuple-element.92.own_ref), channel_id=1, source_target_pairs={{0,2},{1,3},{2,0},{3,1},{4,6},{5,7},{6,4},{7,5},{8,10},{9,11},{10,... | collective-permute-start | bytes 393224 | tf_op jit(solution)/shard_map/user_cg/ppermute | solution.py:327
  34.2 7.9 %collective-permute-start.17 = (f32[256,128]{1,0:T(8,128)S(1)}, f32[256,128]{1,0:T(8,128)S(1)}, u32[]{:S(2)}, u32[]{:S(2)}) collective-permute-start(f32[256,128]{1,0:T(8,128)S(1)} %get-tuple-element.79.own_ref), channel_id=1, source_target_pairs={{0,2},{1,3},{2,0},{3,1},{4,6},{5,7},{6,4},{7,5},{8,10},{9,11},{10,... | collective-permute-start | bytes 393224 | tf_op jit(solution)/shard_map/user_cg/ppermute | solution.py:327
  40.5 6.2 %collective-permute-start.22 = (f32[256,128]{1,0:T(8,128)S(1)}, f32[256,128]{1,0:T(8,128)S(1)}, u32[]{:S(2)}, u32[]{:S(2)}) collective-permute-start(f32[256,128]{1,0:T(8,128)S(1)} %get-tuple-element.94.own_ref), channel_id=1, source_target_pairs={{0,2},{1,3},{2,0},{3,1},{4,6},{5,7},{6,4},{7,5},{8,10},{9,11},{10,... | collective-permute-start | bytes 393224 | tf_op jit(solution)/shard_map/user_cg/ppermute | solution.py:327
  43.5 6.4 %collective-permute-start.18 = (f32[256,128]{1,0:T(8,128)S(1)}, f32[256,128]{1,0:T(8,128)S(1)}, u32[]{:S(2)}, u32[]{:S(2)}) collective-permute-start(f32[256,128]{1,0:T(8,128)S(1)} %get-tuple-element.83.own_ref), channel_id=1, source_target_pairs={{0,2},{1,3},{2,0},{3,1},{4,6},{5,7},{6,4},{7,5},{8,10},{9,11},{10,... | collective-permute-start | bytes 393224 | tf_op jit(solution)/shard_map/user_cg/ppermute | solution.py:327
  48.3 5.9 %collective-permute-start.23 = (f32[256,128]{1,0:T(8,128)S(1)}, f32[256,128]{1,0:T(8,128)S(1)}, u32[]{:S(2)}, u32[]{:S(2)}) collective-permute-start(f32[256,128]{1,0:T(8,128)S(1)} %get-tuple-element.98.own_ref), channel_id=1, source_target_pairs={{0,2},{1,3},{2,0},{3,1},{4,6},{5,7},{6,4},{7,5},{8,10},{9,11},{10,... | collective-permute-start | bytes 393224 | tf_op jit(solution)/shard_map/user_cg/ppermute | solution.py:327
  51.5 5.5 %collective-permute-start.19 = (f32[256,128]{1,0:T(8,128)S(1)}, f32[256,128]{1,0:T(8,128)S(1)}, u32[]{:S(2)}, u32[]{:S(2)}) collective-permute-start(f32[256,128]{1,0:T(8,128)S(1)} %get-tuple-element.87.own_ref), channel_id=1, source_target_pairs={{0,2},{1,3},{2,0},{3,1},{4,6},{5,7},{6,4},{7,5},{8,10},{9,11},{10,... | collective-permute-start | bytes 393224 | tf_op jit(solution)/shard_map/user_cg/ppermute | solution.py:327
  62.1 6.4 %collective-permute-start.29 = (f32[512,128]{1,0:T(8,128)S(1)}, f32[512,128]{1,0:T(8,128)S(1)}, u32[]{:S(2)}, u32[]{:S(2)}) collective-permute-start(f32[512,128]{1,0:T(8,128)S(1)} %get-tuple-element.108.refs_0_), channel_id=1, source_target_pairs={{0,8},{4,12},{8,0},{12,4},{16,24},{20,28},{24,16},{28,20},{1,9},{5... | collective-permute-start | bytes 786440 | tf_op jit(solution)/shard_map/gather_users/ppermute | solution.py:327
  64.1 7.8 %collective-permute-start.27 = (f32[512,128]{1,0:T(8,128)S(1)}, f32[512,128]{1,0:T(8,128)S(1)}, u32[]{:S(2)}, u32[]{:S(2)}) collective-permute-start(f32[512,128]{1,0:T(8,128)S(1)} %get-tuple-element.108.refs_0_), channel_id=1, source_target_pairs={{0,4},{4,0},{8,12},{12,8},{16,20},{20,16},{24,28},{28,24},{1,5},{5... | collective-permute-start | bytes 786440 | tf_op jit(solution)/shard_map/gather_users/ppermute | solution.py:327
  68.5 6.4 %collective-permute-start.31 = (f32[512,128]{1,0:T(8,128)S(1)}, f32[512,128]{1,0:T(8,128)S(1)}, u32[]{:S(2)}, u32[]{:S(2)}) collective-permute-start(f32[512,128]{1,0:T(8,128)S(1)} %collective-permute-done.29.refs_4_), channel_id=1, source_target_pairs={{0,4},{4,0},{8,12},{12,8},{16,20},{20,16},{24,28},{28,24},{1,5},{5... | collective-permute-start | bytes 786440 | tf_op jit(solution)/shard_map/gather_users/ppermute | solution.py:327
  70.4 4.5 %collective-permute-start.26 = (f32[512,128]{1,0:T(8,128)S(1)}, f32[512,128]{1,0:T(8,128)S(1)}, u32[]{:S(2)}, u32[]{:S(2)}) collective-permute-start(f32[512,128]{1,0:T(8,128)S(1)} %get-tuple-element.108.refs_0_), channel_id=1, source_target_pairs={{0,1},{1,0},{2,3},{3,2},{4,5},{5,4},{6,7},{7,6},{8,9},{9,8},{10,11... | collective-permute-start | bytes 786440 | tf_op jit(solution)/shard_map/gather_users/ppermute | solution.py:327
  70.4 4.5 %collective-permute-start.30 = (f32[512,128]{1,0:T(8,128)S(1)}, f32[512,128]{1,0:T(8,128)S(1)}, u32[]{:S(2)}, u32[]{:S(2)}) collective-permute-start(f32[512,128]{1,0:T(8,128)S(1)} %collective-permute-done.29.refs_4_), channel_id=1, source_target_pairs={{0,1},{1,0},{2,3},{3,2},{4,5},{5,4},{6,7},{7,6},{8,9},{9,8},{10,11... | collective-permute-start | bytes 786440 | tf_op jit(solution)/shard_map/gather_users/ppermute | solution.py:327
  77.4 6.6 %collective-permute-start.37 = (f32[128,128]{1,0:T(8,128)S(1)}, f32[128,128]{1,0:T(8,128)S(1)}, u32[]{:S(2)}, u32[]{:S(2)}) collective-permute-start(f32[128,128]{1,0:T(8,128)S(1)} %get-tuple-element.126.own_ref), channel_id=1, source_target_pairs={{0,16},{4,20},{8,24},{12,28},{16,0},{20,4},{24,8},{28,12},{1,17},{... | collective-permute-start | bytes 196616 | tf_op jit(solution)/shard_map/item_cg/ppermute | solution.py:327
  79.3 25.2 %collective-permute-start.25 = (f32[128,128]{1,0:T(8,128)S(1)}, f32[128,128]{1,0:T(8,128)S(1)}, u32[]{:S(2)}, u32[]{:S(2)}) collective-permute-start(f32[128,128]{1,0:T(8,128)S(1)} %get-tuple-element.104), channel_id=1, source_target_pairs={{0,1},{1,0},{2,3},{3,2},{4,5},{5,4},{6,7},{7,6},{8,9},{9,8},{10,11... | collective-permute-start | bytes 196616 | tf_op jit(solution)/shard_map/user_cg/ppermute | solution.py:327
  79.3 7.5 %collective-permute-start.33 = (f32[128,128]{1,0:T(8,128)S(1)}, f32[128,128]{1,0:T(8,128)S(1)}, u32[]{:S(2)}, u32[]{:S(2)}) collective-permute-start(f32[128,128]{1,0:T(8,128)S(1)} %get-tuple-element.113.own_ref), channel_id=1, source_target_pairs={{0,16},{4,20},{8,24},{12,28},{16,0},{20,4},{24,8},{28,12},{1,17},{... | collective-permute-start | bytes 196616 | tf_op jit(solution)/shard_map/item_cg/ppermute | solution.py:327
  85.5 6.7 %collective-permute-start.38 = (f32[128,128]{1,0:T(8,128)S(1)}, f32[128,128]{1,0:T(8,128)S(1)}, u32[]{:S(2)}, u32[]{:S(2)}) collective-permute-start(f32[128,128]{1,0:T(8,128)S(1)} %get-tuple-element.128.own_ref), channel_id=1, source_target_pairs={{0,16},{4,20},{8,24},{12,28},{16,0},{20,4},{24,8},{28,12},{1,17},{... | collective-permute-start | bytes 196616 | tf_op jit(solution)/shard_map/item_cg/ppermute | solution.py:327
  88.3 5.5 %collective-permute-start.34 = (f32[128,128]{1,0:T(8,128)S(1)}, f32[128,128]{1,0:T(8,128)S(1)}, u32[]{:S(2)}, u32[]{:S(2)}) collective-permute-start(f32[128,128]{1,0:T(8,128)S(1)} %get-tuple-element.117.own_ref), channel_id=1, source_target_pairs={{0,16},{4,20},{8,24},{12,28},{16,0},{20,4},{24,8},{28,12},{1,17},{... | collective-permute-start | bytes 196616 | tf_op jit(solution)/shard_map/item_cg/ppermute | solution.py:327
  93.7 5.7 %collective-permute-start.39 = (f32[128,128]{1,0:T(8,128)S(1)}, f32[128,128]{1,0:T(8,128)S(1)}, u32[]{:S(2)}, u32[]{:S(2)}) collective-permute-start(f32[128,128]{1,0:T(8,128)S(1)} %get-tuple-element.132.own_ref), channel_id=1, source_target_pairs={{0,16},{4,20},{8,24},{12,28},{16,0},{20,4},{24,8},{28,12},{1,17},{... | collective-permute-start | bytes 196616 | tf_op jit(solution)/shard_map/item_cg/ppermute | solution.py:327
  95.3 5.5 %collective-permute-start.35 = (f32[128,128]{1,0:T(8,128)S(1)}, f32[128,128]{1,0:T(8,128)S(1)}, u32[]{:S(2)}, u32[]{:S(2)}) collective-permute-start(f32[128,128]{1,0:T(8,128)S(1)} %get-tuple-element.121.own_ref), channel_id=1, source_target_pairs={{0,16},{4,20},{8,24},{12,28},{16,0},{20,4},{24,8},{28,12},{1,17},{... | collective-permute-start | bytes 196616 | tf_op jit(solution)/shard_map/item_cg/ppermute | solution.py:327
  100.4 4.8 %collective-permute-start.40 = (f32[8,128]{1,0:T(8,128)S(1)}, f32[8,128]{1,0:T(8,128)S(1)}, u32[]{:S(2)}, u32[]{:S(2)}) collective-permute-start(f32[8,128]{1,0:T(8,128)S(1)} %get-tuple-element.136.refs_8_), channel_id=1, source_target_pairs={{0,16},{4,20},{8,24},{12,28},{16,0},{20,4},{24,8},{28,12},{1,17},{... | collective-permute-start | bytes 12296 | tf_op jit(solution)/shard_map/item_cg/ppermute | solution.py:327
  101.8 4.6 %collective-permute-start.36 = (f32[8,128]{1,0:T(8,128)S(1)}, f32[8,128]{1,0:T(8,128)S(1)}, u32[]{:S(2)}, u32[]{:S(2)}) collective-permute-start(f32[8,128]{1,0:T(8,128)S(1)} %get-tuple-element.125.refs_3_), channel_id=1, source_target_pairs={{0,16},{4,20},{8,24},{12,28},{16,0},{20,4},{24,8},{28,12},{1,17},{... | collective-permute-start | bytes 12296 | tf_op jit(solution)/shard_map/item_cg/ppermute | solution.py:327
  (17 other events, 53.7 us)
